TPU v7x, 256 devices: a whole 4x4x8 slice. The times are simulated.
256 devices in a mesh: section: 16 (over y, x_lo, core), tensor: 8 (over z), dp: 2 (over x_hi).
Axes of the slice: x: 4 (x_hi: 2, x_lo: 2; x = x_hi * 2 + x_lo), y: 4, z: 8, core: 2. Of those that a mesh axis runs over, the one named last changes fastest.
Arguments:
- hidden_student: bfloat16 [4, 128, 2560], P('dp', 'section'), parts along dimension 0, may hold values from -8 to 8
- hidden_teacher: bfloat16 [4, 128, 4096], P('dp', 'section'), parts along dimension 0, may hold values from -8 to 8
- targets: int32 [4, 128], P('dp'), parts along dimension 0, may hold values from 0 to 81919
- w_student: bfloat16 [81920, 2560], P(('section', 'tensor')), may hold values from -4 to 4
- w_teacher: bfloat16 [81920, 4096], P(('section', 'tensor')), may hold values from -4 to 4
Outputs:
- loss: float32 [4], P('dp'), parts along dimension 0
- grad_hidden: bfloat16 [4, 128, 2560], P('dp', 'section', 'tensor'), parts along dimension 0
- grad_weight: bfloat16 [163840, 2560], P(('dp', 'section', 'tensor')), parts along dimension 0
There are 2 independent parts, one for each index of `dp`. A program takes and returns all parts, laid end to end along the dimension named above; an argument that names none is the same for every part. Nothing has to cross between parts.
All inputs are finite; a program needn't handle non-finite values.
Results may differ from a plain program's by a relative error of at most 0.0048.
Values may be sent and summed in bfloat16 or wider, within the bound.
No kernel may reach another device: no remote copies, remote signals or barrier semaphores. Data moves between devices by JAX's collectives and lax.ppermute only.
A program may use at most 64 MiB of HBM per device.

v0:
```python
import jax
import jax.numpy as jnp
from jax import lax
from jax.sharding import PartitionSpec as P

reciprocal_heat = 0.5
heat_factor = 2.0
distill_mixing_factor = 0.5


def softmax_terms(
    pupil_raw_values, mentor_raw_values, pupil_maximal_entry, mentor_maximal_entry, target_hit
):
    student_exp = jnp.exp(pupil_raw_values - pupil_maximal_entry[:, None])
    warmed_mentor_powers = jnp.exp(
        (pupil_raw_values - pupil_maximal_entry[:, None]) * reciprocal_heat
    )
    mentor_powers = jnp.exp((mentor_raw_values - mentor_maximal_entry[:, None]) * reciprocal_heat)
    cross_entropy_terms = mentor_powers * ((mentor_raw_values - pupil_raw_values) * reciprocal_heat)
    target_terms = jnp.where(target_hit, pupil_raw_values, jnp.float32(0.0))
    totals = (
        jnp.sum(student_exp, axis=1),
        jnp.sum(warmed_mentor_powers, axis=1),
        jnp.sum(mentor_powers, axis=1),
        jnp.sum(cross_entropy_terms, axis=1),
        jnp.sum(target_terms, axis=1),
    )
    return ((student_exp, warmed_mentor_powers, mentor_powers), totals)


def head_block(student_block, teacher_block, target_block, w_student, w_teacher, vocab_start):
    block_micro = student_block.shape[0]
    gathered = lax.all_gather(student_block, "section", axis=1, tiled=True)
    token_count = gathered.shape[1]
    flat_rows = block_micro * token_count
    student_flat = gathered.reshape(flat_rows, gathered.shape[2])
    pupil_raw_values = lax.dot_general(
        student_flat, w_student, (((1,), (1,)), ((), ())), preferred_element_type=jnp.float32
    )
    mentor_raw_values = jnp.einsum(
        "mtd,vd->mtv",
        lax.all_gather(teacher_block, "section", axis=1, tiled=True),
        w_teacher,
        preferred_element_type=jnp.float32,
    )
    mentor_raw_values = mentor_raw_values.reshape(flat_rows, w_teacher.shape[0])
    vocab_local = w_student.shape[0]
    column_ids = vocab_start + lax.broadcasted_iota(jnp.int32, (1, vocab_local), 1)
    target_hit = column_ids == target_block.reshape(flat_rows, 1)
    pupil_maximal_entry, mentor_maximal_entry = lax.pmax(
        (jnp.max(pupil_raw_values, axis=1), jnp.max(mentor_raw_values, axis=1)),
        ("section", "tensor"),
    )
    exps, totals = softmax_terms(
        pupil_raw_values, mentor_raw_values, pupil_maximal_entry, mentor_maximal_entry, target_hit
    )
    student_total, warmed_mentor_partition, mentor_partition, mismatch_accrued, target_value = (
        lax.psum((totals[0], totals[1], totals[2], totals[3], totals[4]), ("section", "tensor"))
    )
    student_exp, warmed_mentor_powers, mentor_powers = exps
    pupil_partition_lognat = pupil_maximal_entry + jnp.log(student_total)
    warmed_mentor_lognorm_value = pupil_maximal_entry * reciprocal_heat + jnp.log(
        warmed_mentor_partition
    )
    mentor_partition_lognat = mentor_maximal_entry * reciprocal_heat + jnp.log(mentor_partition)
    sample_penalty = distill_mixing_factor * heat_factor**2 * (
        mismatch_accrued / mentor_partition - mentor_partition_lognat + warmed_mentor_lognorm_value
    ) + (1.0 - distill_mixing_factor) * (pupil_partition_lognat - target_value)
    block_loss = jnp.mean(sample_penalty.reshape(block_micro, token_count), axis=1)
    pupil_raw_slope = (
        distill_mixing_factor
        * heat_factor
        * (
            warmed_mentor_powers / warmed_mentor_partition[:, None]
            - mentor_powers / mentor_partition[:, None]
        )
    )
    pupil_raw_slope = pupil_raw_slope + (1.0 - distill_mixing_factor) * (
        student_exp / student_total[:, None] - target_hit.astype(jnp.float32)
    )
    pupil_raw_slope = pupil_raw_slope.astype(jnp.bfloat16)
    grad_terms = jnp.dot(pupil_raw_slope, w_student, preferred_element_type=jnp.float32)
    grad_terms = grad_terms.reshape(block_micro, token_count, w_student.shape[1])
    partial_grad = lax.psum_scatter(grad_terms, "tensor", scatter_dimension=2, tiled=True)
    block_grad = lax.psum_scatter(partial_grad, "section", scatter_dimension=1, tiled=True)
    weight_part = lax.dot_general(
        pupil_raw_slope, student_flat, (((0,), (0,)), ((), ())), preferred_element_type=jnp.float32
    )
    return (block_loss, block_grad.astype(jnp.bfloat16), weight_part)


def per_device(hidden_student, hidden_teacher, targets, w_student, w_teacher):
    micro_count = hidden_student.shape[0]
    vocab_local = w_student.shape[0]
    vocab_start = lax.axis_index(("section", "tensor")) * vocab_local
    span_list = [(span_index, 1) for span_index in range(micro_count)]
    losses = []
    grad_blocks = []
    weight_total = jnp.zeros((vocab_local, w_student.shape[1]), jnp.float32)
    for span_start, span_width in span_list:
        block_loss, block_grad, weight_part = head_block(
            hidden_student[span_start : span_start + span_width],
            hidden_teacher[span_start : span_start + span_width],
            targets[span_start : span_start + span_width],
            w_student,
            w_teacher,
            vocab_start,
        )
        losses.append(block_loss)
        grad_blocks.append(block_grad)
        weight_total = weight_total + weight_part
    loss = jnp.concatenate(losses, axis=0)
    grad_hidden = jnp.concatenate(grad_blocks, axis=0)
    return (loss, grad_hidden, weight_total.astype(jnp.bfloat16))


def solution(mesh):
    placed = (
        P("dp", "section", None),
        P("dp", "section", None),
        P("dp", None),
        P(("section", "tensor"), None),
        P(("section", "tensor"), None),
    )
    return jax.shard_map(
        per_device,
        mesh=mesh,
        in_specs=placed,
        out_specs=(P("dp"), P("dp", "section", "tensor"), P(("dp", "section", "tensor"), None)),
        check_vma=False,
    )
```

profile of v0, /device:TPU:4, one launch (start us, length us, event | category | flops | bytes accessed | tf_op | source)
XLA Modules:
  0.0 798.5 jit_solution(13249215198669787747)
XLA Ops:
  7.2 0.0 copy-start
  7.2 0.0 all-gather.3.cloned.1.call-start
  7.2 1.7 fusion.31
  8.9 0.0 all-gather.3.cloned.1.call-update
  8.9 0.0 all-gather.5.cloned.1.call-start
  9.0 0.7 all-gather.5.cloned.1.call-update
  9.7 0.0 reduce-scatter.7.cloned.1.call-start
  9.7 0.8 fusion.32
  10.5 0.8 slice_bitcast_fusion.1
  11.3 22.7 %all_gather.13 = bf16[1,128,2560]{2,1,0:T(8,128)(2,1)S(1)} all-gather(bf16[1,8,2560]{2,1,0:T(8,128)(2,1)S(1)} %get-tuple-element.35), channel_id=1, replica_groups=mesh['section'=16,'tensor'=8,'dp'=2] {'section'}, dimensions={1}, use_global_device_ids=true | all-gather | bytes 696320 | tf_op jit(solution)/shard_map/all_gather | solution.py:33
  34.0 0.0 copy-start.3
  34.0 19.9 %all_gather.15 = bf16[1,128,2560]{2,1,0:T(8,128)(2,1)S(1)} all-gather(bf16[1,8,2560]{2,1,0:T(8,128)(2,1)S(1)} %get-tuple-element.36), channel_id=1, replica_groups=mesh['section'=16,'tensor'=8,'dp'=2] {'section'}, dimensions={1}, use_global_device_ids=true | all-gather | bytes 696320 | tf_op jit(solution)/shard_map/all_gather | solution.py:33
  53.9 0.0 copy-done.3
  53.9 0.0 copy-done
  53.9 0.0 copy-start.1
  53.9 1.9 fusion.36
  55.7 0.0 copy-done.1
  55.7 1.9 fusion.34
  57.6 5.3 fusion.35
  62.9 22.3 %all-gather.5.cloned.1.call-done = bf16[1,128,4096]{2,1,0:T(8,128)(2,1)} async-done(((bf16[1,8,4096]{2,1,0:T(8,128)(2,1)}), bf16[1,128,4096]{2,1,0:T(8,128)(2,1)}) %all-gather.5.cloned.1.call-update) | async-done | bytes 1048592 | tf_op jit(solution)/shard_map/all_gather | solution.py:42
  85.2 5.3 fusion.33
  90.5 280.2 %all-reduce.3 = (f32[128]{0:T(128)S(1)}, f32[128]{0:T(128)S(1)}, f32[128]{0:T(128)S(1)}, f32[128]{0:T(128)S(1)}) all-reduce(f32[128]{0:T(128)S(1)} %get-tuple-element.44, f32[128]{0:T(128)S(1)} %get-tuple-element.46, f32[128]{0:T(128)S(1)} %get-tuple-element.48, ...), channel_id=1, replica_groups=mesh['section'=16,'tensor'=8,'dp'=2] {'section','tensor'}, use_global_device_ids=true, to_apply=%region_16.17 | all-reduce | flops 512 | bytes 4096 | tf_op jit(solution)/shard_map/pmax | solution.py:50
  370.7 1.9 multiply_reduce_fusion.1
  372.6 279.7 %all-reduce.2 = (f32[128]{0:T(128)S(1)}, f32[128]{0:T(128)S(1)}, f32[128]{0:T(128)S(1)}, f32[128]{0:T(128)S(1)}, f32[128]{0:T(128)S(1)}, /*index=5*/f32[128]{0:T...) all-reduce(f32[128]{0:T(128)S(1)} %get-tuple-element.39, ...), channel_id=1, replica_groups=mesh['section'=16,'tensor'=8,'dp'=2] {'section','tensor'}, use_global_device_ids=true, to_apply=%region_28.29 | all-reduce | flops 1280 | bytes 10240 | tf_op jit(solution)/shard_map/psum | solution.py:58
  652.3 3.6 fusion.26
  655.9 0.0 reduce-scatter.7.cloned.1.call-update
  655.9 0.0 reduce-scatter.5.cloned.1.call-start
  656.0 0.0 copy-start.6
  656.0 3.6 fusion.29
  659.6 0.0 reduce-scatter.5.cloned.1.call-update
  659.6 0.0 copy-done.6
  659.6 0.6 dynamic-slice
  660.9 0.6 add_reduce_fusion
  662.8 0.6 pad_maximum_fusion.1
  663.4 0.0 copy-start.2
  663.4 0.0 copy-start.4
  663.4 2.7 fusion.7
  666.1 0.0 copy-done.2
  666.1 0.0 copy-done.4
  666.1 0.0 copy-done.5
  666.1 3.0 add_convert_fusion
  669.1 21.7 %reduce-scatter.7.cloned.1.call-done = f32[1,128,320]{1,0,2:T(1,128)} async-done(((f32[1,128,2560]{1,0,2:T(1,128)}), f32[1,128,320]{1,0,2:T(1,128)}) %reduce-scatter.7.cloned.1.call-update) | async-done | bytes 163856 | tf_op jit(solution)/shard_map/reduce_scatter | solution.py:84
  690.8 1.0 copy.11
  691.8 39.3 %reduce-scatter.5.cloned.1.call-done = f32[1,128,320]{1,0,2:T(1,128)} async-done(((f32[1,128,2560]{1,0,2:T(1,128)}), f32[1,128,320]{1,0,2:T(1,128)}) %reduce-scatter.5.cloned.1.call-update) | async-done | bytes 163856 | tf_op jit(solution)/shard_map/reduce_scatter | solution.py:84
  731.1 1.7 copy.9
  732.9 57.8 %all-reduce.6 = (bf16[1,128,320]{2,1,0:T(8,128)(2,1)}, bf16[1,128,320]{2,1,0:T(8,128)(2,1)}) all-reduce(f32[1,128,320]{2,1,0:T(8,128)S(1)} %copy.11, f32[1,128,320]{2,1,0:T(8,128)} %copy.9), channel_id=5, replica_groups=mesh['section'=16,'tensor'=8,'dp'=2] {'section'}, use_global_device_ids=true, to_apply=%region_33.34.clone | all-reduce | flops 81920 | bytes 491520
  790.7 0.7 dynamic-slice_convert_fusion
  791.4 0.6 pad_maximum_fusion
  (3 shorter events, 0.0 us)
Async XLA Ops:
  7.2 46.7 %copy-start = (bf16[640,2560]{1,0:T(8,128)(2,1)S(1)}, bf16[640,2560]{1,0:T(8,128)(2,1)}, u32[]{:S(2)}) copy-start(bf16[640,2560]{1,0:T(8,128)(2,1)} %param.8) | copy-start | bytes 9830404
  7.2 50.4 %all-gather.3.cloned.1.call-start = ((), (), s32[]{:S(2)}) async-start(), calls=%async_computation.2 | async-start | bytes 1114112 | tf_op jit(solution)/shard_map/all_gather | solution.py:42
  8.9 76.3 %all-gather.5.cloned.1.call-start = ((), (), s32[]{:S(2)}) async-start(), calls=%async_computation.3 | async-start | bytes 1114112 | tf_op jit(solution)/shard_map/all_gather | solution.py:42
  9.7 681.1 %reduce-scatter.7.cloned.1.call-start = ((), (), s32[]{:S(2)}) async-start(), calls=%async_computation.5 | async-start | bytes 1474560 | tf_op jit(solution)/shard_map/reduce_scatter | solution.py:84
  34.0 19.9 %copy-start.3 = (bf16[1,128,2560]{2,1,0:T(8,128)(2,1)}, bf16[1,128,2560]{2,1,0:T(8,128)(2,1)S(1)}, u32[]{:S(2)}) copy-start(bf16[1,128,2560]{2,1,0:T(8,128)(2,1)S(1)} %all_gather.13) | copy-start | bytes 1966084
  53.9 1.9 copy-start.1
  655.9 75.2 %reduce-scatter.5.cloned.1.call-start = ((), (), s32[]{:S(2)}) async-start(), calls=%async_computation.4 | async-start | bytes 1474560 | tf_op jit(solution)/shard_map/reduce_scatter | solution.py:84
  656.0 3.7 copy-start.6
  663.4 2.7 copy-start.2
  663.4 2.7 copy-start.4
  663.4 2.7 copy-start.5
Sparse Core Ops, SparseCore 0:
  9.9 38.1 all-gather.2
  49.9 35.3 all-gather.4
  656.0 34.7 reduce-scatter.6
  693.2 37.9 reduce-scatter.4
where the time goes:
time: 799 us
  blocking collectives  660 us (83%)
  waiting for transfers between devices  84.1 us (11%)
  matrix products  27.2 us (3%)
  between operations  15.8 us (2%)
    pmax x1, blocking collectives, head_block(): lax.pmax((jnp.max(pupil_raw_values, axis=1), jnp.max(mentor_raw_values, a...  280 us
    psum x1, blocking collectives, head_block(): lax.psum((totals[0], totals[1], totals[2], totals[3], totals[4]), ('secti...  280 us
    reduce_scatter x2, waiting for transfers between devices, head_block(): lax.psum_scatter(grad_terms, 'tensor', scatter_dimension=2, tiled=True)  61 us
    unnamed x1, blocking collectives  57.8 us
    all_gather x2, blocking collectives, head_block(): gathered = lax.all_gather(student_block, 'section', axis=1, tiled=True)  42.6 us
    all_gather x2, waiting for transfers between devices, head_block(): lax.all_gather(teacher_block, 'section', axis=1, tiled=True)  22.3 us
  transfers between devices with their start and end apart: 4, of which 3 were waited for; matrix products, arithmetic and copies ran while one was open for 3% of the time, Pallas kernels for 0%

commit v1 on v0

v1 whole, which is shorter than its diff:
```python
import jax
import jax.numpy as jnp
import numpy as np
from jax import lax
from jax.sharding import Mesh, PartitionSpec as P

RING_Y, PAIR_X, CORES, RING_Z = 4, 2, 2, 8
SIZES = {"y": RING_Y, "x": PAIR_X, "c": CORES, "z": RING_Z}
bf16, f32 = jnp.bfloat16, jnp.float32


def swap(value, axis, mask=1):
    return lax.ppermute(value, axis, [(i, i ^ mask) for i in range(SIZES[axis])])


def shift(value, axis, step):
    size = SIZES[axis]
    return lax.ppermute(value, axis, [(i, (i + step) % size) for i in range(size)])


def rotate(value, dim, start):
    size = value.shape[dim]
    return lax.dynamic_slice_in_dim(jnp.concatenate([value, value], dim), start, size, dim)


def to_relative(value, y, x, c):
    lead = value.shape[:-1]
    v = value.reshape(*lead, RING_Y, PAIR_X, CORES, -1)
    n = len(lead)
    v = rotate(rotate(rotate(v, n, y), n + 1, x), n + 2, c)
    return v.reshape(*lead, -1)


def to_canonical(value, y, x, c):
    return to_relative(value, lax.rem(RING_Y - y, RING_Y), x, c)


def gather_rows(block):
    half = block.shape[0] // 2
    from_prev = shift(block, "y", 1)
    from_next = shift(block, "y", 3)
    across = swap(block, "x")
    across_prev = shift(across, "y", 1)
    across_next = shift(across, "y", 3)
    far_a = shift(from_prev[:half], "y", 1)
    far_b = shift(from_next[half:], "y", 3)
    across_far_a = shift(across_prev[:half], "y", 1)
    across_far_b = shift(across_next[half:], "y", 3)
    far = jnp.concatenate([far_a, far_b], 0)
    across_far = jnp.concatenate([across_far_a, across_far_b], 0)
    mine = [block, across, from_next, across_next, far, across_far, from_prev, across_prev]
    out = []
    for piece in mine:
        out += [piece, swap(piece, "c")]
    return jnp.concatenate(out, 0)


def merge(parts):
    top = parts[0][0]
    for p in parts[1:]:
        top = jnp.maximum(top, p[0])
    total = parts[0][1] * jnp.exp(parts[0][0] - top)
    for p in parts[1:]:
        total = total + p[1] * jnp.exp(p[0] - top)
    return jnp.stack([top, total])


def exchange_totals(part):
    part = merge([part, swap(part, "c")])
    part = merge([part, swap(part, "x")])
    part = merge([part, shift(part, "y", 1), shift(part, "y", 3), shift(part, "y", 2)])
    part = merge([part, swap(part, "z", 1)])
    part = merge([part, swap(part, "z", 2)])
    part = merge([part, swap(part, "z", 4)])
    return part


def reduce_rows(partial, z):
    rows, width = partial.shape
    block = rows // 16
    q = partial.reshape(8, 2, block, width)
    q = q[:, 0] + swap(q[:, 1].astype(bf16), "c").astype(f32)
    q = q.reshape(RING_Y, 2, block, width)
    moved = [shift(q[d].astype(bf16), "y", d) for d in range(1, RING_Y)]
    r = q[0] + moved[0].astype(f32) + moved[1].astype(f32) + moved[2].astype(f32)
    s = r[0] + swap(r[1].astype(bf16), "x").astype(f32)
    s = s.reshape(block, RING_Z, width // RING_Z).transpose(1, 0, 2)
    s = s.reshape(2, 2, 2, block, width // RING_Z)
    pick = lambda v, dim, at: lax.dynamic_index_in_dim(v, at, dim, keepdims=False)
    z0, z1, z2 = z % 2, (z // 2) % 2, z // 4
    s = pick(s, 2, z0) + swap(pick(s, 2, 1 - z0), "z", 1)
    s = pick(s, 1, z1) + swap(pick(s, 1, 1 - z1), "z", 2)
    s = pick(s, 0, z2) + swap(pick(s, 0, 1 - z2), "z", 4)
    return s


def per_device(hidden_student, hidden_teacher, targets, w_student, w_teacher):
    y, x, c, z = (lax.axis_index(a) for a in ("y", "x", "c", "z"))
    micro, tokens, width_s = hidden_student.shape
    width_t = hidden_teacher.shape[2]
    vocab = w_student.shape[0]
    start = (((y * PAIR_X + x) * CORES + c) * RING_Z + z) * vocab
    rows = micro * tokens
    block = jnp.concatenate(
        [hidden_student.reshape(rows, width_s), hidden_teacher.reshape(rows, width_t)], 1
    )
    h = gather_rows(block)
    hs, ht = h[:, :width_s], h[:, width_s:]
    tgt = targets.reshape(micro, 16, tokens).transpose(1, 0, 2).reshape(1, -1)
    tgt = to_relative(tgt, y, x, c) - start
    dims = (((1,), (1,)), ((), ()))
    s = lax.dot_general(w_student, hs, dims, preferred_element_type=f32)
    t = lax.dot_general(w_teacher, ht, dims, preferred_element_type=f32)
    hit = lax.broadcasted_iota(jnp.int32, s.shape, 0) == tgt
    ms = jnp.max(s, axis=0, keepdims=True)
    mt = jnp.max(t, axis=0, keepdims=True)
    e2 = jnp.exp((s - ms) * 0.5)
    et = jnp.exp((t - mt) * 0.5)
    total = lambda v: jnp.sum(v, axis=0, keepdims=True)
    zero = jnp.zeros_like(ms)
    sums = [total(jnp.exp(s - ms)), total(e2), total(et), total(et * ((t - s) * 0.5))]
    sums += [total(jnp.where(hit, s, 0.0)), zero, zero, zero]
    tops = [ms, ms * 0.5, mt * 0.5, mt * 0.5, zero, zero, zero, zero]
    part = jnp.stack([jnp.concatenate(tops, 0), jnp.concatenate(sums, 0)])
    part = exchange_totals(to_canonical(part, y, x, c))
    part = to_relative(part, y, x, c)
    ms, half_mt = part[0, 0:1], part[0, 2:3]
    z1, z2, zt, cross, picked = (part[1, i : i + 1] for i in range(5))
    row_loss = 2.0 * (cross / zt - (half_mt + jnp.log(zt)) + (ms * 0.5 + jnp.log(z2))) + 0.5 * (
        ms + jnp.log(z1) - picked
    )
    loss = jnp.mean(row_loss.reshape(16, micro, tokens), axis=(0, 2))
    g = jnp.exp((s - ms) * 0.5) / z2 - jnp.exp(t * 0.5 - half_mt) / zt
    g = g + 0.5 * (jnp.exp(s - ms) / z1 - hit.astype(f32))
    g = g.astype(bf16)
    partial = lax.dot_general(g, w_student, (((0,), (0,)), ((), ())), preferred_element_type=f32)
    grad_hidden = reduce_rows(partial, z).astype(bf16).reshape(micro, tokens, -1)
    grad_weight = jnp.dot(g, hs, preferred_element_type=f32).astype(bf16)
    return loss, grad_hidden, grad_weight


def solution(mesh):
    sec = ("y", "x", "c")
    devices = np.asarray(mesh.devices).reshape(RING_Y, PAIR_X, CORES, RING_Z, -1)
    fine = Mesh(devices, sec + ("z", "dp"))
    return jax.shard_map(
        per_device,
        mesh=fine,
        in_specs=(
            P("dp", sec, None),
            P("dp", sec, None),
            P("dp", None),
            P(sec + ("z",), None),
            P(sec + ("z",), None),
        ),
        out_specs=(P("dp"), P("dp", sec, "z"), P(("dp",) + sec + ("z",), None)),
        check_vma=False,
    )
```

time: 799 us -> 140 us (0.18)
  blocking collectives: 660 us -> 0 us
  starting transfers between devices: 0.16 us -> 44.6 us
  waiting for transfers between devices: 84.1 us -> 48.1 us
  local copies, waits for them, and re-layouts: 7.33 us -> 22.5 us
  between operations: 15.8 us -> 1.12 us
  matrix products: 27.2 us -> 14 us
    pmax x1 -> x0, blocking collectives: 280 us -> none  [head_block(): lax.pmax((jnp.max(pupil_raw_values, axis=1), jnp.max(mentor_raw_values, a...]
    psum x1 -> x0, blocking collectives: 280 us -> none  [head_block(): lax.psum((totals[0], totals[1], totals[2], totals[3], totals[4]), ('secti...]
    reduce_scatter x2 -> x0, waiting for transfers between devices: 61 us -> none  [head_block(): lax.psum_scatter(grad_terms, 'tensor', scatter_dimension=2, tiled=True)]
    unnamed x1 -> x0, blocking collectives: 57.8 us -> none
    ppermute x0 -> x33, waiting for transfers between devices: none -> 48.1 us  [the longest x14 27.7 us: shift(): lax.ppermute(value, axis, [(i, (i + step) % size) for i in range(size)])]
    ppermute x0 -> x33, starting transfers between devices: none -> 44.6 us  [the longest x19 25.7 us: swap(): lax.ppermute(value, axis, [(i, i ^ mask) for i in range(SIZES[axis])])]
    all_gather x2 -> x0, blocking collectives: 42.6 us -> none  [head_block(): gathered = lax.all_gather(student_block, 'section', axis=1, tiled=True)]
    all_gather x2 -> x0, waiting for transfers between devices: 22.3 us -> none  [head_block(): lax.all_gather(teacher_block, 'section', axis=1, tiled=True)]
  transfers between devices with their start and end apart: 4 -> 33, of which waited for: 3 -> 15; matrix products, arithmetic and copies ran while one was open for 3% -> 16% of each run, Pallas kernels for 0% -> 0%
where the time goes in v1:
time: 140 us; the launch traced here: 139 us
  waiting for transfers between devices  48.1 us (34%)
  starting transfers between devices  44.6 us (32%)
  local copies, waits for them, and re-layouts  22.5 us (16%)
  matrix products  14 us (10%)
  other arithmetic  8.51 us (6%)
    ppermute x14, waiting for transfers between devices, shift(): lax.ppermute(value, axis, [(i, (i + step) % size) for i in range(size)])  27.7 us
    ppermute x19, starting transfers between devices, swap(): lax.ppermute(value, axis, [(i, i ^ mask) for i in range(SIZES[axis])])  25.7 us
    ppermute x19, waiting for transfers between devices, swap(): lax.ppermute(value, axis, [(i, i ^ mask) for i in range(SIZES[axis])])  20.4 us
    ppermute x14, starting transfers between devices, shift(): lax.ppermute(value, axis, [(i, (i + step) % size) for i in range(size)])  18.9 us
    unnamed x40, local copies, waits for them, and re-layouts  15.2 us
    dot_general x1, matrix products, per_device(): grad_weight = jnp.dot(g, hs, preferred_element_type=f32).astype(bf16)  4.95 us
    dot_general x1, matrix products, per_device(): s = lax.dot_general(w_student, hs, dims, preferred_element_type=f32)  3.51 us
    dot_general x1, matrix products, per_device(): lax.dot_general(g, w_student, (((0,), (0,)), ((), ())), preferred_element...  2.87 us
  transfers between devices with their start and end apart: 33, of which 15 were waited for; matrix products, arithmetic and copies ran while one was open for 16% of the time, Pallas kernels for 0%

profile of v1, /device:TPU:4, one launch (start us, length us, event | category | flops | bytes accessed | tf_op | source)
XLA Modules:
  0.0 138.8 jit_solution(11917814343811007937)
XLA Ops:
  0.6 1.9 %pad_maximum_fusion.2 = (bf16[16,6656]{1,0:T(8,128)(2,1)}, bf16[256,6656]{1,0:T(8,128)(2,1)}) fusion(bf16[16,4096]{1,0:T(8,128)(2,1)} %bitcast.99, bf16[16,2560]{1,0:T(8,128)(2,1)} %bitcast.100), kind=kLoop, calls=%fused_computation.53 | loop fusion | flops 425983 | bytes 638976 | tf_op jit(solution)/shard_map/concatenate | solution.py:104
  2.5 1.2 collective-permute-start.1
  3.7 3.0 %collective-permute-start.3 = (bf16[16,6656]{1,0:T(8,128)(2,1)}, bf16[16,6656]{1,0:T(8,128)(2,1)}, u32[]{:S(2)}, u32[]{:S(2)}) collective-permute-start(bf16[16,6656]{1,0:T(8,128)(2,1)} %get-tuple-element.26), channel_id=1, source_target_pairs={{0,192},{64,0},{128,64},{192,128},{1,193},{65,1},{129,65},{193,129... | collective-permute-start | bytes 638984 | tf_op jit(solution)/shard_map/ppermute | solution.py:18
  6.8 0.8 reshape.191
  7.8 7.7 %collective-permute-done.7 = bf16[16,6656]{1,0:T(8,128)(2,1)S(1)} collective-permute-done((bf16[16,6656]{1,0:T(8,128)(2,1)}, bf16[16,6656]{1,0:T(8,128)(2,1)S(1)}, u32[]{:S(2)}, u32[]{:S(2)}) %collective-permute-start.7) | collective-permute-done | bytes 213024 | tf_op jit(solution)/shard_map/ppermute | solution.py:18
  15.7 0.9 slice.177
  16.6 3.2 %collective-permute-start.9 = (bf16[8,6656]{1,0:T(8,128)(2,1)S(1)}, bf16[8,6656]{1,0:T(8,128)(2,1)S(1)}, u32[]{:S(2)}, u32[]{:S(2)}) collective-permute-start(bf16[8,6656]{1,0:T(8,128)(2,1)S(1)} %slice.177), channel_id=1, source_target_pairs={{0,192},{64,0},{128,64},{192,128},{1,193},{65,1},{129,65},{193,129... | collective-permute-start | bytes 319496 | tf_op jit(solution)/shard_map/ppermute | solution.py:18
  20.4 1.6 %constant_dynamic-update-slice_fusion.16 = bf16[256,6656]{1,0:T(8,128)(2,1)} fusion(bf16[256,6656]{1,0:T(8,128)(2,1)} %get-tuple-element.27, bf16[16,6656]{1,0:T(8,128)(2,1)} %collective-permute-done), kind=kLoop, calls=%fused_computation.86 | loop fusion | bytes 425984
  22.0 1.6 %constant_dynamic-update-slice_fusion.15 = bf16[256,6656]{1,0:T(8,128)(2,1)} fusion(bf16[256,6656]{1,0:T(8,128)(2,1)} %constant_dynamic-update-slice_fusion.16, bf16[16,6656]{1,0:T(8,128)(2,1)} %collective-permute-done.1), kind=kLoop, calls=%fused_computation.85 | loop fusion | bytes 425984
  23.7 1.9 %collective-permute-start.11 = (bf16[16,6656]{1,0:T(8,128)(2,1)}, bf16[16,6656]{1,0:T(8,128)(2,1)S(1)}, u32[]{:S(2)}, u32[]{:S(2)}) collective-permute-start(bf16[16,6656]{1,0:T(8,128)(2,1)} %collective-permute-done.1), channel_id=1, source_target_pairs={{0,64},{64,128},{128,192},{192,0},{1,65},{65,129},{129,193},{193,1... | collective-permute-start | bytes 638984 | tf_op jit(solution)/shard_map/ppermute | solution.py:18
  25.6 6.6 %collective-permute-done.11 = bf16[16,6656]{1,0:T(8,128)(2,1)S(1)} collective-permute-done((bf16[16,6656]{1,0:T(8,128)(2,1)}, bf16[16,6656]{1,0:T(8,128)(2,1)S(1)}, u32[]{:S(2)}, u32[]{:S(2)}) %collective-permute-start.11) | collective-permute-done | bytes 213024 | tf_op jit(solution)/shard_map/ppermute | solution.py:18
  32.9 2.8 %collective-permute-start.13 = (bf16[8,6656]{1,0:T(8,128)(2,1)S(1)}, bf16[8,6656]{1,0:T(8,128)(2,1)S(1)}, u32[]{:S(2)}, u32[]{:S(2)}) collective-permute-start(bf16[8,6656]{1,0:T(8,128)(2,1)S(1)} %slice.179), channel_id=1, source_target_pairs={{0,192},{64,0},{128,64},{192,128},{1,193},{65,1},{129,65},{193,129... | collective-permute-start | bytes 319496 | tf_op jit(solution)/shard_map/ppermute | solution.py:18
  36.4 1.6 %constant_dynamic-update-slice_fusion.13 = bf16[256,6656]{1,0:T(8,128)(2,1)} fusion(bf16[256,6656]{1,0:T(8,128)(2,1)} %constant_dynamic-update-slice_fusion.14, bf16[16,6656]{1,0:T(8,128)(2,1)} %collective-permute-done.3), kind=kLoop, calls=%fused_computation.83 | loop fusion | bytes 425984
  46.3 0.7 constant_dynamic-update-slice_fusion.1
  47.8 3.5 %fusion.60 = (f32[256]{0:T(256)S(1)}, f32[256,640]{1,0:T(8,128)}) fusion(bf16[640,2560]{1,0:T(8,128)(2,1)S(1)} %copy-done, bf16[256,6656]{1,0:T(8,128)(2,1)} %constant_dynamic-update-slice_fusion), kind=kOutput, calls=%fused_computation.155 | convolution fusion | flops 839024384 | bytes 5243904 | tf_op jit(solution)/shard_map/dot_general | solution.py:112
  51.3 2.7 %fusion.61 = (f32[256]{0:T(256)S(1)}, f32[256,640]{1,0:T(8,128)}) fusion(bf16[640,4096]{1,0:T(8,128)(2,1)S(1)} %copy-done.7, bf16[256,6656]{1,0:T(8,128)(2,1)S(1)} %copy-done.4), kind=kOutput, calls=%fused_computation.156 | convolution fusion | flops 1342340864 | bytes 7996416 | tf_op jit(solution)/shard_map/dot_general | solution.py:113
  54.1 2.0 %fusion.11 = (f32[256]{0:T(256)S(1)}, f32[256]{0:T(256)S(1)}, f32[256]{0:T(256)S(1)}, f32[256]{0:T(256)S(1)}, f32[256]{0:T(256)S(1)}) fusion(f32[256,640]{1,0:T(8,128)} %get-tuple-element.41, f32[256,640]{1,0:T(8,128)} %get-tuple-element.39, f32[256]{0:T(256)S(1)} %get-tuple-element.40, s32[256]{0:T(256)S(1)} %sub.207, f32[256]{0:T(256)S(1)} %get-tuple-element.38), kind=kLoop, calls=%fused_computation.17 | loop fusion | flops 2292480 | bytes 1318912 | tf_op jit(solution)/shard_map/reduce_sum | solution.py:119
  57.2 0.8 reshape.192
  58.8 0.8 collective-permute-done.17
  59.6 0.9 collective-permute-start.18
  60.5 2.9 %collective-permute-done.18 = f32[2,8,256]{2,1,0:T(8,128)S(1)} collective-permute-done((f32[2,8,256]{2,1,0:T(8,128)S(1)}, f32[2,8,256]{2,1,0:T(8,128)S(1)}, u32[]{:S(2)}, u32[]{:S(2)}) %collective-permute-start.18) | collective-permute-done | bytes 16416 | tf_op jit(solution)/shard_map/ppermute | solution.py:13
  63.6 3.2 %collective-permute-start.20 = (f32[2,8,256]{2,1,0:T(8,128)S(1)}, f32[2,8,256]{2,1,0:T(8,128)S(1)}, u32[]{:S(2)}, u32[]{:S(2)}) collective-permute-start(f32[2,8,256]{2,1,0:T(8,128)S(1)} %pad_maximum_fusion.4), channel_id=1, source_target_pairs={{0,192},{64,0},{128,64},{192,128},{1,193},{65,1},{129,65},{193,129... | collective-permute-start | bytes 49160 | tf_op jit(solution)/shard_map/ppermute | solution.py:18
  67.1 1.4 %collective-permute-done.19 = f32[2,8,256]{2,1,0:T(8,128)S(1)} collective-permute-done((f32[2,8,256]{2,1,0:T(8,128)S(1)}, f32[2,8,256]{2,1,0:T(8,128)S(1)}, u32[]{:S(2)}, u32[]{:S(2)}) %collective-permute-start.19) | collective-permute-done | bytes 16416 | tf_op jit(solution)/shard_map/ppermute | solution.py:18
  68.5 3.5 %collective-permute-done.21 = f32[2,8,256]{2,1,0:T(8,128)S(1)} collective-permute-done((f32[2,8,256]{2,1,0:T(8,128)S(1)}, f32[2,8,256]{2,1,0:T(8,128)S(1)}, u32[]{:S(2)}, u32[]{:S(2)}) %collective-permute-start.21) | collective-permute-done | bytes 16416 | tf_op jit(solution)/shard_map/ppermute | solution.py:18
  72.1 2.0 %collective-permute-start.22 = (f32[2,8,256]{2,1,0:T(8,128)S(1)}, f32[2,8,256]{2,1,0:T(8,128)S(1)}, u32[]{:S(2)}, u32[]{:S(2)}) collective-permute-start(f32[2,8,256]{2,1,0:T(8,128)S(1)} %pad_maximum_fusion.5), channel_id=1, source_target_pairs={{0,2},{2,0},{4,6},{6,4},{8,10},{10,8},{12,14},{14,12},{1,3},{3,1},... | collective-permute-start | bytes 49160 | tf_op jit(solution)/shard_map/ppermute | solution.py:13
  74.1 1.8 %collective-permute-done.22 = f32[2,8,256]{2,1,0:T(8,128)S(1)} collective-permute-done((f32[2,8,256]{2,1,0:T(8,128)S(1)}, f32[2,8,256]{2,1,0:T(8,128)S(1)}, u32[]{:S(2)}, u32[]{:S(2)}) %collective-permute-start.22) | collective-permute-done | bytes 16416 | tf_op jit(solution)/shard_map/ppermute | solution.py:13
  75.9 3.4 %collective-permute-start.23 = (f32[2,8,256]{2,1,0:T(8,128)S(1)}, f32[2,8,256]{2,1,0:T(8,128)S(1)}, u32[]{:S(2)}, u32[]{:S(2)}) collective-permute-start(f32[2,8,256]{2,1,0:T(8,128)S(1)} %pad_maximum_fusion.6), channel_id=1, source_target_pairs={{0,4},{2,6},{4,0},{6,2},{8,12},{10,14},{12,8},{14,10},{1,5},{3,7},... | collective-permute-start | bytes 49160 | tf_op jit(solution)/shard_map/ppermute | solution.py:13
  79.3 1.7 %collective-permute-done.23 = f32[2,8,256]{2,1,0:T(8,128)S(1)} collective-permute-done((f32[2,8,256]{2,1,0:T(8,128)S(1)}, f32[2,8,256]{2,1,0:T(8,128)S(1)}, u32[]{:S(2)}, u32[]{:S(2)}) %collective-permute-start.23) | collective-permute-done | bytes 16416 | tf_op jit(solution)/shard_map/ppermute | solution.py:13
  81.0 6.9 %collective-permute-start.24 = (f32[2,8,256]{2,1,0:T(8,128)S(1)}, f32[2,8,256]{2,1,0:T(8,128)S(1)}, u32[]{:S(2)}, u32[]{:S(2)}) collective-permute-start(f32[2,8,256]{2,1,0:T(8,128)S(1)} %pad_maximum_fusion.7), channel_id=1, source_target_pairs={{0,8},{2,10},{4,12},{6,14},{8,0},{10,2},{12,4},{14,6},{1,9},{3,11}... | collective-permute-start | bytes 49160 | tf_op jit(solution)/shard_map/ppermute | solution.py:13
  88.0 1.7 %collective-permute-done.24 = f32[2,8,256]{2,1,0:T(8,128)S(1)} collective-permute-done((f32[2,8,256]{2,1,0:T(8,128)S(1)}, f32[2,8,256]{2,1,0:T(8,128)S(1)}, u32[]{:S(2)}, u32[]{:S(2)}) %collective-permute-start.24) | collective-permute-done | bytes 16416 | tf_op jit(solution)/shard_map/ppermute | solution.py:13
  90.7 2.9 %fusion.53 = f32[256,2560]{1,0:T(8,128)S(1)} fusion(bf16[640,2560]{1,0:T(8,128)(2,1)S(1)} %copy-done, f32[256,640]{1,0:T(8,128)} %get-tuple-element.41, f32[256,640]{1,0:T(8,128)} %get-tuple-element.39, f32[256]{0:T(256)S(1)} %bitcast.104, f32[256]{0:T(256)S(1)} %bitcast.110, f32[256]{0:T(256)S(1)} %bitcast.108, f32[256]{0:T(256)S(1)} %bitcast.106, ...), kind=kOutput, calls=%fused_computation.150 | convolution fusion | flops 841154560 | bytes 7215104 | tf_op jit(solution)/shard_map/dot_general | solution.py:136
  93.8 2.1 %collective-permute-done.25 = bf16[8,16,2560]{2,1,0:T(8,128)(2,1)S(1)} collective-permute-done((bf16[8,16,2560]{2,1,0:T(8,128)(2,1)S(1)}, bf16[8,16,2560]{2,1,0:T(8,128)(2,1)S(1)}, u32[]{:S(2)}, u32[]{:S(2)}) %collective-permute-start.25) | collective-permute-done | bytes 655392 | tf_op jit(solution)/shard_map/ppermute | solution.py:13
  96.4 2.3 %collective-permute-start.27 = (bf16[2,16,2560]{2,1,0:T(8,128)(2,1)S(1)}, bf16[2,16,2560]{2,1,0:T(8,128)(2,1)S(1)}, u32[]{:S(2)}, u32[]{:S(2)}) collective-permute-start(bf16[2,16,2560]{2,1,0:T(8,128)(2,1)S(1)} %get-tuple-element.25), channel_id=1, source_target_pairs={{0,128},{64,192},{128,0},{192,64},{1,129},{65,193},{129,1},{193,65... | collective-permute-start | bytes 491528 | tf_op jit(solution)/shard_map/ppermute | solution.py:18
  98.8 0.9 collective-permute-start.28
  99.7 7.7 %collective-permute-done.26 = bf16[2,16,2560]{2,1,0:T(8,128)(2,1)S(1)} collective-permute-done((bf16[2,16,2560]{2,1,0:T(8,128)(2,1)S(1)}, bf16[2,16,2560]{2,1,0:T(8,128)(2,1)S(1)}, u32[]{:S(2)}, u32[]{:S(2)}) %collective-permute-start.26) | collective-permute-done | bytes 163872 | tf_op jit(solution)/shard_map/ppermute | solution.py:18
  108.1 0.7 copy-done.1
  108.8 0.9 collective-permute-start.29
  109.7 3.6 %collective-permute-done.29 = bf16[16,2560]{1,0:T(8,128)(2,1)S(1)} collective-permute-done((bf16[16,2560]{1,0:T(8,128)(2,1)S(1)}, bf16[16,2560]{1,0:T(8,128)(2,1)S(1)}, u32[]{:S(2)}, u32[]{:S(2)}) %collective-permute-start.29) | collective-permute-done | bytes 81952 | tf_op jit(solution)/shard_map/ppermute | solution.py:13
  113.4 0.9 fusion.22
  114.3 0.8 reshape.195
  115.1 1.0 copy.16
  116.7 1.0 collective-permute-start.30
  117.7 3.9 %collective-permute-done.30 = f32[2,2,16,320]{3,2,1,0:T(8,128)} collective-permute-done((f32[2,2,16,320]{3,2,1,0:T(8,128)}, f32[2,2,16,320]{3,2,1,0:T(8,128)}, u32[]{:S(2)}, u32[]{:S(2)}) %collective-permute-start.30) | collective-permute-done | bytes 81952 | tf_op jit(solution)/shard_map/ppermute | solution.py:13
  121.6 0.9 bitcast_add_fusion
  123.2 2.0 %collective-permute-start.31 = (f32[2,16,320]{2,1,0:T(8,128)S(1)}, f32[2,16,320]{2,1,0:T(8,128)S(1)}, u32[]{:S(2)}, u32[]{:S(2)}) collective-permute-start(f32[2,16,320]{2,1,0:T(8,128)S(1)} %dynamic-slice_bitcast_fusion.1), channel_id=1, source_target_pairs={{0,4},{2,6},{4,0},{6,2},{8,12},{10,14},{12,8},{14,10},{1,5},{3,7},... | collective-permute-start | bytes 122888 | tf_op jit(solution)/shard_map/ppermute | solution.py:13
  125.2 5.0 %convolution_convert_fusion = bf16[640,2560]{1,0:T(8,128)(2,1)} fusion(bf16[256,6656]{1,0:T(8,128)(2,1)} %constant_dynamic-update-slice_fusion, f32[256,640]{1,0:T(8,128)} %get-tuple-element.41, f32[256,640]{1,0:T(8,128)} %get-tuple-element.39, f32[256]{0:T(256)S(1)} %bitcast.105, f32[256]{0:T(256)S(1)} %bitcast.111, f32[256]{0:T(256)S(1)} %bitcast.109, ...), kind=kOutput, calls=%fused_computation | convolution fusion | flops 842792960 | bytes 5904384 | tf_op jit(solution)/shard_map/dot_general | solution.py:138
  130.4 5.5 %collective-permute-start.32 = (f32[16,320]{1,0:T(8,128)S(1)}, f32[16,320]{1,0:T(8,128)S(1)}, u32[]{:S(2)}, u32[]{:S(2)}) collective-permute-start(f32[16,320]{1,0:T(8,128)S(1)} %dynamic-slice_bitcast_fusion.2), channel_id=1, source_target_pairs={{0,8},{2,10},{4,12},{6,14},{8,0},{10,2},{12,4},{14,6},{1,9},{3,11}... | collective-permute-start | bytes 61448 | tf_op jit(solution)/shard_map/ppermute | solution.py:13
  136.4 1.8 %collective-permute-done.32 = f32[16,320]{1,0:T(8,128)S(1)} collective-permute-done((f32[16,320]{1,0:T(8,128)S(1)}, f32[16,320]{1,0:T(8,128)S(1)}, u32[]{:S(2)}, u32[]{:S(2)}) %collective-permute-start.32) | collective-permute-done | bytes 20512 | tf_op jit(solution)/shard_map/ppermute | solution.py:13
  (131 shorter events, 18.9 us)
Async XLA Ops:
  0.6 47.1 %copy-start = (bf16[640,2560]{1,0:T(8,128)(2,1)S(1)}, bf16[640,2560]{1,0:T(8,128)(2,1)}, u32[]{:S(2)}) copy-start(bf16[640,2560]{1,0:T(8,128)(2,1)} %param.8) | copy-start | bytes 9830404
  2.5 17.3 %collective-permute-start.1 = (bf16[16,6656]{1,0:T(8,128)(2,1)}, bf16[16,6656]{1,0:T(8,128)(2,1)}, u32[]{:S(2)}, u32[]{:S(2)}) collective-permute-start(bf16[16,6656]{1,0:T(8,128)(2,1)} %get-tuple-element.26), channel_id=1, source_target_pairs={{0,32},{32,0},{1,33},{33,1},{2,34},{34,2},{3,35},{35,3},{4,36},{36... | collective-permute-start | bytes 638984 | tf_op jit(solution)/shard_map/ppermute | solution.py:13
  3.7 16.6 %collective-permute-start = (bf16[16,6656]{1,0:T(8,128)(2,1)}, bf16[16,6656]{1,0:T(8,128)(2,1)}, u32[]{:S(2)}, u32[]{:S(2)}) collective-permute-start(bf16[16,6656]{1,0:T(8,128)(2,1)} %get-tuple-element.26), channel_id=1, source_target_pairs={{0,16},{16,0},{1,17},{17,1},{2,18},{18,2},{3,19},{19,3},{4,20},{20... | collective-permute-start | bytes 638984 | tf_op jit(solution)/shard_map/ppermute | solution.py:13
  3.7 11.9 %collective-permute-start.3 = (bf16[16,6656]{1,0:T(8,128)(2,1)}, bf16[16,6656]{1,0:T(8,128)(2,1)}, u32[]{:S(2)}, u32[]{:S(2)}) collective-permute-start(bf16[16,6656]{1,0:T(8,128)(2,1)} %get-tuple-element.26), channel_id=1, source_target_pairs={{0,192},{64,0},{128,64},{192,128},{1,193},{65,1},{129,65},{193,129... | collective-permute-start | bytes 638984 | tf_op jit(solution)/shard_map/ppermute | solution.py:18
  6.8 8.8 %collective-permute-start.7 = (bf16[16,6656]{1,0:T(8,128)(2,1)}, bf16[16,6656]{1,0:T(8,128)(2,1)S(1)}, u32[]{:S(2)}, u32[]{:S(2)}) collective-permute-start(bf16[16,6656]{1,0:T(8,128)(2,1)} %get-tuple-element.26), channel_id=1, source_target_pairs={{0,64},{64,128},{128,192},{192,0},{1,65},{65,129},{129,193},{193,1... | collective-permute-start | bytes 638984 | tf_op jit(solution)/shard_map/ppermute | solution.py:18
  7.8 46.2 %copy-start.5 = (s32[256]{0:T(256)}, s32[256]{0:T(256)S(1)}, u32[]{:S(2)}) copy-start(s32[256]{0:T(256)S(1)} %sub.207) | copy-start | bytes 3076
  15.6 8.1 %collective-permute-start.8 = (bf16[8,6656]{1,0:T(8,128)(2,1)S(1)}, bf16[8,6656]{1,0:T(8,128)(2,1)S(1)}, u32[]{:S(2)}, u32[]{:S(2)}) collective-permute-start(bf16[8,6656]{1,0:T(8,128)(2,1)S(1)} %slice.176), channel_id=1, source_target_pairs={{0,64},{64,128},{128,192},{192,0},{1,65},{65,129},{129,193},{193,1... | collective-permute-start | bytes 319496 | tf_op jit(solution)/shard_map/ppermute | solution.py:18
  16.6 9.0 %collective-permute-start.9 = (bf16[8,6656]{1,0:T(8,128)(2,1)S(1)}, bf16[8,6656]{1,0:T(8,128)(2,1)S(1)}, u32[]{:S(2)}, u32[]{:S(2)}) collective-permute-start(bf16[8,6656]{1,0:T(8,128)(2,1)S(1)} %slice.177), channel_id=1, source_target_pairs={{0,192},{64,0},{128,64},{192,128},{1,193},{65,1},{129,65},{193,129... | collective-permute-start | bytes 319496 | tf_op jit(solution)/shard_map/ppermute | solution.py:18
  19.8 18.2 %collective-permute-start.4 = (bf16[16,6656]{1,0:T(8,128)(2,1)}, bf16[16,6656]{1,0:T(8,128)(2,1)S(1)}, u32[]{:S(2)}, u32[]{:S(2)}) collective-permute-start(bf16[16,6656]{1,0:T(8,128)(2,1)} %collective-permute-done.3), channel_id=1, source_target_pairs={{0,16},{16,0},{1,17},{17,1},{2,18},{18,2},{3,19},{19,3},{4,20},{20... | collective-permute-start | bytes 638984 | tf_op jit(solution)/shard_map/ppermute | solution.py:13
  19.8 13.1 %collective-permute-start.2 = (bf16[16,6656]{1,0:T(8,128)(2,1)}, bf16[16,6656]{1,0:T(8,128)(2,1)S(1)}, u32[]{:S(2)}, u32[]{:S(2)}) collective-permute-start(bf16[16,6656]{1,0:T(8,128)(2,1)} %collective-permute-done.1), channel_id=1, source_target_pairs={{0,16},{16,0},{1,17},{17,1},{2,18},{18,2},{3,19},{19,3},{4,20},{20... | collective-permute-start | bytes 638984 | tf_op jit(solution)/shard_map/ppermute | solution.py:13
  20.3 12.0 %collective-permute-start.5 = (bf16[16,6656]{1,0:T(8,128)(2,1)}, bf16[16,6656]{1,0:T(8,128)(2,1)S(1)}, u32[]{:S(2)}, u32[]{:S(2)}) collective-permute-start(bf16[16,6656]{1,0:T(8,128)(2,1)} %collective-permute-done.1), channel_id=1, source_target_pairs={{0,192},{64,0},{128,64},{192,128},{1,193},{65,1},{129,65},{193,129... | collective-permute-start | bytes 638984 | tf_op jit(solution)/shard_map/ppermute | solution.py:18
  23.7 8.6 %collective-permute-start.11 = (bf16[16,6656]{1,0:T(8,128)(2,1)}, bf16[16,6656]{1,0:T(8,128)(2,1)S(1)}, u32[]{:S(2)}, u32[]{:S(2)}) collective-permute-start(bf16[16,6656]{1,0:T(8,128)(2,1)} %collective-permute-done.1), channel_id=1, source_target_pairs={{0,64},{64,128},{128,192},{192,0},{1,65},{65,129},{129,193},{193,1... | collective-permute-start | bytes 638984 | tf_op jit(solution)/shard_map/ppermute | solution.py:18
  25.6 20.0 %collective-permute-start.15 = (bf16[16,6656]{1,0:T(8,128)(2,1)S(1)}, bf16[16,6656]{1,0:T(8,128)(2,1)S(1)}, u32[]{:S(2)}, u32[]{:S(2)}) collective-permute-start(bf16[16,6656]{1,0:T(8,128)(2,1)S(1)} %collective-permute-done.7), channel_id=1, source_target_pairs={{0,16},{16,0},{1,17},{17,1},{2,18},{18,2},{3,19},{19,3},{4,20},{20... | collective-permute-start | bytes 638984 | tf_op jit(solution)/shard_map/ppermute | solution.py:13
  32.3 10.0 %collective-permute-start.10 = (bf16[16,6656]{1,0:T(8,128)(2,1)S(1)}, bf16[16,6656]{1,0:T(8,128)(2,1)S(1)}, u32[]{:S(2)}, u32[]{:S(2)}) collective-permute-start(bf16[16,6656]{1,0:T(8,128)(2,1)S(1)} %pad_maximum_fusion), channel_id=1, source_target_pairs={{0,16},{16,0},{1,17},{17,1},{2,18},{18,2},{3,19},{19,3},{4,20},{20... | collective-permute-start | bytes 638984 | tf_op jit(solution)/shard_map/ppermute | solution.py:13
  32.3 7.1 %collective-permute-start.12 = (bf16[8,6656]{1,0:T(8,128)(2,1)S(1)}, bf16[8,6656]{1,0:T(8,128)(2,1)S(1)}, u32[]{:S(2)}, u32[]{:S(2)}) collective-permute-start(bf16[8,6656]{1,0:T(8,128)(2,1)S(1)} %slice.178), channel_id=1, source_target_pairs={{0,64},{64,128},{128,192},{192,0},{1,65},{65,129},{129,193},{193,1... | collective-permute-start | bytes 319496 | tf_op jit(solution)/shard_map/ppermute | solution.py:18
  32.9 7.0 %collective-permute-start.13 = (bf16[8,6656]{1,0:T(8,128)(2,1)S(1)}, bf16[8,6656]{1,0:T(8,128)(2,1)S(1)}, u32[]{:S(2)}, u32[]{:S(2)}) collective-permute-start(bf16[8,6656]{1,0:T(8,128)(2,1)S(1)} %slice.179), channel_id=1, source_target_pairs={{0,192},{64,0},{128,64},{192,128},{1,193},{65,1},{129,65},{193,129... | collective-permute-start | bytes 319496 | tf_op jit(solution)/shard_map/ppermute | solution.py:18
  38.0 2.2 %collective-permute-start.6 = (bf16[16,6656]{1,0:T(8,128)(2,1)S(1)}, bf16[16,6656]{1,0:T(8,128)(2,1)S(1)}, u32[]{:S(2)}, u32[]{:S(2)}) collective-permute-start(bf16[16,6656]{1,0:T(8,128)(2,1)S(1)} %collective-permute-done.5), channel_id=1, source_target_pairs={{0,16},{16,0},{1,17},{17,1},{2,18},{18,2},{3,19},{19,3},{4,20},{20... | collective-permute-start | bytes 638984 | tf_op jit(solution)/shard_map/ppermute | solution.py:13
  39.4 7.6 %collective-permute-start.16 = (bf16[16,6656]{1,0:T(8,128)(2,1)S(1)}, bf16[16,6656]{1,0:T(8,128)(2,1)S(1)}, u32[]{:S(2)}, u32[]{:S(2)}) collective-permute-start(bf16[16,6656]{1,0:T(8,128)(2,1)S(1)} %collective-permute-done.11), channel_id=1, source_target_pairs={{0,16},{16,0},{1,17},{17,1},{2,18},{18,2},{3,19},{19,3},{4,20},{20... | collective-permute-start | bytes 638984 | tf_op jit(solution)/shard_map/ppermute | solution.py:13
  39.9 4.3 %collective-permute-start.14 = (bf16[16,6656]{1,0:T(8,128)(2,1)S(1)}, bf16[16,6656]{1,0:T(8,128)(2,1)S(1)}, u32[]{:S(2)}, u32[]{:S(2)}) collective-permute-start(bf16[16,6656]{1,0:T(8,128)(2,1)S(1)} %pad_maximum_fusion.1), channel_id=1, source_target_pairs={{0,16},{16,0},{1,17},{17,1},{2,18},{18,2},{3,19},{19,3},{4,20},{20... | collective-permute-start | bytes 638984 | tf_op jit(solution)/shard_map/ppermute | solution.py:13
  42.9 8.3 %copy-start.7 = (bf16[640,4096]{1,0:T(8,128)(2,1)S(1)}, bf16[640,4096]{1,0:T(8,128)(2,1)}, u32[]{:S(2)}) copy-start(bf16[640,4096]{1,0:T(8,128)(2,1)} %param.9) | copy-start | bytes 15728644
  47.8 3.5 %copy-start.4 = (bf16[256,6656]{1,0:T(8,128)(2,1)S(1)}, bf16[256,6656]{1,0:T(8,128)(2,1)}, u32[]{:S(2)}) copy-start(bf16[256,6656]{1,0:T(8,128)(2,1)} %constant_dynamic-update-slice_fusion) | copy-start | bytes 10223620
  58.0 1.5 %collective-permute-start.17 = (f32[2,8,256]{2,1,0:T(8,128)}, f32[2,8,256]{2,1,0:T(8,128)S(1)}, u32[]{:S(2)}, u32[]{:S(2)}) collective-permute-start(f32[2,8,256]{2,1,0:T(8,128)} %reshape.192), channel_id=1, source_target_pairs={{0,16},{16,0},{1,17},{17,1},{2,18},{18,2},{3,19},{19,3},{4,20},{20... | collective-permute-start | bytes 49160 | tf_op jit(solution)/shard_map/ppermute | solution.py:13
  59.6 3.8 %collective-permute-start.18 = (f32[2,8,256]{2,1,0:T(8,128)S(1)}, f32[2,8,256]{2,1,0:T(8,128)S(1)}, u32[]{:S(2)}, u32[]{:S(2)}) collective-permute-start(f32[2,8,256]{2,1,0:T(8,128)S(1)} %pad_maximum_fusion.3), channel_id=1, source_target_pairs={{0,32},{32,0},{1,33},{33,1},{2,34},{34,2},{3,35},{35,3},{4,36},{36... | collective-permute-start | bytes 49160 | tf_op jit(solution)/shard_map/ppermute | solution.py:13
  63.5 5.0 %collective-permute-start.19 = (f32[2,8,256]{2,1,0:T(8,128)S(1)}, f32[2,8,256]{2,1,0:T(8,128)S(1)}, u32[]{:S(2)}, u32[]{:S(2)}) collective-permute-start(f32[2,8,256]{2,1,0:T(8,128)S(1)} %pad_maximum_fusion.4), channel_id=1, source_target_pairs={{0,64},{64,128},{128,192},{192,0},{1,65},{65,129},{129,193},{193,1... | collective-permute-start | bytes 49160 | tf_op jit(solution)/shard_map/ppermute | solution.py:18
  63.6 4.9 %collective-permute-start.20 = (f32[2,8,256]{2,1,0:T(8,128)S(1)}, f32[2,8,256]{2,1,0:T(8,128)S(1)}, u32[]{:S(2)}, u32[]{:S(2)}) collective-permute-start(f32[2,8,256]{2,1,0:T(8,128)S(1)} %pad_maximum_fusion.4), channel_id=1, source_target_pairs={{0,192},{64,0},{128,64},{192,128},{1,193},{65,1},{129,65},{193,129... | collective-permute-start | bytes 49160 | tf_op jit(solution)/shard_map/ppermute | solution.py:18
  66.8 5.2 %collective-permute-start.21 = (f32[2,8,256]{2,1,0:T(8,128)S(1)}, f32[2,8,256]{2,1,0:T(8,128)S(1)}, u32[]{:S(2)}, u32[]{:S(2)}) collective-permute-start(f32[2,8,256]{2,1,0:T(8,128)S(1)} %pad_maximum_fusion.4), channel_id=1, source_target_pairs={{0,128},{64,192},{128,0},{192,64},{1,129},{65,193},{129,1},{193,65... | collective-permute-start | bytes 49160 | tf_op jit(solution)/shard_map/ppermute | solution.py:18
  72.1 3.8 %collective-permute-start.22 = (f32[2,8,256]{2,1,0:T(8,128)S(1)}, f32[2,8,256]{2,1,0:T(8,128)S(1)}, u32[]{:S(2)}, u32[]{:S(2)}) collective-permute-start(f32[2,8,256]{2,1,0:T(8,128)S(1)} %pad_maximum_fusion.5), channel_id=1, source_target_pairs={{0,2},{2,0},{4,6},{6,4},{8,10},{10,8},{12,14},{14,12},{1,3},{3,1},... | collective-permute-start | bytes 49160 | tf_op jit(solution)/shard_map/ppermute | solution.py:13
  75.9 5.1 %collective-permute-start.23 = (f32[2,8,256]{2,1,0:T(8,128)S(1)}, f32[2,8,256]{2,1,0:T(8,128)S(1)}, u32[]{:S(2)}, u32[]{:S(2)}) collective-permute-start(f32[2,8,256]{2,1,0:T(8,128)S(1)} %pad_maximum_fusion.6), channel_id=1, source_target_pairs={{0,4},{2,6},{4,0},{6,2},{8,12},{10,14},{12,8},{14,10},{1,5},{3,7},... | collective-permute-start | bytes 49160 | tf_op jit(solution)/shard_map/ppermute | solution.py:13
  81.0 8.7 %collective-permute-start.24 = (f32[2,8,256]{2,1,0:T(8,128)S(1)}, f32[2,8,256]{2,1,0:T(8,128)S(1)}, u32[]{:S(2)}, u32[]{:S(2)}) collective-permute-start(f32[2,8,256]{2,1,0:T(8,128)S(1)} %pad_maximum_fusion.7), channel_id=1, source_target_pairs={{0,8},{2,10},{4,12},{6,14},{8,0},{10,2},{12,4},{14,6},{1,9},{3,11}... | collective-permute-start | bytes 49160 | tf_op jit(solution)/shard_map/ppermute | solution.py:13
  93.7 31.5 %copy-start.6 = (s32[256]{0:T(256)S(1)}, s32[256]{0:T(256)}, u32[]{:S(2)}) copy-start(s32[256]{0:T(256)} %copy-done.5) | copy-start | bytes 3076
  93.7 2.2 %collective-permute-start.25 = (bf16[8,16,2560]{2,1,0:T(8,128)(2,1)S(1)}, bf16[8,16,2560]{2,1,0:T(8,128)(2,1)S(1)}, u32[]{:S(2)}, u32[]{:S(2)}) collective-permute-start(bf16[8,16,2560]{2,1,0:T(8,128)(2,1)S(1)} %fusion.6), channel_id=1, source_target_pairs={{0,16},{16,0},{1,17},{17,1},{2,18},{18,2},{3,19},{19,3},{4,20},{20... | collective-permute-start | bytes 1966088 | tf_op jit(solution)/shard_map/ppermute | solution.py:13
  96.1 11.3 %collective-permute-start.26 = (bf16[2,16,2560]{2,1,0:T(8,128)(2,1)S(1)}, bf16[2,16,2560]{2,1,0:T(8,128)(2,1)S(1)}, u32[]{:S(2)}, u32[]{:S(2)}) collective-permute-start(bf16[2,16,2560]{2,1,0:T(8,128)(2,1)S(1)} %get-tuple-element.23), channel_id=1, source_target_pairs={{0,64},{64,128},{128,192},{192,0},{1,65},{65,129},{129,193},{193,1... | collective-permute-start | bytes 491528 | tf_op jit(solution)/shard_map/ppermute | solution.py:18
  96.4 11.0 %collective-permute-start.27 = (bf16[2,16,2560]{2,1,0:T(8,128)(2,1)S(1)}, bf16[2,16,2560]{2,1,0:T(8,128)(2,1)S(1)}, u32[]{:S(2)}, u32[]{:S(2)}) collective-permute-start(bf16[2,16,2560]{2,1,0:T(8,128)(2,1)S(1)} %get-tuple-element.25), channel_id=1, source_target_pairs={{0,128},{64,192},{128,0},{192,64},{1,129},{65,193},{129,1},{193,65... | collective-permute-start | bytes 491528 | tf_op jit(solution)/shard_map/ppermute | solution.py:18
  98.8 9.3 %collective-permute-start.28 = (bf16[2,16,2560]{2,1,0:T(8,128)(2,1)S(1)}, bf16[2,16,2560]{2,1,0:T(8,128)(2,1)S(1)}, u32[]{:S(2)}, u32[]{:S(2)}) collective-permute-start(bf16[2,16,2560]{2,1,0:T(8,128)(2,1)S(1)} %get-tuple-element.24), channel_id=1, source_target_pairs={{0,192},{64,0},{128,64},{192,128},{1,193},{65,1},{129,65},{193,129... | collective-permute-start | bytes 491528 | tf_op jit(solution)/shard_map/ppermute | solution.py:18
  108.1 0.7 copy-start.1
  108.8 4.5 %collective-permute-start.29 = (bf16[16,2560]{1,0:T(8,128)(2,1)S(1)}, bf16[16,2560]{1,0:T(8,128)(2,1)S(1)}, u32[]{:S(2)}, u32[]{:S(2)}) collective-permute-start(bf16[16,2560]{1,0:T(8,128)(2,1)S(1)} %fusion.33), channel_id=1, source_target_pairs={{0,32},{32,0},{1,33},{33,1},{2,34},{34,2},{3,35},{35,3},{4,36},{36... | collective-permute-start | bytes 245768 | tf_op jit(solution)/shard_map/ppermute | solution.py:13
  116.7 4.9 %collective-permute-start.30 = (f32[2,2,16,320]{3,2,1,0:T(8,128)}, f32[2,2,16,320]{3,2,1,0:T(8,128)}, u32[]{:S(2)}, u32[]{:S(2)}) collective-permute-start(f32[2,2,16,320]{3,2,1,0:T(8,128)} %dynamic-slice_bitcast_fusion), channel_id=1, source_target_pairs={{0,2},{2,0},{4,6},{6,4},{8,10},{10,8},{12,14},{14,12},{1,3},{3,1},... | collective-permute-start | bytes 245768 | tf_op jit(solution)/shard_map/ppermute | solution.py:13
  122.5 0.6 copy-start.2
  123.2 7.2 %copy-start.3 = (f32[2,2,16,320]{3,2,1,0:T(8,128)S(1)}, f32[2,2,16,320]{3,2,1,0:T(8,128)}, u32[]{:S(2)}) copy-start(f32[2,2,16,320]{3,2,1,0:T(8,128)} %copy-done.2) | copy-start | bytes 245764
  123.2 7.2 %collective-permute-start.31 = (f32[2,16,320]{2,1,0:T(8,128)S(1)}, f32[2,16,320]{2,1,0:T(8,128)S(1)}, u32[]{:S(2)}, u32[]{:S(2)}) collective-permute-start(f32[2,16,320]{2,1,0:T(8,128)S(1)} %dynamic-slice_bitcast_fusion.1), channel_id=1, source_target_pairs={{0,4},{2,6},{4,0},{6,2},{8,12},{10,14},{12,8},{14,10},{1,5},{3,7},... | collective-permute-start | bytes 122888 | tf_op jit(solution)/shard_map/ppermute | solution.py:13
  130.4 7.8 %collective-permute-start.32 = (f32[16,320]{1,0:T(8,128)S(1)}, f32[16,320]{1,0:T(8,128)S(1)}, u32[]{:S(2)}, u32[]{:S(2)}) collective-permute-start(f32[16,320]{1,0:T(8,128)S(1)} %dynamic-slice_bitcast_fusion.2), channel_id=1, source_target_pairs={{0,8},{2,10},{4,12},{6,14},{8,0},{10,2},{12,4},{14,6},{1,9},{3,11}... | collective-permute-start | bytes 61448 | tf_op jit(solution)/shard_map/ppermute | solution.py:13

commit v2 on v1

v2 whole, which is shorter than its diff:
```python
import jax
import jax.numpy as jnp
import numpy as np
from jax import lax
from jax.experimental import pallas as pl
from jax.experimental.pallas import tpu as pltpu
from jax.sharding import Mesh, PartitionSpec as P

RING_Y, PAIR_X, CORES, RING_Z = 4, 2, 2, 8
SIZES = {"y": RING_Y, "x": PAIR_X, "c": CORES, "z": RING_Z}
MB = 1 << 20
bf16, f32 = jnp.bfloat16, jnp.float32
VMEM = pl.BlockSpec(memory_space=pltpu.VMEM)
SMEM = pl.BlockSpec(memory_space=pltpu.SMEM)


def swap(value, axis, mask=1):
    return lax.ppermute(value, axis, [(i, i ^ mask) for i in range(SIZES[axis])])


def shift(value, axis, step):
    size = SIZES[axis]
    return lax.ppermute(value, axis, [(i, (i + step) % size) for i in range(size)])


EARLY = ((0, 0), (0, 1), (1, 0), (3, 0))
LATE = ((2, 0), (2, 1), (1, 1), (3, 1))


def gather_rows(block):
    across = swap(block, "x")
    prev = shift(block, "y", 1)
    next_ = shift(block, "y", 3)
    prev_across = swap(prev, "x")
    next_across = swap(next_, "x")
    held, across = lax.optimization_barrier((block, across))
    far = shift(held, "y", 2)
    far_across = shift(across, "y", 2)
    early = [block, across, next_, prev]
    return early + [swap(piece, "c") for piece in early], (far, far_across, next_across, prev_across)


def first_entry(vocab):
    y, x, c, z = (lax.axis_index(a) for a in ("y", "x", "c", "z"))
    return (((y * PAIR_X + x) * CORES + c) * RING_Z + z) * vocab


def permuted(v, pick, back):
    dims = (((1,), (1,)), ((), ())) if back else (((1,), (0,)), ((), ()))
    out = None
    for _ in range(3):
        part = v.astype(bf16)
        v = v - part.astype(f32)
        moved = lax.dot_general(part, pick, dims, preferred_element_type=f32)
        out = moved if out is None else out + moved
    return out


def join_kernel(a_ref, b_ref, tgt_ref, out_ref, row_ref, pick_ref, sems):
    width = a_ref.shape[1]
    copies = [
        pltpu.make_async_copy(a_ref, out_ref.at[:, :width], sems.at[0]),
        pltpu.make_async_copy(b_ref, out_ref.at[:, width:], sems.at[1]),
    ]
    for copy in copies:
        copy.start()
    to = lax.broadcasted_iota(jnp.int32, (1, 256), 1)
    place = lax.rem(to // 16, 4) + to // 128 * 4
    dy, dx = jnp.zeros_like(to), jnp.zeros_like(to)
    for i, (v, w) in enumerate(EARLY + LATE):
        dy = jnp.where(place == i, v, dy)
        dx = jnp.where(place == i, w, dx)
    at_c = lax.rem(lax.rem(to // 64, CORES) + lax.axis_index("c"), CORES)
    at_y = lax.rem(dy + lax.axis_index("y"), RING_Y)
    at_x = lax.rem(dx + lax.axis_index("x"), PAIR_X)
    section = (at_y * PAIR_X + at_x) * CORES + at_c
    source = lax.rem(to // 8, 2) * 128 + section * 8 + lax.rem(to, 8)
    pick = lax.broadcasted_iota(jnp.int32, (256, 256), 0) == source
    pick = jnp.where(pick, 1.0, 0.0).astype(bf16)
    pick_ref[...] = pick
    tgt = jnp.concatenate([tgt_ref[0:1], tgt_ref[1:2]], 1).astype(f32)
    tgt = jnp.concatenate([tgt, jnp.zeros((7, 256), f32)], 0)
    row_ref[...] = permuted(tgt, pick, False)[0:1].astype(jnp.int32)
    for copy in copies:
        copy.wait()


def join(student, teacher, targets):
    rows = student.shape[0]
    width = student.shape[1] + teacher.shape[1]
    shape = jax.ShapeDtypeStruct
    return pl.pallas_call(
        join_kernel,
        out_shape=(
            shape((rows, width), bf16),
            shape((1, 256), jnp.int32),
            shape((256, 256), bf16),
        ),
        in_specs=[pl.BlockSpec(memory_space=pl.ANY)] * 2 + [VMEM],
        out_specs=(VMEM,) * 3,
        scratch_shapes=[pltpu.SemaphoreType.DMA((2,))],
        compiler_params=pltpu.CompilerParams(vmem_limit_bytes=4 * MB),
        name="join",
    )(student, teacher, targets)


def half_logits(blocks, ws_ref, wt_ref, tgt, s_ref, t_ref, hs_ref, ht_ref):
    width = ws_ref.shape[1]
    for i, ref in enumerate(blocks):
        hs_ref[i * 16 : i * 16 + 16, :] = ref[:, :width]
        ht_ref[i * 16 : i * 16 + 16, :] = ref[:, width:]
    dims = (((1,), (1,)), ((), ()))
    s = lax.dot_general(ws_ref[...], hs_ref[...], dims, preferred_element_type=f32)
    s_ref[...] = s
    ms = jnp.max(s, axis=0, keepdims=True)
    total = lambda v: jnp.sum(v, axis=0, keepdims=True)
    hit = lax.broadcasted_iota(jnp.int32, s.shape, 0) == tgt - first_entry(s.shape[0])
    z1 = total(jnp.exp(s - ms))
    z2 = total(jnp.exp((s - ms) * 0.5))
    picked = total(jnp.where(hit, s, 0.0))
    t = lax.dot_general(wt_ref[...], ht_ref[...], dims, preferred_element_type=f32)
    t_ref[...] = t
    mt = jnp.max(t, axis=0, keepdims=True)
    et = jnp.exp((t - mt) * 0.5)
    zt = total(et)
    cross = total(et * ((t - s_ref[...]) * 0.5))
    zero = jnp.zeros_like(ms)
    rows = [ms, ms * 0.5, mt * 0.5, mt * 0.5, zero, zero, zero, zero]
    return jnp.concatenate(rows + [z1, z2, zt, cross, picked, zero, zero, zero], 0)


def early_kernel(*refs):
    ws_ref, wt_ref, tgt_ref = refs[8:11]
    s_ref, t_ref, hs_ref, part_ref, ht_ref = refs[11:]
    tgt = tgt_ref[:, :128]
    part_ref[...] = half_logits(refs[:8], ws_ref, wt_ref, tgt, s_ref, t_ref, hs_ref, ht_ref)


def late_kernel(*refs):
    ws_ref, wt_ref, tgt_ref, early_ref, pick_ref = refs[8:13]
    s_ref, t_ref, hs_ref, part_ref, ht_ref = refs[13:]
    tgt = tgt_ref[:, 128:]
    part = half_logits(refs[:8], ws_ref, wt_ref, tgt, s_ref, t_ref, hs_ref, ht_ref)
    part = jnp.concatenate([early_ref[...], part], 1)
    part_ref[...] = permuted(part, pick_ref[...], True)


def compute_logits(blocks, ws, wt, tgt, extra=()):
    vocab, width = ws.shape
    rows = 128
    shape = jax.ShapeDtypeStruct
    return pl.pallas_call(
        late_kernel if extra else early_kernel,
        out_shape=(
            shape((vocab, rows), f32),
            shape((vocab, rows), f32),
            shape((rows, width), bf16),
            shape((16, 2 * rows if extra else rows), f32),
        ),
        in_specs=[VMEM] * (11 + len(extra)),
        out_specs=(VMEM,) * 4,
        scratch_shapes=[pltpu.VMEM((rows, wt.shape[1]), bf16)],
        compiler_params=pltpu.CompilerParams(vmem_limit_bytes=20 * MB),
        cost_estimate=pl.CostEstimate(
            flops=2 * vocab * rows * (width + wt.shape[1]),
            bytes_accessed=12 * MB,
            transcendentals=3 * vocab * rows,
        ),
        name="late_logits" if extra else "early_logits",
    )(*blocks, ws, wt, tgt, *extra)


def slope_kernel(*refs):
    s_refs, t_refs = refs[:2], refs[2:4]
    part_ref, pick_ref, tgt_ref, ws_ref, g_ref, send_ref, keep_ref, loss_ref = refs[4:]
    part = permuted(part_ref[...], pick_ref[...], False)
    first = first_entry(ws_ref.shape[0])
    ms, half_mt = part[0:1], part[2:3]
    z1, z2, zt, cross, picked = (part[8 + i : 9 + i] for i in range(5))
    loss = 2.0 * (cross / zt - (half_mt + jnp.log(zt)) + (ms * 0.5 + jnp.log(z2)))
    loss = loss + 0.5 * (ms + jnp.log(z1) - picked)
    micro = lax.rem(lax.broadcasted_iota(jnp.int32, loss.shape, 1) // 8, 2)
    for i in range(2):
        loss_ref[i] = jnp.sum(jnp.where(micro == i, loss, 0.0)) * (1.0 / 128.0)
    tgt = tgt_ref[...] - first
    r2, rt, r1 = 1.0 / z2, 1.0 / zt, 0.5 / z1
    for i in range(2):
        at = slice(i * 128, i * 128 + 128)
        d = s_refs[i][...] - ms[:, at]
        hit = lax.broadcasted_iota(jnp.int32, d.shape, 0) == tgt[:, at]
        g = jnp.exp(d * 0.5) * r2[:, at]
        g = g - jnp.exp(t_refs[i][...] * 0.5 - half_mt[:, at]) * rt[:, at]
        g = g + (jnp.exp(d) * r1[:, at] - jnp.where(hit, 0.5, 0.0))
        g_ref[:, at] = g.astype(bf16)
    p = lax.dot_general(
        g_ref[...], ws_ref[...], (((0,), (0,)), ((), ())), preferred_element_type=f32
    )
    for i, (dy, dx) in enumerate(EARLY + LATE):
        out = slice((dy * PAIR_X + dx) * 16, (dy * PAIR_X + dx) * 16 + 16)
        row = i // 4 * 128 + i % 4 * 16
        keep_ref[out] = p[row : row + 16]
        send_ref[out] = p[row + 64 : row + 80].astype(bf16)


def compute_slope(s, t, part, pick, tgt, ws):
    vocab, width = ws.shape
    rows = 256
    shape = jax.ShapeDtypeStruct
    return pl.pallas_call(
        slope_kernel,
        out_shape=(
            shape((vocab, rows), bf16),
            shape((rows // 2, width), bf16),
            shape((rows // 2, width), f32),
            shape((2,), f32),
        ),
        in_specs=[VMEM] * 8,
        out_specs=(VMEM,) * 3 + (SMEM,),
        compiler_params=pltpu.CompilerParams(vmem_limit_bytes=20 * MB),
        cost_estimate=pl.CostEstimate(
            flops=2 * vocab * rows * width, bytes_accessed=8 * MB, transcendentals=3 * vocab * rows
        ),
        name="slope",
    )(*s, *t, part, pick, tgt, ws)


def weight_kernel(g_ref, a_ref, b_ref, out_ref, done_ref):
    h = jnp.concatenate([a_ref[...], b_ref[...]], 0)
    out_ref[...] = jnp.dot(g_ref[...], h, preferred_element_type=f32).astype(bf16)
    done_ref[...] = jnp.zeros(done_ref.shape, f32)


def compute_weight(g, early, late):
    vocab, rows = g.shape
    width = early.shape[1]
    tile = 128
    shape = jax.ShapeDtypeStruct
    return pl.pallas_call(
        weight_kernel,
        out_shape=(shape((vocab, width), bf16), shape((8, 128), f32)),
        grid=(vocab // tile,),
        in_specs=[
            pl.BlockSpec((tile, rows), lambda i: (i, 0)),
            pl.BlockSpec((rows // 2, width), lambda i: (0, 0)),
            pl.BlockSpec((rows // 2, width), lambda i: (0, 0)),
        ],
        out_specs=(
            pl.BlockSpec((tile, width), lambda i: (i, 0)),
            pl.BlockSpec((8, 128), lambda i: (0, 0)),
        ),
        compiler_params=pltpu.CompilerParams(vmem_limit_bytes=12 * MB),
        cost_estimate=pl.CostEstimate(
            flops=2 * vocab * rows * width, bytes_accessed=6 * MB, transcendentals=0
        ),
        name="weight",
    )(g, early, late)


def split_kernel(own_ref, got_ref, ahead_ref, behind_ref, keep_ref, tmp_ref):
    z = lax.axis_index("z")
    width = own_ref.shape[1] // RING_Z
    v = own_ref[...] + got_ref[...].astype(f32)
    for k in range(RING_Z):
        tmp_ref[k] = v[:, k * width : (k + 1) * width]
    at = lambda d: tmp_ref[lax.rem(z + (d + RING_Z), RING_Z)]
    for i, d in enumerate((2, 3, 4)):
        ahead_ref[i] = at(d)
    for i, d in enumerate((-3, -2)):
        behind_ref[i] = at(d)
    for i, d in enumerate((-1, 0, 1)):
        keep_ref[i] = at(d)


def split_features(own, got):
    rows, width = own.shape
    shape = lambda n: jax.ShapeDtypeStruct((n, rows, width // RING_Z), f32)
    return pl.pallas_call(
        split_kernel,
        out_shape=(shape(3), shape(2), shape(3)),
        in_specs=[VMEM, VMEM],
        out_specs=(VMEM,) * 3,
        scratch_shapes=[pltpu.VMEM((RING_Z, rows, width // RING_Z), f32)],
        compiler_params=pltpu.CompilerParams(vmem_limit_bytes=4 * MB),
        name="split",
    )(own, got)


def merge(parts):
    tops = [p[:8] for p in parts]
    top = tops[0]
    for v in tops[1:]:
        top = jnp.maximum(top, v)
    total = parts[0][8:] * jnp.exp(tops[0] - top)
    for v, p in zip(tops[1:], parts[1:]):
        total = total + p[8:] * jnp.exp(v - top)
    return jnp.concatenate([top, total], 0)


def exchange_totals(part):
    part = merge([part, swap(part, "c")])
    part = merge([part, swap(part, "x")])
    part = merge([part, shift(part, "y", 1), shift(part, "y", 3), shift(part, "y", 2)])
    prev, next_ = shift(part, "z", 1), shift(part, "z", 7)
    two, three = merge([part, prev]), merge([part, prev, next_])
    return merge([three, shift(three, "z", 3), shift(two, "z", 5)])


def core_kernel(keep_ref, got_ref, own_ref, *out_refs):
    rows = own_ref.shape[0]
    own_ref[...] = keep_ref[:rows] + got_ref[:rows].astype(f32)
    for i, ref in enumerate(out_refs):
        at = slice((i + 1) * rows, (i + 2) * rows)
        ref[...] = (keep_ref[at] + got_ref[at].astype(f32)).astype(bf16)


def add_core(keep, got):
    rows, width = keep.shape
    rows = rows // RING_Y
    shape = jax.ShapeDtypeStruct
    return pl.pallas_call(
        core_kernel,
        out_shape=(shape((rows, width), f32),) + (shape((rows, width), bf16),) * 3,
        in_specs=[VMEM] * 2,
        out_specs=(VMEM,) * 4,
        compiler_params=pltpu.CompilerParams(vmem_limit_bytes=8 * MB),
        name="add_core",
    )(keep, got)


def ring_kernel(own_ref, a_ref, b_ref, c_ref, after_ref, keep_ref, send_ref):
    rows = keep_ref.shape[0]
    for i, ref in enumerate((keep_ref, send_ref)):
        at = slice(i * rows, (i + 1) * rows)
        total = own_ref[at] + a_ref[at].astype(f32)
        total = total + b_ref[at].astype(f32) + c_ref[at].astype(f32)
        ref[...] = total.astype(ref.dtype)


def add_ring(own, moved, after):
    rows, width = own.shape
    rows = rows // PAIR_X
    shape = jax.ShapeDtypeStruct
    return pl.pallas_call(
        ring_kernel,
        out_shape=(shape((rows, width), f32), shape((rows, width), bf16)),
        in_specs=[VMEM] * 5,
        out_specs=(VMEM,) * 2,
        compiler_params=pltpu.CompilerParams(vmem_limit_bytes=6 * MB),
        name="add_ring",
    )(own, *moved, after)


def reduce_rows(send, keep, after):
    own, *parts = add_core(keep, swap(send, "c"))
    moved = [shift(part, "y", d + 1) for d, part in enumerate(parts)]
    own, part = add_ring(own, moved, after)
    ahead, behind, mine = split_features(own, swap(part, "x"))
    from_a, from_b = shift(ahead, "z", 3), shift(behind, "z", 5)
    to_next = mine[2] + from_a[2] + from_b[1]
    to_prev = mine[0] + from_a[0]
    own = mine[1] + from_a[1] + from_b[0]
    return own + shift(to_next, "z", 1) + shift(to_prev, "z", 7)


def per_device(hidden_student, hidden_teacher, targets, w_student, w_teacher):
    micro, tokens, _ = hidden_student.shape
    rows = micro * tokens
    block, tgt, pick = join(
        hidden_student.reshape(rows, -1), hidden_teacher.reshape(rows, -1), targets
    )
    early, late = gather_rows(block)
    s_early, t_early, h_early, part = compute_logits(early, w_student, w_teacher, tgt)
    late, part = lax.optimization_barrier((late, part))
    late = list(late) + [swap(piece, "c") for piece in late]
    s_late, t_late, h_late, part = compute_logits(late, w_student, w_teacher, tgt, (part, pick))
    part = exchange_totals(part)
    s, t = (s_early, s_late), (t_early, t_late)
    g, send, keep, loss = compute_slope(s, t, part, pick, tgt, w_student)
    grad_weight, done = compute_weight(g, h_early, h_late)
    grad_hidden = reduce_rows(send, keep, done)
    return loss, grad_hidden.astype(bf16).reshape(micro, tokens, -1), grad_weight


def solution(mesh):
    sec = ("y", "x", "c")
    devices = np.asarray(mesh.devices).reshape(RING_Y, PAIR_X, CORES, RING_Z, -1)
    fine = Mesh(devices, sec + ("z", "dp"))
    return jax.shard_map(
        per_device,
        mesh=fine,
        in_specs=(
            P("dp", sec, None),
            P("dp", sec, None),
            P("dp", None),
            P(sec + ("z",), None),
            P(sec + ("z",), None),
        ),
        out_specs=(P("dp"), P("dp", sec, "z"), P(("dp",) + sec + ("z",), None)),
        check_vma=False,
    )
```

time: 140 us -> 101 us (0.72)
  local copies, waits for them, and re-layouts: 22.5 us -> 6.88 us
  matrix products: 14 us -> 0 us
  Pallas kernels: 0 us -> 11.5 us
  waiting for transfers between devices: 48.1 us -> 39.2 us
  other arithmetic: 8.51 us -> 0.73 us
  starting transfers between devices: 44.6 us -> 41.9 us
    ppermute x19 -> x15, starting transfers between devices: 25.7 us -> 7.62 us  [swap(): lax.ppermute(value, axis, [(i, i ^ mask) for i in range(SIZES[axis])])]
    ppermute x14 -> x18, starting transfers between devices: 18.9 us -> 34.3 us  [shift(): lax.ppermute(value, axis, [(i, (i + step) % size) for i in range(size)])]
    dot_general x4 -> x0, matrix products: 14 us -> none  [the longest x1 4.95 us: per_device(): grad_weight = jnp.dot(g, hs, preferred_element_type=f32).astype(bf16)]
    pallas_call x0 -> x8, Pallas kernels: none -> 11.5 us  [the longest x2 5.44 us: compute_logits(): pl.pallas_call(late_kernel if extra else early_kernel, out_shape=(shape((...]
    unnamed x40 -> x14, local copies, waits for them, and re-layouts: 15.2 us -> 6.88 us
    ppermute x19 -> x15, waiting for transfers between devices: 20.4 us -> 12.5 us  [swap(): lax.ppermute(value, axis, [(i, i ^ mask) for i in range(SIZES[axis])])]
    concatenate x11 -> x6, other arithmetic: 3.01 us -> 0.02 us  [merge(): return jnp.concatenate([top, total], 0)]
    reshape x4 -> x0, local copies, waits for them, and re-layouts: 2.52 us -> none  [the longest x2 0.99 us: to_relative(): return v.reshape(*lead, -1)]
  transfers between devices with their start and end apart: 33 -> 33, of which waited for: 15 -> 22; matrix products, arithmetic and copies ran while one was open for 16% -> 0% of each run, Pallas kernels for 0% -> 6%
where the time goes in v2:
time: 101 us
  starting transfers between devices  41.9 us (41%)
  waiting for transfers between devices  39.2 us (39%)
  Pallas kernels  11.5 us (11%)
  local copies, waits for them, and re-layouts  6.88 us (7%)
    ppermute x18, starting transfers between devices, shift(): lax.ppermute(value, axis, [(i, (i + step) % size) for i in range(size)])  34.3 us
    ppermute x18, waiting for transfers between devices, shift(): lax.ppermute(value, axis, [(i, (i + step) % size) for i in range(size)])  26.7 us
    ppermute x15, waiting for transfers between devices, swap(): lax.ppermute(value, axis, [(i, i ^ mask) for i in range(SIZES[axis])])  12.5 us
    ppermute x15, starting transfers between devices, swap(): lax.ppermute(value, axis, [(i, i ^ mask) for i in range(SIZES[axis])])  7.62 us
    unnamed x14, local copies, waits for them, and re-layouts  6.88 us
    pallas_call x2, Pallas kernels, compute_logits(): pl.pallas_call(late_kernel if extra else early_kernel, out_shape=(shape((...  5.44 us
    pallas_call x1, Pallas kernels, compute_weight(): pl.pallas_call(weight_kernel, out_shape=(shape((vocab, width), bf16), sha...  3.53 us
  transfers between devices with their start and end apart: 33, of which 22 were waited for; matrix products, arithmetic and copies ran while one was open for 0% of the time, Pallas kernels for 6%

profile of v2, /device:TPU:4, one launch (start us, length us, event | category | flops | bytes accessed | tf_op | source)
XLA Modules:
  0.0 101.0 jit_solution(16051052553104850395)
XLA Ops:
  0.6 0.9 copy-done.4
  1.5 0.9 copy-done.5
  2.4 0.7 copy-done.6
  3.5 1.7 %collective-permute-start.2 = (bf16[16,6656]{1,0:T(8,128)(2,1)S(1)}, bf16[16,6656]{1,0:T(8,128)(2,1)S(1)}, u32[]{:S(2)}, u32[]{:S(2)}) collective-permute-start(bf16[16,6656]{1,0:T(8,128)(2,1)S(1)} %get-tuple-element.40.refs_0_), channel_id=1, source_target_pairs={{0,64},{64,128},{128,192},{192,0},{1,65},{65,129},{129,193},{193,1... | collective-permute-start | bytes 638984 | tf_op jit(solution)/shard_map/ppermute | solution.py:23
  5.1 1.7 %collective-permute-start.1 = (bf16[16,6656]{1,0:T(8,128)(2,1)S(1)}, bf16[16,6656]{1,0:T(8,128)(2,1)S(1)}, u32[]{:S(2)}, u32[]{:S(2)}) collective-permute-start(bf16[16,6656]{1,0:T(8,128)(2,1)S(1)} %get-tuple-element.40.refs_0_), channel_id=1, source_target_pairs={{0,192},{64,0},{128,64},{192,128},{1,193},{65,1},{129,65},{193,129... | collective-permute-start | bytes 638984 | tf_op jit(solution)/shard_map/ppermute | solution.py:23
  6.8 1.2 %collective-permute-start = (bf16[16,6656]{1,0:T(8,128)(2,1)S(1)}, bf16[16,6656]{1,0:T(8,128)(2,1)S(1)}, u32[]{:S(2)}, u32[]{:S(2)}) collective-permute-start(bf16[16,6656]{1,0:T(8,128)(2,1)S(1)} %get-tuple-element.40.refs_0_), channel_id=1, source_target_pairs={{0,32},{32,0},{1,33},{33,1},{2,34},{34,2},{3,35},{35,3},{4,36},{36... | collective-permute-start | bytes 638984 | tf_op jit(solution)/shard_map/ppermute | solution.py:18
  8.0 3.8 %collective-permute-done.2.refs_3_ = bf16[16,6656]{1,0:T(8,128)(2,1)S(1)} collective-permute-done((bf16[16,6656]{1,0:T(8,128)(2,1)S(1)}, bf16[16,6656]{1,0:T(8,128)(2,1)S(1)}, u32[]{:S(2)}, u32[]{:S(2)}) %collective-permute-start.2) | collective-permute-done | bytes 213024 | tf_op jit(solution)/shard_map/ppermute | solution.py:23
  11.8 0.5 collective-permute-start.5
  12.3 1.0 %collective-permute-done.refs_1_ = bf16[16,6656]{1,0:T(8,128)(2,1)S(1)} collective-permute-done((bf16[16,6656]{1,0:T(8,128)(2,1)S(1)}, bf16[16,6656]{1,0:T(8,128)(2,1)S(1)}, u32[]{:S(2)}, u32[]{:S(2)}) %collective-permute-start) | collective-permute-done | bytes 213024 | tf_op jit(solution)/shard_map/ppermute | solution.py:18
  13.4 1.9 %collective-permute-start.7 = (bf16[16,6656]{1,0:T(8,128)(2,1)S(1)}, bf16[16,6656]{1,0:T(8,128)(2,1)S(1)}, u32[]{:S(2)}, u32[]{:S(2)}) collective-permute-start(bf16[16,6656]{1,0:T(8,128)(2,1)S(1)} %get-tuple-element.40.refs_0_), channel_id=1, source_target_pairs={{0,128},{64,192},{128,0},{192,64},{1,129},{65,193},{129,1},{193,65... | collective-permute-start | bytes 638984 | tf_op jit(solution)/shard_map/ppermute | solution.py:23
  15.3 1.2 %collective-permute-start.10 = (bf16[16,6656]{1,0:T(8,128)(2,1)S(1)}, bf16[16,6656]{1,0:T(8,128)(2,1)S(1)}, u32[]{:S(2)}, u32[]{:S(2)}) collective-permute-start(bf16[16,6656]{1,0:T(8,128)(2,1)S(1)} %collective-permute-done.2.refs_3_), channel_id=1, source_target_pairs={{0,32},{32,0},{1,33},{33,1},{2,34},{34,2},{3,35},{35,3},{4,36},{36... | collective-permute-start | bytes 638984 | tf_op jit(solution)/shard_map/ppermute | solution.py:18
  16.5 0.8 collective-permute-start.9
  17.3 1.6 %collective-permute-start.8 = (bf16[16,6656]{1,0:T(8,128)(2,1)S(1)}, bf16[16,6656]{1,0:T(8,128)(2,1)S(1)}, u32[]{:S(2)}, u32[]{:S(2)}) collective-permute-start(bf16[16,6656]{1,0:T(8,128)(2,1)S(1)} %collective-permute-done.refs_1_), channel_id=1, source_target_pairs={{0,128},{64,192},{128,0},{192,64},{1,129},{65,193},{129,1},{193,65... | collective-permute-start | bytes 638984 | tf_op jit(solution)/shard_map/ppermute | solution.py:23
  18.9 1.9 %copy-done = bf16[640,2560]{1,0:T(8,128)(2,1)S(1)} copy-done((bf16[640,2560]{1,0:T(8,128)(2,1)S(1)}, bf16[640,2560]{1,0:T(8,128)(2,1)}, u32[]{:S(2)}) %copy-start) | copy-done | bytes 3276824
  20.9 2.5 %copy-done.2 = bf16[640,4096]{1,0:T(8,128)(2,1)S(1)} copy-done((bf16[640,4096]{1,0:T(8,128)(2,1)S(1)}, bf16[640,4096]{1,0:T(8,128)(2,1)}, u32[]{:S(2)}) %copy-start.2) | copy-done | bytes 5242904
  23.4 2.6 %early_logits.1 = (f32[640,128]{1,0:T(8,128)S(1)}, f32[640,128]{1,0:T(8,128)S(1)}, bf16[128,2560]{1,0:T(8,128)(2,1)S(1)}, f32[16,128]{1,0:T(8,128)S(1)}) custom-call(bf16[16,6656]{1,0:T(8,128)(2,1)S(1)} %get-tuple-element.40.refs_0_, bf16[16,6656]{1,0:T(8,128)(2,1)S(1)} %collective-permute-done.refs_1_, bf16[16,6656]{1,0:T(8,128)(2,1)S(1)} %collective-permute-done.1.refs_2_, ...), custom_call_target="tpu_custom_call" | custom-call | flops 1090519040 | bytes 12582912 | tf_op jit(solution)/shard_map/early_logits/pallas_call | solution.py:152
  25.9 1.2 %collective-permute-done.9.refs_2_ = bf16[16,6656]{1,0:T(8,128)(2,1)S(1)} collective-permute-done((bf16[16,6656]{1,0:T(8,128)(2,1)S(1)}, bf16[16,6656]{1,0:T(8,128)(2,1)S(1)}, u32[]{:S(2)}, u32[]{:S(2)}) %collective-permute-start.9) | collective-permute-done | bytes 213024 | tf_op jit(solution)/shard_map/ppermute | solution.py:18
  27.2 0.5 collective-permute-start.12
  29.6 2.9 %late_logits.1 = (f32[640,128]{1,0:T(8,128)S(1)}, f32[640,128]{1,0:T(8,128)S(1)}, bf16[128,2560]{1,0:T(8,128)(2,1)S(1)}, f32[16,256]{1,0:T(8,128)S(1)}) custom-call(bf16[16,6656]{1,0:T(8,128)(2,1)S(1)} %collective-permute-done.7.refs_0_, bf16[16,6656]{1,0:T(8,128)(2,1)S(1)} %collective-permute-done.8.refs_1_, ...), custom_call_target="tpu_custom_call" | custom-call | flops 1090519040 | bytes 12582912 | tf_op jit(solution)/shard_map/late_logits/pallas_call | solution.py:152
  32.7 1.0 collective-permute-done.15
  33.7 1.3 %collective-permute-start.16 = (f32[16,256]{1,0:T(8,128)S(1)}, f32[16,256]{1,0:T(8,128)S(1)}, u32[]{:S(2)}, u32[]{:S(2)}) collective-permute-start(f32[16,256]{1,0:T(8,128)S(1)} %pad_maximum_fusion), channel_id=1, source_target_pairs={{0,32},{32,0},{1,33},{33,1},{2,34},{34,2},{3,35},{35,3},{4,36},{36... | collective-permute-start | bytes 49160 | tf_op jit(solution)/shard_map/ppermute | solution.py:18
  34.9 2.5 %collective-permute-done.16 = f32[16,256]{1,0:T(8,128)S(1)} collective-permute-done((f32[16,256]{1,0:T(8,128)S(1)}, f32[16,256]{1,0:T(8,128)S(1)}, u32[]{:S(2)}, u32[]{:S(2)}) %collective-permute-start.16) | collective-permute-done | bytes 16416 | tf_op jit(solution)/shard_map/ppermute | solution.py:18
  37.5 1.8 %collective-permute-start.19 = (f32[16,256]{1,0:T(8,128)S(1)}, f32[16,256]{1,0:T(8,128)S(1)}, u32[]{:S(2)}, u32[]{:S(2)}) collective-permute-start(f32[16,256]{1,0:T(8,128)S(1)} %pad_maximum_fusion.1), channel_id=1, source_target_pairs={{0,128},{64,192},{128,0},{192,64},{1,129},{65,193},{129,1},{193,65... | collective-permute-start | bytes 49160 | tf_op jit(solution)/shard_map/ppermute | solution.py:23
  39.4 1.6 %collective-permute-start.18 = (f32[16,256]{1,0:T(8,128)S(1)}, f32[16,256]{1,0:T(8,128)S(1)}, u32[]{:S(2)}, u32[]{:S(2)}) collective-permute-start(f32[16,256]{1,0:T(8,128)S(1)} %pad_maximum_fusion.1), channel_id=1, source_target_pairs={{0,192},{64,0},{128,64},{192,128},{1,193},{65,1},{129,65},{193,129... | collective-permute-start | bytes 49160 | tf_op jit(solution)/shard_map/ppermute | solution.py:23
  41.4 1.5 %collective-permute-done.19 = f32[16,256]{1,0:T(8,128)S(1)} collective-permute-done((f32[16,256]{1,0:T(8,128)S(1)}, f32[16,256]{1,0:T(8,128)S(1)}, u32[]{:S(2)}, u32[]{:S(2)}) %collective-permute-start.19) | collective-permute-done | bytes 16416 | tf_op jit(solution)/shard_map/ppermute | solution.py:23
  43.1 2.8 %collective-permute-done.17 = f32[16,256]{1,0:T(8,128)S(1)} collective-permute-done((f32[16,256]{1,0:T(8,128)S(1)}, f32[16,256]{1,0:T(8,128)S(1)}, u32[]{:S(2)}, u32[]{:S(2)}) %collective-permute-start.17) | collective-permute-done | bytes 16416 | tf_op jit(solution)/shard_map/ppermute | solution.py:23
  45.9 5.9 %collective-permute-start.21 = (f32[16,256]{1,0:T(8,128)S(1)}, f32[16,256]{1,0:T(8,128)S(1)}, u32[]{:S(2)}, u32[]{:S(2)}) collective-permute-start(f32[16,256]{1,0:T(8,128)S(1)} %pad_maximum_fusion.2), channel_id=1, source_target_pairs={{0,14},{2,0},{4,2},{6,4},{8,6},{10,8},{12,10},{14,12},{1,15},{3,1}... | collective-permute-start | bytes 49160 | tf_op jit(solution)/shard_map/ppermute | solution.py:23
  51.9 1.4 %collective-permute-done.21 = f32[16,256]{1,0:T(8,128)S(1)} collective-permute-done((f32[16,256]{1,0:T(8,128)S(1)}, f32[16,256]{1,0:T(8,128)S(1)}, u32[]{:S(2)}, u32[]{:S(2)}) %collective-permute-start.21) | collective-permute-done | bytes 16416 | tf_op jit(solution)/shard_map/ppermute | solution.py:23
  53.3 3.5 %collective-permute-done.20 = f32[16,256]{1,0:T(8,128)S(1)} collective-permute-done((f32[16,256]{1,0:T(8,128)S(1)}, f32[16,256]{1,0:T(8,128)S(1)}, u32[]{:S(2)}, u32[]{:S(2)}) %collective-permute-start.20) | collective-permute-done | bytes 16416 | tf_op jit(solution)/shard_map/ppermute | solution.py:23
  57.0 5.0 %collective-permute-start.23 = (f32[16,256]{1,0:T(8,128)S(1)}, f32[16,256]{1,0:T(8,128)S(1)}, u32[]{:S(2)}, u32[]{:S(2)}) collective-permute-start(f32[16,256]{1,0:T(8,128)S(1)} %pad_maximum_fusion.4), channel_id=1, source_target_pairs={{0,10},{2,12},{4,14},{6,0},{8,2},{10,4},{12,6},{14,8},{1,11},{3,13... | collective-permute-start | bytes 49160 | tf_op jit(solution)/shard_map/ppermute | solution.py:23
  62.0 1.7 %collective-permute-done.22 = f32[16,256]{1,0:T(8,128)S(1)} collective-permute-done((f32[16,256]{1,0:T(8,128)S(1)}, f32[16,256]{1,0:T(8,128)S(1)}, u32[]{:S(2)}, u32[]{:S(2)}) %collective-permute-start.22) | collective-permute-done | bytes 16416 | tf_op jit(solution)/shard_map/ppermute | solution.py:23
  63.7 1.8 %slope.1 = (bf16[640,256]{1,0:T(8,128)(2,1)S(1)}, bf16[128,2560]{1,0:T(8,128)(2,1)S(1)}, f32[128,2560]{1,0:T(8,128)S(1)}, f32[2]{0:T(128)}) custom-call(f32[640,128]{1,0:T(8,128)S(1)} %get-tuple-element.39.refs_0_, f32[640,128]{1,0:T(8,128)S(1)} %get-tuple-element.48.refs_1_, f32[640,128]{1,0:T(8,128)S(1)} %get-tuple-element.49.refs_2_, ...), custom_call_target="tpu_custom_call" | custom-call | flops 838860800 | bytes 8388608 | tf_op jit(solution)/shard_map/slope/pallas_call | solution.py:209
  65.7 2.1 %collective-permute-done.24.got_ref = bf16[128,2560]{1,0:T(8,128)(2,1)S(1)} collective-permute-done((bf16[128,2560]{1,0:T(8,128)(2,1)S(1)}, bf16[128,2560]{1,0:T(8,128)(2,1)S(1)}, u32[]{:S(2)}, u32[]{:S(2)}) %collective-permute-start.24) | collective-permute-done | bytes 655392 | tf_op jit(solution)/shard_map/ppermute | solution.py:18
  68.0 1.5 %collective-permute-start.26 = (bf16[32,2560]{1,0:T(8,128)(2,1)S(1)}, bf16[32,2560]{1,0:T(8,128)(2,1)S(1)}, u32[]{:S(2)}, u32[]{:S(2)}) collective-permute-start(bf16[32,2560]{1,0:T(8,128)(2,1)S(1)} %get-tuple-element.57), channel_id=1, source_target_pairs={{0,128},{64,192},{128,0},{192,64},{1,129},{65,193},{129,1},{193,65... | collective-permute-start | bytes 491528 | tf_op jit(solution)/shard_map/ppermute | solution.py:23
  69.4 1.8 %collective-permute-start.27 = (bf16[32,2560]{1,0:T(8,128)(2,1)S(1)}, bf16[32,2560]{1,0:T(8,128)(2,1)S(1)}, u32[]{:S(2)}, u32[]{:S(2)}) collective-permute-start(bf16[32,2560]{1,0:T(8,128)(2,1)S(1)} %get-tuple-element.58), channel_id=1, source_target_pairs={{0,192},{64,0},{128,64},{192,128},{1,193},{65,1},{129,65},{193,129... | collective-permute-start | bytes 491528 | tf_op jit(solution)/shard_map/ppermute | solution.py:23
  71.2 3.5 %weight.1 = (bf16[640,2560]{1,0:T(8,128)(2,1)}, f32[8,128]{1,0:T(8,128)S(1)}) custom-call(bf16[640,256]{1,0:T(8,128)(2,1)S(1)} %get-tuple-element.59.g_ref, bf16[128,2560]{1,0:T(8,128)(2,1)S(1)} %get-tuple-element.60.a_ref, bf16[128,2560]{1,0:T(8,128)(2,1)S(1)} %get-tuple-element.61.b_ref), custom_call_target="tpu_custom_call" | custom-call | flops 838860800 | bytes 6291456 | tf_op jit(solution)/shard_map/weight/pallas_call | solution.py:238
  74.7 4.2 %collective-permute-done.25.a_ref = bf16[32,2560]{1,0:T(8,128)(2,1)S(1)} collective-permute-done((bf16[32,2560]{1,0:T(8,128)(2,1)S(1)}, bf16[32,2560]{1,0:T(8,128)(2,1)S(1)}, u32[]{:S(2)}, u32[]{:S(2)}) %collective-permute-start.25) | collective-permute-done | bytes 163872 | tf_op jit(solution)/shard_map/ppermute | solution.py:23
  78.9 0.6 collective-permute-done.27.c_ref
  79.6 1.3 %collective-permute-start.28 = (bf16[16,2560]{1,0:T(8,128)(2,1)S(1)}, bf16[16,2560]{1,0:T(8,128)(2,1)S(1)}, u32[]{:S(2)}, u32[]{:S(2)}) collective-permute-start(bf16[16,2560]{1,0:T(8,128)(2,1)S(1)} %get-tuple-element.64), channel_id=1, source_target_pairs={{0,32},{32,0},{1,33},{33,1},{2,34},{34,2},{3,35},{35,3},{4,36},{36... | collective-permute-start | bytes 245768 | tf_op jit(solution)/shard_map/ppermute | solution.py:18
  80.9 3.3 %collective-permute-done.28.got_ref = bf16[16,2560]{1,0:T(8,128)(2,1)S(1)} collective-permute-done((bf16[16,2560]{1,0:T(8,128)(2,1)S(1)}, bf16[16,2560]{1,0:T(8,128)(2,1)S(1)}, u32[]{:S(2)}, u32[]{:S(2)}) %collective-permute-start.28) | collective-permute-done | bytes 81952 | tf_op jit(solution)/shard_map/ppermute | solution.py:18
  84.3 2.7 %collective-permute-start.29 = (f32[3,16,320]{2,1,0:T(8,128)S(1)}, f32[3,16,320]{2,1,0:T(8,128)S(1)}, u32[]{:S(2)}, u32[]{:S(2)}) collective-permute-start(f32[3,16,320]{2,1,0:T(8,128)S(1)} %get-tuple-element.66), channel_id=1, source_target_pairs={{0,6},{2,8},{4,10},{6,12},{8,14},{10,0},{12,2},{14,4},{1,7},{3,9},... | collective-permute-start | bytes 184328 | tf_op jit(solution)/shard_map/ppermute | solution.py:23
  87.0 2.5 %collective-permute-start.30 = (f32[2,16,320]{2,1,0:T(8,128)S(1)}, f32[2,16,320]{2,1,0:T(8,128)S(1)}, u32[]{:S(2)}, u32[]{:S(2)}) collective-permute-start(f32[2,16,320]{2,1,0:T(8,128)S(1)} %get-tuple-element.67), channel_id=1, source_target_pairs={{0,10},{2,12},{4,14},{6,0},{8,2},{10,4},{12,6},{14,8},{1,11},{3,13... | collective-permute-start | bytes 122888 | tf_op jit(solution)/shard_map/ppermute | solution.py:23
  89.5 3.4 %collective-permute-done.30 = f32[2,16,320]{2,1,0:T(8,128)S(1)} collective-permute-done((f32[2,16,320]{2,1,0:T(8,128)S(1)}, f32[2,16,320]{2,1,0:T(8,128)S(1)}, u32[]{:S(2)}, u32[]{:S(2)}) %collective-permute-start.30) | collective-permute-done | bytes 40992 | tf_op jit(solution)/shard_map/ppermute | solution.py:23
  92.9 1.3 %collective-permute-start.31 = (f32[16,320]{1,0:T(8,128)S(1)}, f32[16,320]{1,0:T(8,128)S(1)}, u32[]{:S(2)}, u32[]{:S(2)}) collective-permute-start(f32[16,320]{1,0:T(8,128)S(1)} %get-tuple-element.80), channel_id=1, source_target_pairs={{0,2},{2,4},{4,6},{6,8},{8,10},{10,12},{12,14},{14,0},{1,3},{3,5},... | collective-permute-start | bytes 61448 | tf_op jit(solution)/shard_map/ppermute | solution.py:23
  94.2 2.7 %collective-permute-start.32 = (f32[16,320]{1,0:T(8,128)S(1)}, f32[16,320]{1,0:T(8,128)S(1)}, u32[]{:S(2)}, u32[]{:S(2)}) collective-permute-start(f32[16,320]{1,0:T(8,128)S(1)} %get-tuple-element.81), channel_id=1, source_target_pairs={{0,14},{2,0},{4,2},{6,4},{8,6},{10,8},{12,10},{14,12},{1,15},{3,1}... | collective-permute-start | bytes 61448 | tf_op jit(solution)/shard_map/ppermute | solution.py:23
  96.9 1.7 %collective-permute-done.31 = f32[16,320]{1,0:T(8,128)S(1)} collective-permute-done((f32[16,320]{1,0:T(8,128)S(1)}, f32[16,320]{1,0:T(8,128)S(1)}, u32[]{:S(2)}, u32[]{:S(2)}) %collective-permute-start.31) | collective-permute-done | bytes 20512 | tf_op jit(solution)/shard_map/ppermute | solution.py:23
  98.6 1.8 %collective-permute-done.32 = f32[16,320]{1,0:T(8,128)S(1)} collective-permute-done((f32[16,320]{1,0:T(8,128)S(1)}, f32[16,320]{1,0:T(8,128)S(1)}, u32[]{:S(2)}, u32[]{:S(2)}) %collective-permute-start.32) | collective-permute-done | bytes 20512 | tf_op jit(solution)/shard_map/ppermute | solution.py:23
  100.4 0.6 fusion.6
  (54 shorter events, 3.9 us)
Async XLA Ops:
  0.6 0.9 copy-start.4
  1.5 0.9 copy-start.5
  2.4 0.7 copy-start.6
  3.5 8.3 %collective-permute-start.2 = (bf16[16,6656]{1,0:T(8,128)(2,1)S(1)}, bf16[16,6656]{1,0:T(8,128)(2,1)S(1)}, u32[]{:S(2)}, u32[]{:S(2)}) collective-permute-start(bf16[16,6656]{1,0:T(8,128)(2,1)S(1)} %get-tuple-element.40.refs_0_), channel_id=1, source_target_pairs={{0,64},{64,128},{128,192},{192,0},{1,65},{65,129},{129,193},{193,1... | collective-permute-start | bytes 638984 | tf_op jit(solution)/shard_map/ppermute | solution.py:23
  5.1 6.7 %collective-permute-start.1 = (bf16[16,6656]{1,0:T(8,128)(2,1)S(1)}, bf16[16,6656]{1,0:T(8,128)(2,1)S(1)}, u32[]{:S(2)}, u32[]{:S(2)}) collective-permute-start(bf16[16,6656]{1,0:T(8,128)(2,1)S(1)} %get-tuple-element.40.refs_0_), channel_id=1, source_target_pairs={{0,192},{64,0},{128,64},{192,128},{1,193},{65,1},{129,65},{193,129... | collective-permute-start | bytes 638984 | tf_op jit(solution)/shard_map/ppermute | solution.py:23
  6.8 6.6 %collective-permute-start = (bf16[16,6656]{1,0:T(8,128)(2,1)S(1)}, bf16[16,6656]{1,0:T(8,128)(2,1)S(1)}, u32[]{:S(2)}, u32[]{:S(2)}) collective-permute-start(bf16[16,6656]{1,0:T(8,128)(2,1)S(1)} %get-tuple-element.40.refs_0_), channel_id=1, source_target_pairs={{0,32},{32,0},{1,33},{33,1},{2,34},{34,2},{3,35},{35,3},{4,36},{36... | collective-permute-start | bytes 638984 | tf_op jit(solution)/shard_map/ppermute | solution.py:18
  8.0 7.3 %collective-permute-start.3 = (bf16[16,6656]{1,0:T(8,128)(2,1)S(1)}, bf16[16,6656]{1,0:T(8,128)(2,1)S(1)}, u32[]{:S(2)}, u32[]{:S(2)}) collective-permute-start(bf16[16,6656]{1,0:T(8,128)(2,1)S(1)} %get-tuple-element.40.refs_0_), channel_id=1, source_target_pairs={{0,16},{16,0},{1,17},{17,1},{2,18},{18,2},{3,19},{19,3},{4,20},{20... | collective-permute-start | bytes 638984 | tf_op jit(solution)/shard_map/ppermute | solution.py:18
  11.8 4.6 %collective-permute-start.6 = (bf16[16,6656]{1,0:T(8,128)(2,1)S(1)}, bf16[16,6656]{1,0:T(8,128)(2,1)S(1)}, u32[]{:S(2)}, u32[]{:S(2)}) collective-permute-start(bf16[16,6656]{1,0:T(8,128)(2,1)S(1)} %collective-permute-done.2.refs_3_), channel_id=1, source_target_pairs={{0,16},{16,0},{1,17},{17,1},{2,18},{18,2},{3,19},{19,3},{4,20},{20... | collective-permute-start | bytes 638984 | tf_op jit(solution)/shard_map/ppermute | solution.py:18
  11.8 5.5 %collective-permute-start.5 = (bf16[16,6656]{1,0:T(8,128)(2,1)S(1)}, bf16[16,6656]{1,0:T(8,128)(2,1)S(1)}, u32[]{:S(2)}, u32[]{:S(2)}) collective-permute-start(bf16[16,6656]{1,0:T(8,128)(2,1)S(1)} %collective-permute-done.1.refs_2_), channel_id=1, source_target_pairs={{0,16},{16,0},{1,17},{17,1},{2,18},{18,2},{3,19},{19,3},{4,20},{20... | collective-permute-start | bytes 638984 | tf_op jit(solution)/shard_map/ppermute | solution.py:18
  13.4 5.6 %collective-permute-start.4 = (bf16[16,6656]{1,0:T(8,128)(2,1)S(1)}, bf16[16,6656]{1,0:T(8,128)(2,1)S(1)}, u32[]{:S(2)}, u32[]{:S(2)}) collective-permute-start(bf16[16,6656]{1,0:T(8,128)(2,1)S(1)} %collective-permute-done.refs_1_), channel_id=1, source_target_pairs={{0,16},{16,0},{1,17},{17,1},{2,18},{18,2},{3,19},{19,3},{4,20},{20... | collective-permute-start | bytes 638984 | tf_op jit(solution)/shard_map/ppermute | solution.py:18
  13.4 13.8 %collective-permute-start.7 = (bf16[16,6656]{1,0:T(8,128)(2,1)S(1)}, bf16[16,6656]{1,0:T(8,128)(2,1)S(1)}, u32[]{:S(2)}, u32[]{:S(2)}) collective-permute-start(bf16[16,6656]{1,0:T(8,128)(2,1)S(1)} %get-tuple-element.40.refs_0_), channel_id=1, source_target_pairs={{0,128},{64,192},{128,0},{192,64},{1,129},{65,193},{129,1},{193,65... | collective-permute-start | bytes 638984 | tf_op jit(solution)/shard_map/ppermute | solution.py:23
  15.3 10.7 %collective-permute-start.10 = (bf16[16,6656]{1,0:T(8,128)(2,1)S(1)}, bf16[16,6656]{1,0:T(8,128)(2,1)S(1)}, u32[]{:S(2)}, u32[]{:S(2)}) collective-permute-start(bf16[16,6656]{1,0:T(8,128)(2,1)S(1)} %collective-permute-done.2.refs_3_), channel_id=1, source_target_pairs={{0,32},{32,0},{1,33},{33,1},{2,34},{34,2},{3,35},{35,3},{4,36},{36... | collective-permute-start | bytes 638984 | tf_op jit(solution)/shard_map/ppermute | solution.py:18
  16.5 10.7 %collective-permute-start.9 = (bf16[16,6656]{1,0:T(8,128)(2,1)S(1)}, bf16[16,6656]{1,0:T(8,128)(2,1)S(1)}, u32[]{:S(2)}, u32[]{:S(2)}) collective-permute-start(bf16[16,6656]{1,0:T(8,128)(2,1)S(1)} %collective-permute-done.1.refs_2_), channel_id=1, source_target_pairs={{0,32},{32,0},{1,33},{33,1},{2,34},{34,2},{3,35},{35,3},{4,36},{36... | collective-permute-start | bytes 638984 | tf_op jit(solution)/shard_map/ppermute | solution.py:18
  17.3 9.9 %collective-permute-start.8 = (bf16[16,6656]{1,0:T(8,128)(2,1)S(1)}, bf16[16,6656]{1,0:T(8,128)(2,1)S(1)}, u32[]{:S(2)}, u32[]{:S(2)}) collective-permute-start(bf16[16,6656]{1,0:T(8,128)(2,1)S(1)} %collective-permute-done.refs_1_), channel_id=1, source_target_pairs={{0,128},{64,192},{128,0},{192,64},{1,129},{65,193},{129,1},{193,65... | collective-permute-start | bytes 638984 | tf_op jit(solution)/shard_map/ppermute | solution.py:23
  18.9 1.9 %copy-start = (bf16[640,2560]{1,0:T(8,128)(2,1)S(1)}, bf16[640,2560]{1,0:T(8,128)(2,1)}, u32[]{:S(2)}) copy-start(bf16[640,2560]{1,0:T(8,128)(2,1)} %refs_7_.1) | copy-start | bytes 9830404
  20.9 2.5 %copy-start.2 = (bf16[640,4096]{1,0:T(8,128)(2,1)S(1)}, bf16[640,4096]{1,0:T(8,128)(2,1)}, u32[]{:S(2)}) copy-start(bf16[640,4096]{1,0:T(8,128)(2,1)} %refs_9_.3) | copy-start | bytes 15728644
  23.4 6.2 %copy-start.1 = (bf16[640,2560]{1,0:T(8,128)(2,1)S(1)}, bf16[640,2560]{1,0:T(8,128)(2,1)}, u32[]{:S(2)}) copy-start(bf16[640,2560]{1,0:T(8,128)(2,1)} %refs_7_.1) | copy-start | bytes 9830404
  23.4 6.2 %copy-start.3 = (bf16[640,4096]{1,0:T(8,128)(2,1)S(1)}, bf16[640,4096]{1,0:T(8,128)(2,1)}, u32[]{:S(2)}) copy-start(bf16[640,4096]{1,0:T(8,128)(2,1)} %refs_9_.3) | copy-start | bytes 15728644
  27.2 1.5 %collective-permute-start.11 = (bf16[16,6656]{1,0:T(8,128)(2,1)S(1)}, bf16[16,6656]{1,0:T(8,128)(2,1)S(1)}, u32[]{:S(2)}, u32[]{:S(2)}) collective-permute-start(bf16[16,6656]{1,0:T(8,128)(2,1)S(1)} %collective-permute-done.7.refs_0_), channel_id=1, source_target_pairs={{0,16},{16,0},{1,17},{17,1},{2,18},{18,2},{3,19},{19,3},{4,20},{20... | collective-permute-start | bytes 638984 | tf_op jit(solution)/shard_map/ppermute | solution.py:18
  27.2 1.8 %collective-permute-start.12 = (bf16[16,6656]{1,0:T(8,128)(2,1)S(1)}, bf16[16,6656]{1,0:T(8,128)(2,1)S(1)}, u32[]{:S(2)}, u32[]{:S(2)}) collective-permute-start(bf16[16,6656]{1,0:T(8,128)(2,1)S(1)} %collective-permute-done.8.refs_1_), channel_id=1, source_target_pairs={{0,16},{16,0},{1,17},{17,1},{2,18},{18,2},{3,19},{19,3},{4,20},{20... | collective-permute-start | bytes 638984 | tf_op jit(solution)/shard_map/ppermute | solution.py:18
  27.7 1.6 %collective-permute-start.13 = (bf16[16,6656]{1,0:T(8,128)(2,1)S(1)}, bf16[16,6656]{1,0:T(8,128)(2,1)S(1)}, u32[]{:S(2)}, u32[]{:S(2)}) collective-permute-start(bf16[16,6656]{1,0:T(8,128)(2,1)S(1)} %collective-permute-done.9.refs_2_), channel_id=1, source_target_pairs={{0,16},{16,0},{1,17},{17,1},{2,18},{18,2},{3,19},{19,3},{4,20},{20... | collective-permute-start | bytes 638984 | tf_op jit(solution)/shard_map/ppermute | solution.py:18
  27.8 1.8 %collective-permute-start.14 = (bf16[16,6656]{1,0:T(8,128)(2,1)S(1)}, bf16[16,6656]{1,0:T(8,128)(2,1)S(1)}, u32[]{:S(2)}, u32[]{:S(2)}) collective-permute-start(bf16[16,6656]{1,0:T(8,128)(2,1)S(1)} %collective-permute-done.10.refs_3_), channel_id=1, source_target_pairs={{0,16},{16,0},{1,17},{17,1},{2,18},{18,2},{3,19},{19,3},{4,20},{20... | collective-permute-start | bytes 638984 | tf_op jit(solution)/shard_map/ppermute | solution.py:18
  32.4 1.2 %collective-permute-start.15 = (f32[16,256]{1,0:T(8,128)S(1)}, f32[16,256]{1,0:T(8,128)S(1)}, u32[]{:S(2)}, u32[]{:S(2)}) collective-permute-start(f32[16,256]{1,0:T(8,128)S(1)} %get-tuple-element.51), channel_id=1, source_target_pairs={{0,16},{16,0},{1,17},{17,1},{2,18},{18,2},{3,19},{19,3},{4,20},{20... | collective-permute-start | bytes 49160 | tf_op jit(solution)/shard_map/ppermute | solution.py:18
  33.7 3.8 %collective-permute-start.16 = (f32[16,256]{1,0:T(8,128)S(1)}, f32[16,256]{1,0:T(8,128)S(1)}, u32[]{:S(2)}, u32[]{:S(2)}) collective-permute-start(f32[16,256]{1,0:T(8,128)S(1)} %pad_maximum_fusion), channel_id=1, source_target_pairs={{0,32},{32,0},{1,33},{33,1},{2,34},{34,2},{3,35},{35,3},{4,36},{36... | collective-permute-start | bytes 49160 | tf_op jit(solution)/shard_map/ppermute | solution.py:18
  37.5 5.3 %collective-permute-start.19 = (f32[16,256]{1,0:T(8,128)S(1)}, f32[16,256]{1,0:T(8,128)S(1)}, u32[]{:S(2)}, u32[]{:S(2)}) collective-permute-start(f32[16,256]{1,0:T(8,128)S(1)} %pad_maximum_fusion.1), channel_id=1, source_target_pairs={{0,128},{64,192},{128,0},{192,64},{1,129},{65,193},{129,1},{193,65... | collective-permute-start | bytes 49160 | tf_op jit(solution)/shard_map/ppermute | solution.py:23
  39.4 3.7 %collective-permute-start.18 = (f32[16,256]{1,0:T(8,128)S(1)}, f32[16,256]{1,0:T(8,128)S(1)}, u32[]{:S(2)}, u32[]{:S(2)}) collective-permute-start(f32[16,256]{1,0:T(8,128)S(1)} %pad_maximum_fusion.1), channel_id=1, source_target_pairs={{0,192},{64,0},{128,64},{192,128},{1,193},{65,1},{129,65},{193,129... | collective-permute-start | bytes 49160 | tf_op jit(solution)/shard_map/ppermute | solution.py:23
  40.9 4.9 %collective-permute-start.17 = (f32[16,256]{1,0:T(8,128)S(1)}, f32[16,256]{1,0:T(8,128)S(1)}, u32[]{:S(2)}, u32[]{:S(2)}) collective-permute-start(f32[16,256]{1,0:T(8,128)S(1)} %pad_maximum_fusion.1), channel_id=1, source_target_pairs={{0,64},{64,128},{128,192},{192,0},{1,65},{65,129},{129,193},{193,1... | collective-permute-start | bytes 49160 | tf_op jit(solution)/shard_map/ppermute | solution.py:23
  45.9 7.4 %collective-permute-start.21 = (f32[16,256]{1,0:T(8,128)S(1)}, f32[16,256]{1,0:T(8,128)S(1)}, u32[]{:S(2)}, u32[]{:S(2)}) collective-permute-start(f32[16,256]{1,0:T(8,128)S(1)} %pad_maximum_fusion.2), channel_id=1, source_target_pairs={{0,14},{2,0},{4,2},{6,4},{8,6},{10,8},{12,10},{14,12},{1,15},{3,1}... | collective-permute-start | bytes 49160 | tf_op jit(solution)/shard_map/ppermute | solution.py:23
  51.9 4.9 %collective-permute-start.20 = (f32[16,256]{1,0:T(8,128)S(1)}, f32[16,256]{1,0:T(8,128)S(1)}, u32[]{:S(2)}, u32[]{:S(2)}) collective-permute-start(f32[16,256]{1,0:T(8,128)S(1)} %pad_maximum_fusion.2), channel_id=1, source_target_pairs={{0,2},{2,4},{4,6},{6,8},{8,10},{10,12},{12,14},{14,0},{1,3},{3,5},... | collective-permute-start | bytes 49160 | tf_op jit(solution)/shard_map/ppermute | solution.py:23
  56.9 6.8 %collective-permute-start.22 = (f32[16,256]{1,0:T(8,128)S(1)}, f32[16,256]{1,0:T(8,128)S(1)}, u32[]{:S(2)}, u32[]{:S(2)}) collective-permute-start(f32[16,256]{1,0:T(8,128)S(1)} %pad_maximum_fusion.3), channel_id=1, source_target_pairs={{0,6},{2,8},{4,10},{6,12},{8,14},{10,0},{12,2},{14,4},{1,7},{3,9},... | collective-permute-start | bytes 49160 | tf_op jit(solution)/shard_map/ppermute | solution.py:23
  57.0 6.7 %collective-permute-start.23 = (f32[16,256]{1,0:T(8,128)S(1)}, f32[16,256]{1,0:T(8,128)S(1)}, u32[]{:S(2)}, u32[]{:S(2)}) collective-permute-start(f32[16,256]{1,0:T(8,128)S(1)} %pad_maximum_fusion.4), channel_id=1, source_target_pairs={{0,10},{2,12},{4,14},{6,0},{8,2},{10,4},{12,6},{14,8},{1,11},{3,13... | collective-permute-start | bytes 49160 | tf_op jit(solution)/shard_map/ppermute | solution.py:23
  65.6 2.2 %collective-permute-start.24 = (bf16[128,2560]{1,0:T(8,128)(2,1)S(1)}, bf16[128,2560]{1,0:T(8,128)(2,1)S(1)}, u32[]{:S(2)}, u32[]{:S(2)}) collective-permute-start(bf16[128,2560]{1,0:T(8,128)(2,1)S(1)} %get-tuple-element.54), channel_id=1, source_target_pairs={{0,16},{16,0},{1,17},{17,1},{2,18},{18,2},{3,19},{19,3},{4,20},{20... | collective-permute-start | bytes 1966088 | tf_op jit(solution)/shard_map/ppermute | solution.py:18
  67.9 11.0 %collective-permute-start.25 = (bf16[32,2560]{1,0:T(8,128)(2,1)S(1)}, bf16[32,2560]{1,0:T(8,128)(2,1)S(1)}, u32[]{:S(2)}, u32[]{:S(2)}) collective-permute-start(bf16[32,2560]{1,0:T(8,128)(2,1)S(1)} %get-tuple-element.56), channel_id=1, source_target_pairs={{0,64},{64,128},{128,192},{192,0},{1,65},{65,129},{129,193},{193,1... | collective-permute-start | bytes 491528 | tf_op jit(solution)/shard_map/ppermute | solution.py:23
  68.0 11.0 %collective-permute-start.26 = (bf16[32,2560]{1,0:T(8,128)(2,1)S(1)}, bf16[32,2560]{1,0:T(8,128)(2,1)S(1)}, u32[]{:S(2)}, u32[]{:S(2)}) collective-permute-start(bf16[32,2560]{1,0:T(8,128)(2,1)S(1)} %get-tuple-element.57), channel_id=1, source_target_pairs={{0,128},{64,192},{128,0},{192,64},{1,129},{65,193},{129,1},{193,65... | collective-permute-start | bytes 491528 | tf_op jit(solution)/shard_map/ppermute | solution.py:23
  69.4 10.1 %collective-permute-start.27 = (bf16[32,2560]{1,0:T(8,128)(2,1)S(1)}, bf16[32,2560]{1,0:T(8,128)(2,1)S(1)}, u32[]{:S(2)}, u32[]{:S(2)}) collective-permute-start(bf16[32,2560]{1,0:T(8,128)(2,1)S(1)} %get-tuple-element.58), channel_id=1, source_target_pairs={{0,192},{64,0},{128,64},{192,128},{1,193},{65,1},{129,65},{193,129... | collective-permute-start | bytes 491528 | tf_op jit(solution)/shard_map/ppermute | solution.py:23
  79.6 4.5 %collective-permute-start.28 = (bf16[16,2560]{1,0:T(8,128)(2,1)S(1)}, bf16[16,2560]{1,0:T(8,128)(2,1)S(1)}, u32[]{:S(2)}, u32[]{:S(2)}) collective-permute-start(bf16[16,2560]{1,0:T(8,128)(2,1)S(1)} %get-tuple-element.64), channel_id=1, source_target_pairs={{0,32},{32,0},{1,33},{33,1},{2,34},{34,2},{3,35},{35,3},{4,36},{36... | collective-permute-start | bytes 245768 | tf_op jit(solution)/shard_map/ppermute | solution.py:18
  84.3 8.6 %collective-permute-start.29 = (f32[3,16,320]{2,1,0:T(8,128)S(1)}, f32[3,16,320]{2,1,0:T(8,128)S(1)}, u32[]{:S(2)}, u32[]{:S(2)}) collective-permute-start(f32[3,16,320]{2,1,0:T(8,128)S(1)} %get-tuple-element.66), channel_id=1, source_target_pairs={{0,6},{2,8},{4,10},{6,12},{8,14},{10,0},{12,2},{14,4},{1,7},{3,9},... | collective-permute-start | bytes 184328 | tf_op jit(solution)/shard_map/ppermute | solution.py:23
  87.0 5.9 %collective-permute-start.30 = (f32[2,16,320]{2,1,0:T(8,128)S(1)}, f32[2,16,320]{2,1,0:T(8,128)S(1)}, u32[]{:S(2)}, u32[]{:S(2)}) collective-permute-start(f32[2,16,320]{2,1,0:T(8,128)S(1)} %get-tuple-element.67), channel_id=1, source_target_pairs={{0,10},{2,12},{4,14},{6,0},{8,2},{10,4},{12,6},{14,8},{1,11},{3,13... | collective-permute-start | bytes 122888 | tf_op jit(solution)/shard_map/ppermute | solution.py:23
  92.9 5.7 %collective-permute-start.31 = (f32[16,320]{1,0:T(8,128)S(1)}, f32[16,320]{1,0:T(8,128)S(1)}, u32[]{:S(2)}, u32[]{:S(2)}) collective-permute-start(f32[16,320]{1,0:T(8,128)S(1)} %get-tuple-element.80), channel_id=1, source_target_pairs={{0,2},{2,4},{4,6},{6,8},{8,10},{10,12},{12,14},{14,0},{1,3},{3,5},... | collective-permute-start | bytes 61448 | tf_op jit(solution)/shard_map/ppermute | solution.py:23
  94.2 6.2 %collective-permute-start.32 = (f32[16,320]{1,0:T(8,128)S(1)}, f32[16,320]{1,0:T(8,128)S(1)}, u32[]{:S(2)}, u32[]{:S(2)}) collective-permute-start(f32[16,320]{1,0:T(8,128)S(1)} %get-tuple-element.81), channel_id=1, source_target_pairs={{0,14},{2,0},{4,2},{6,4},{8,6},{10,8},{12,10},{14,12},{1,15},{3,1}... | collective-permute-start | bytes 61448 | tf_op jit(solution)/shard_map/ppermute | solution.py:23

commit v3 on v2

--- a/solution.py
+++ b/solution.py
@@ -1,3 +1,5 @@
+import functools
+
 import jax
 import jax.numpy as jnp
 import numpy as np
@@ -9,6 +11,7 @@
 RING_Y, PAIR_X, CORES, RING_Z = 4, 2, 2, 8
 SIZES = {"y": RING_Y, "x": PAIR_X, "c": CORES, "z": RING_Z}
 MB = 1 << 20
+JOIN_MB = 4
 bf16, f32 = jnp.bfloat16, jnp.float32
 VMEM = pl.BlockSpec(memory_space=pltpu.VMEM)
 SMEM = pl.BlockSpec(memory_space=pltpu.SMEM)
@@ -23,21 +26,17 @@
     return lax.ppermute(value, axis, [(i, (i + step) % size) for i in range(size)])
 
 
-EARLY = ((0, 0), (0, 1), (1, 0), (3, 0))
-LATE = ((2, 0), (2, 1), (1, 1), (3, 1))
+EARLY = ((0, 0), (0, 1), (3, 0), (1, 0))
+LATE = ((3, 1), (1, 1), (2, 0), (2, 1))
 
 
 def gather_rows(block):
     across = swap(block, "x")
     prev = shift(block, "y", 1)
     next_ = shift(block, "y", 3)
-    prev_across = swap(prev, "x")
-    next_across = swap(next_, "x")
-    held, across = lax.optimization_barrier((block, across))
-    far = shift(held, "y", 2)
-    far_across = shift(across, "y", 2)
-    early = [block, across, next_, prev]
-    return early + [swap(piece, "c") for piece in early], (far, far_across, next_across, prev_across)
+    sides, here = pair(prev, next_), pair(block, across)
+    early = here, swap(here, "c"), sides, swap(sides, "c")
+    return early, (swap(sides, "x"), shift(here, "y", 2))
 
 
 def first_entry(vocab):
@@ -56,21 +55,50 @@
     return out
 
 
-def join_kernel(a_ref, b_ref, tgt_ref, out_ref, row_ref, pick_ref, sems):
+def join_kernel(a_ref, b_ref, out_ref):
     width = a_ref.shape[1]
-    copies = [
-        pltpu.make_async_copy(a_ref, out_ref.at[:, :width], sems.at[0]),
-        pltpu.make_async_copy(b_ref, out_ref.at[:, width:], sems.at[1]),
-    ]
-    for copy in copies:
-        copy.start()
+    out_ref[:, :width] = a_ref[...]
+    out_ref[:, width:] = b_ref[...]
+
+
+def join(student, teacher):
+    rows = student.shape[0]
+    return pl.pallas_call(
+        join_kernel,
+        out_shape=jax.ShapeDtypeStruct((rows, student.shape[1] + teacher.shape[1]), bf16),
+        in_specs=[VMEM] * 2,
+        out_specs=VMEM,
+        compiler_params=pltpu.CompilerParams(vmem_limit_bytes=JOIN_MB * MB),
+        name="join",
+    )(student, teacher)
+
+
+def pair_kernel(a_ref, b_ref, out_ref):
+    rows = a_ref.shape[0]
+    out_ref[:rows] = a_ref[...]
+    out_ref[rows:] = b_ref[...]
+
+
+def pair(a, b):
+    return pl.pallas_call(
+        pair_kernel,
+        out_shape=jax.ShapeDtypeStruct((2 * a.shape[0], a.shape[1]), bf16),
+        in_specs=[VMEM] * 2,
+        out_specs=VMEM,
+        compiler_params=pltpu.CompilerParams(vmem_limit_bytes=2 * MB),
+        name="pair",
+    )(a, b)
+
+
+def rows_kernel(tgt_ref, row_ref, pick_ref):
     to = lax.broadcasted_iota(jnp.int32, (1, 256), 1)
-    place = lax.rem(to // 16, 4) + to // 128 * 4
+    place = to // 128 * 4 + lax.rem(to // 64, 2) * 2 + lax.rem(to // 16, 2)
+    dc = lax.rem(to // 32, CORES)
     dy, dx = jnp.zeros_like(to), jnp.zeros_like(to)
     for i, (v, w) in enumerate(EARLY + LATE):
         dy = jnp.where(place == i, v, dy)
         dx = jnp.where(place == i, w, dx)
-    at_c = lax.rem(lax.rem(to // 64, CORES) + lax.axis_index("c"), CORES)
+    at_c = lax.rem(dc + lax.axis_index("c"), CORES)
     at_y = lax.rem(dy + lax.axis_index("y"), RING_Y)
     at_x = lax.rem(dx + lax.axis_index("x"), PAIR_X)
     section = (at_y * PAIR_X + at_x) * CORES + at_c
@@ -81,34 +109,25 @@
     tgt = jnp.concatenate([tgt_ref[0:1], tgt_ref[1:2]], 1).astype(f32)
     tgt = jnp.concatenate([tgt, jnp.zeros((7, 256), f32)], 0)
     row_ref[...] = permuted(tgt, pick, False)[0:1].astype(jnp.int32)
-    for copy in copies:
-        copy.wait()
-
-
-def join(student, teacher, targets):
-    rows = student.shape[0]
-    width = student.shape[1] + teacher.shape[1]
-    shape = jax.ShapeDtypeStruct
-    return pl.pallas_call(
-        join_kernel,
-        out_shape=(
-            shape((rows, width), bf16),
-            shape((1, 256), jnp.int32),
-            shape((256, 256), bf16),
-        ),
-        in_specs=[pl.BlockSpec(memory_space=pl.ANY)] * 2 + [VMEM],
-        out_specs=(VMEM,) * 3,
-        scratch_shapes=[pltpu.SemaphoreType.DMA((2,))],
-        compiler_params=pltpu.CompilerParams(vmem_limit_bytes=4 * MB),
-        name="join",
-    )(student, teacher, targets)
+
+
+def row_order(targets):
+    shape = jax.ShapeDtypeStruct
+    return pl.pallas_call(
+        rows_kernel,
+        out_shape=(shape((1, 256), jnp.int32), shape((256, 256), bf16)),
+        in_specs=[VMEM],
+        out_specs=(VMEM,) * 2,
+        compiler_params=pltpu.CompilerParams(vmem_limit_bytes=2 * MB),
+        name="row_order",
+    )(targets)
 
 
 def half_logits(blocks, ws_ref, wt_ref, tgt, s_ref, t_ref, hs_ref, ht_ref):
     width = ws_ref.shape[1]
     for i, ref in enumerate(blocks):
-        hs_ref[i * 16 : i * 16 + 16, :] = ref[:, :width]
-        ht_ref[i * 16 : i * 16 + 16, :] = ref[:, width:]
+        hs_ref[i * 32 : i * 32 + 32, :] = ref[:, :width]
+        ht_ref[i * 32 : i * 32 + 32, :] = ref[:, width:]
     dims = (((1,), (1,)), ((), ()))
     s = lax.dot_general(ws_ref[...], hs_ref[...], dims, preferred_element_type=f32)
     s_ref[...] = s
@@ -130,17 +149,17 @@
 
 
 def early_kernel(*refs):
-    ws_ref, wt_ref, tgt_ref = refs[8:11]
-    s_ref, t_ref, hs_ref, part_ref, ht_ref = refs[11:]
+    ws_ref, wt_ref, tgt_ref = refs[4:7]
+    s_ref, t_ref, hs_ref, part_ref, ht_ref = refs[7:]
     tgt = tgt_ref[:, :128]
-    part_ref[...] = half_logits(refs[:8], ws_ref, wt_ref, tgt, s_ref, t_ref, hs_ref, ht_ref)
+    part_ref[...] = half_logits(refs[:4], ws_ref, wt_ref, tgt, s_ref, t_ref, hs_ref, ht_ref)
 
 
 def late_kernel(*refs):
-    ws_ref, wt_ref, tgt_ref, early_ref, pick_ref = refs[8:13]
-    s_ref, t_ref, hs_ref, part_ref, ht_ref = refs[13:]
+    ws_ref, wt_ref, tgt_ref, early_ref, pick_ref = refs[4:9]
+    s_ref, t_ref, hs_ref, part_ref, ht_ref = refs[9:]
     tgt = tgt_ref[:, 128:]
-    part = half_logits(refs[:8], ws_ref, wt_ref, tgt, s_ref, t_ref, hs_ref, ht_ref)
+    part = half_logits(refs[:4], ws_ref, wt_ref, tgt, s_ref, t_ref, hs_ref, ht_ref)
     part = jnp.concatenate([early_ref[...], part], 1)
     part_ref[...] = permuted(part, pick_ref[...], True)
 
@@ -157,7 +176,7 @@
             shape((rows, width), bf16),
             shape((16, 2 * rows if extra else rows), f32),
         ),
-        in_specs=[VMEM] * (11 + len(extra)),
+        in_specs=[VMEM] * (7 + len(extra)),
         out_specs=(VMEM,) * 4,
         scratch_shapes=[pltpu.VMEM((rows, wt.shape[1]), bf16)],
         compiler_params=pltpu.CompilerParams(vmem_limit_bytes=20 * MB),
@@ -172,8 +191,8 @@
 
 def slope_kernel(*refs):
     s_refs, t_refs = refs[:2], refs[2:4]
-    part_ref, pick_ref, tgt_ref, ws_ref, g_ref, send_ref, keep_ref, loss_ref = refs[4:]
-    part = permuted(part_ref[...], pick_ref[...], False)
+    pick_ref, tgt_ref, ws_ref, g_ref, send_ref, keep_ref, loss_ref = refs[7:]
+    part = permuted(merge([ref[...] for ref in refs[4:7]]), pick_ref[...], False)
     first = first_entry(ws_ref.shape[0])
     ms, half_mt = part[0:1], part[2:3]
     z1, z2, zt, cross, picked = (part[8 + i : 9 + i] for i in range(5))
@@ -197,12 +216,12 @@
     )
     for i, (dy, dx) in enumerate(EARLY + LATE):
         out = slice((dy * PAIR_X + dx) * 16, (dy * PAIR_X + dx) * 16 + 16)
-        row = i // 4 * 128 + i % 4 * 16
+        row = i // 2 * 64 + i % 2 * 16
         keep_ref[out] = p[row : row + 16]
-        send_ref[out] = p[row + 64 : row + 80].astype(bf16)
-
-
-def compute_slope(s, t, part, pick, tgt, ws):
+        send_ref[out] = p[row + 32 : row + 48].astype(bf16)
+
+
+def compute_slope(s, t, parts, pick, tgt, ws):
     vocab, width = ws.shape
     rows = 256
     shape = jax.ShapeDtypeStruct
@@ -214,14 +233,14 @@
             shape((rows // 2, width), f32),
             shape((2,), f32),
         ),
-        in_specs=[VMEM] * 8,
+        in_specs=[VMEM] * 10,
         out_specs=(VMEM,) * 3 + (SMEM,),
         compiler_params=pltpu.CompilerParams(vmem_limit_bytes=20 * MB),
         cost_estimate=pl.CostEstimate(
             flops=2 * vocab * rows * width, bytes_accessed=8 * MB, transcendentals=3 * vocab * rows
         ),
         name="slope",
-    )(*s, *t, part, pick, tgt, ws)
+    )(*s, *t, *parts, pick, tgt, ws)
 
 
 def weight_kernel(g_ref, a_ref, b_ref, out_ref, done_ref):
@@ -265,7 +284,7 @@
     at = lambda d: tmp_ref[lax.rem(z + (d + RING_Z), RING_Z)]
     for i, d in enumerate((2, 3, 4)):
         ahead_ref[i] = at(d)
-    for i, d in enumerate((-3, -2)):
+    for i, d in enumerate((-2, -3)):
         behind_ref[i] = at(d)
     for i, d in enumerate((-1, 0, 1)):
         keep_ref[i] = at(d)
@@ -296,13 +315,30 @@
     return jnp.concatenate([top, total], 0)
 
 
+def merge_kernel(*refs, sizes):
+    for size, ref in zip(sizes, refs[-len(sizes) :]):
+        ref[...] = merge([v[...] for v in refs[:size]])
+
+
+def merged(parts, sizes):
+    shape = jax.ShapeDtypeStruct(parts[0].shape, f32)
+    return pl.pallas_call(
+        functools.partial(merge_kernel, sizes=sizes),
+        out_shape=(shape,) * len(sizes),
+        in_specs=[VMEM] * len(parts),
+        out_specs=(VMEM,) * len(sizes),
+        compiler_params=pltpu.CompilerParams(vmem_limit_bytes=2 * MB),
+        name="merge",
+    )(*parts)
+
+
 def exchange_totals(part):
-    part = merge([part, swap(part, "c")])
-    part = merge([part, swap(part, "x")])
-    part = merge([part, shift(part, "y", 1), shift(part, "y", 3), shift(part, "y", 2)])
-    prev, next_ = shift(part, "z", 1), shift(part, "z", 7)
-    two, three = merge([part, prev]), merge([part, prev, next_])
-    return merge([three, shift(three, "z", 3), shift(two, "z", 5)])
+    (part,) = merged([part, swap(part, "c")], (2,))
+    (part,) = merged([part, swap(part, "x")], (2,))
+    parts = [part, shift(part, "y", 1), shift(part, "y", 3), shift(part, "y", 2)]
+    (part,) = merged(parts, (4,))
+    two, three = merged([part, shift(part, "z", 1), shift(part, "z", 7)], (2, 3))
+    return three, shift(three, "z", 5), shift(two, "z", 2)
 
 
 def core_kernel(keep_ref, got_ref, own_ref, *out_refs):
@@ -355,9 +391,9 @@
     moved = [shift(part, "y", d + 1) for d, part in enumerate(parts)]
     own, part = add_ring(own, moved, after)
     ahead, behind, mine = split_features(own, swap(part, "x"))
-    from_a, from_b = shift(ahead, "z", 3), shift(behind, "z", 5)
-    to_next = mine[2] + from_a[2] + from_b[1]
-    to_prev = mine[0] + from_a[0]
+    from_a, from_b = shift(ahead, "z", 3), shift(behind, "z", 6)
+    to_next = mine[2] + from_a[2]
+    to_prev = mine[0] + from_a[0] + from_b[1]
     own = mine[1] + from_a[1] + from_b[0]
     return own + shift(to_next, "z", 1) + shift(to_prev, "z", 7)
 
@@ -365,17 +401,16 @@
 def per_device(hidden_student, hidden_teacher, targets, w_student, w_teacher):
     micro, tokens, _ = hidden_student.shape
     rows = micro * tokens
-    block, tgt, pick = join(
-        hidden_student.reshape(rows, -1), hidden_teacher.reshape(rows, -1), targets
-    )
-    early, late = gather_rows(block)
+    block = join(hidden_student.reshape(rows, -1), hidden_teacher.reshape(rows, -1))
+    tgt, pick = row_order(targets)
+    early, (sides, far) = gather_rows(block)
     s_early, t_early, h_early, part = compute_logits(early, w_student, w_teacher, tgt)
-    late, part = lax.optimization_barrier((late, part))
-    late = list(late) + [swap(piece, "c") for piece in late]
+    far, part = lax.optimization_barrier((far, part))
+    late = sides, swap(sides, "c"), far, swap(far, "c")
     s_late, t_late, h_late, part = compute_logits(late, w_student, w_teacher, tgt, (part, pick))
-    part = exchange_totals(part)
+    parts = exchange_totals(part)
     s, t = (s_early, s_late), (t_early, t_late)
-    g, send, keep, loss = compute_slope(s, t, part, pick, tgt, w_student)
+    g, send, keep, loss = compute_slope(s, t, parts, pick, tgt, w_student)
     grad_weight, done = compute_weight(g, h_early, h_late)
     grad_hidden = reduce_rows(send, keep, done)
     return loss, grad_hidden.astype(bf16).reshape(micro, tokens, -1), grad_weight

time: 101 us -> 99.1 us (0.981); the launches traced: 101 us -> 98.1 us
  starting transfers between devices: 41.9 us -> 32.8 us
  waiting for transfers between devices: 39.2 us -> 45.6 us
    ppermute x18 -> x17, starting transfers between devices: 34.3 us -> 27.8 us  [shift(): lax.ppermute(value, axis, [(i, (i + step) % size) for i in range(size)])]
    ppermute x18 -> x17, waiting for transfers between devices: 26.7 us -> 31.3 us  [shift(): lax.ppermute(value, axis, [(i, (i + step) % size) for i in range(size)])]
    ppermute x15 -> x10, starting transfers between devices: 7.62 us -> 4.98 us  [swap(): lax.ppermute(value, axis, [(i, i ^ mask) for i in range(SIZES[axis])])]
    ppermute x15 -> x10, waiting for transfers between devices: 12.5 us -> 14.3 us  [swap(): lax.ppermute(value, axis, [(i, i ^ mask) for i in range(SIZES[axis])])]
  transfers between devices with their start and end apart: 33 -> 27, of which waited for: 22 -> 21; matrix products, arithmetic and copies ran while one was open for 0% -> 0% of each run, Pallas kernels for 6% -> 6%
where the time goes in v3:
time: 99.1 us; the launch traced here: 98.1 us
  waiting for transfers between devices  45.6 us (46%)
  starting transfers between devices  32.8 us (33%)
  Pallas kernels  11.4 us (12%)
  local copies, waits for them, and re-layouts  6.88 us (7%)
    ppermute x17, waiting for transfers between devices, shift(): lax.ppermute(value, axis, [(i, (i + step) % size) for i in range(size)])  31.3 us
    ppermute x17, starting transfers between devices, shift(): lax.ppermute(value, axis, [(i, (i + step) % size) for i in range(size)])  27.8 us
    ppermute x10, waiting for transfers between devices, swap(): lax.ppermute(value, axis, [(i, i ^ mask) for i in range(SIZES[axis])])  14.3 us
    unnamed x14, local copies, waits for them, and re-layouts  6.88 us
    pallas_call x2, Pallas kernels, compute_logits(): pl.pallas_call(late_kernel if extra else early_kernel, out_shape=(shape((...  5.42 us
    ppermute x10, starting transfers between devices, swap(): lax.ppermute(value, axis, [(i, i ^ mask) for i in range(SIZES[axis])])  4.98 us
    pallas_call x1, Pallas kernels, compute_weight(): pl.pallas_call(weight_kernel, out_shape=(shape((vocab, width), bf16), sha...  3.53 us
  transfers between devices with their start and end apart: 27, of which 21 were waited for; matrix products, arithmetic and copies ran while one was open for 0% of the time, Pallas kernels for 6%

profile of v3, /device:TPU:4, one launch (start us, length us, event | category | flops | bytes accessed | tf_op | source)
XLA Modules:
  0.0 98.1 jit_solution(3078422010393135746)
XLA Ops:
  0.6 0.9 copy-done.4
  1.5 0.9 copy-done.5
  2.4 1.3 %collective-permute-start = (bf16[16,6656]{1,0:T(8,128)(2,1)S(1)}, bf16[16,6656]{1,0:T(8,128)(2,1)S(1)}, u32[]{:S(2)}, u32[]{:S(2)}) collective-permute-start(bf16[16,6656]{1,0:T(8,128)(2,1)S(1)} %join.1.a_ref), channel_id=1, source_target_pairs={{0,32},{32,0},{1,33},{33,1},{2,34},{34,2},{3,35},{35,3},{4,36},{36... | collective-permute-start | bytes 638984 | tf_op jit(solution)/shard_map/ppermute | solution.py:21
  3.7 3.0 %collective-permute-start.3 = (bf16[16,6656]{1,0:T(8,128)(2,1)S(1)}, bf16[16,6656]{1,0:T(8,128)(2,1)S(1)}, u32[]{:S(2)}, u32[]{:S(2)}) collective-permute-start(bf16[16,6656]{1,0:T(8,128)(2,1)S(1)} %join.1.a_ref), channel_id=1, source_target_pairs={{0,192},{64,0},{128,64},{192,128},{1,193},{65,1},{129,65},{193,129... | collective-permute-start | bytes 638984 | tf_op jit(solution)/shard_map/ppermute | solution.py:26
  6.7 2.8 %collective-permute-done.b_ref = bf16[16,6656]{1,0:T(8,128)(2,1)S(1)} collective-permute-done((bf16[16,6656]{1,0:T(8,128)(2,1)S(1)}, bf16[16,6656]{1,0:T(8,128)(2,1)S(1)}, u32[]{:S(2)}, u32[]{:S(2)}) %collective-permute-start) | collective-permute-done | bytes 213024 | tf_op jit(solution)/shard_map/ppermute | solution.py:21
  9.7 1.3 %collective-permute-done.3.b_ref = bf16[16,6656]{1,0:T(8,128)(2,1)S(1)} collective-permute-done((bf16[16,6656]{1,0:T(8,128)(2,1)S(1)}, bf16[16,6656]{1,0:T(8,128)(2,1)S(1)}, u32[]{:S(2)}, u32[]{:S(2)}) %collective-permute-start.3) | collective-permute-done | bytes 213024 | tf_op jit(solution)/shard_map/ppermute | solution.py:26
  11.0 3.4 %collective-permute-done.2.a_ref = bf16[16,6656]{1,0:T(8,128)(2,1)S(1)} collective-permute-done((bf16[16,6656]{1,0:T(8,128)(2,1)S(1)}, bf16[16,6656]{1,0:T(8,128)(2,1)S(1)}, u32[]{:S(2)}, u32[]{:S(2)}) %collective-permute-start.2) | collective-permute-done | bytes 213024 | tf_op jit(solution)/shard_map/ppermute | solution.py:26
  14.6 0.9 collective-permute-start.5
  15.5 0.7 copy-done.6
  16.5 1.9 %copy-done = bf16[640,2560]{1,0:T(8,128)(2,1)S(1)} copy-done((bf16[640,2560]{1,0:T(8,128)(2,1)S(1)}, bf16[640,2560]{1,0:T(8,128)(2,1)}, u32[]{:S(2)}) %copy-start) | copy-done | bytes 3276824
  18.4 2.5 %copy-done.2 = bf16[640,4096]{1,0:T(8,128)(2,1)S(1)} copy-done((bf16[640,4096]{1,0:T(8,128)(2,1)S(1)}, bf16[640,4096]{1,0:T(8,128)(2,1)}, u32[]{:S(2)}) %copy-start.2) | copy-done | bytes 5242904
  20.9 2.6 %early_logits.1 = (f32[640,128]{1,0:T(8,128)S(1)}, f32[640,128]{1,0:T(8,128)S(1)}, bf16[128,2560]{1,0:T(8,128)(2,1)S(1)}, f32[16,128]{1,0:T(8,128)S(1)}) custom-call(bf16[32,6656]{1,0:T(8,128)(2,1)S(1)} %pair.2.refs_0_, bf16[32,6656]{1,0:T(8,128)(2,1)S(1)} %collective-permute-done.1.refs_1_, bf16[32,6656]{1,0:T(8,128)(2,1)S(1)} %pair.3.refs_2_, ...), custom_call_target="tpu_custom_call" | custom-call | flops 1090519040 | bytes 12582912 | tf_op jit(solution)/shard_map/early_logits/pallas_call | solution.py:171
  23.4 4.8 %collective-permute-done.7.refs_2_ = bf16[32,6656]{1,0:T(8,128)(2,1)S(1)} collective-permute-done((bf16[32,6656]{1,0:T(8,128)(2,1)S(1)}, bf16[32,6656]{1,0:T(8,128)(2,1)S(1)}, u32[]{:S(2)}, u32[]{:S(2)}) %collective-permute-start.7) | collective-permute-done | bytes 426016 | tf_op jit(solution)/shard_map/ppermute | solution.py:26
  28.3 0.5 collective-permute-start.8
  28.8 1.3 %collective-permute-done.6.refs_1_ = bf16[32,6656]{1,0:T(8,128)(2,1)S(1)} collective-permute-done((bf16[32,6656]{1,0:T(8,128)(2,1)S(1)}, bf16[32,6656]{1,0:T(8,128)(2,1)S(1)}, u32[]{:S(2)}, u32[]{:S(2)}) %collective-permute-start.6) | collective-permute-done | bytes 426016 | tf_op jit(solution)/shard_map/ppermute | solution.py:21
  30.0 0.6 collective-permute-done.8.refs_3_
  30.6 2.9 %late_logits.1 = (f32[640,128]{1,0:T(8,128)S(1)}, f32[640,128]{1,0:T(8,128)S(1)}, bf16[128,2560]{1,0:T(8,128)(2,1)S(1)}, f32[16,256]{1,0:T(8,128)S(1)}) custom-call(bf16[32,6656]{1,0:T(8,128)(2,1)S(1)} %collective-permute-done.5.refs_0_, bf16[32,6656]{1,0:T(8,128)(2,1)S(1)} %collective-permute-done.6.refs_1_, ...), custom_call_target="tpu_custom_call" | custom-call | flops 1090519040 | bytes 12582912 | tf_op jit(solution)/shard_map/late_logits/pallas_call | solution.py:171
  33.7 1.1 %collective-permute-done.9.refs_1_ = f32[16,256]{1,0:T(8,128)S(1)} collective-permute-done((f32[16,256]{1,0:T(8,128)S(1)}, f32[16,256]{1,0:T(8,128)S(1)}, u32[]{:S(2)}, u32[]{:S(2)}) %collective-permute-start.9) | collective-permute-done | bytes 16416 | tf_op jit(solution)/shard_map/ppermute | solution.py:21
  34.7 0.9 collective-permute-start.10
  35.7 2.9 %collective-permute-done.10.refs_1_ = f32[16,256]{1,0:T(8,128)S(1)} collective-permute-done((f32[16,256]{1,0:T(8,128)S(1)}, f32[16,256]{1,0:T(8,128)S(1)}, u32[]{:S(2)}, u32[]{:S(2)}) %collective-permute-start.10) | collective-permute-done | bytes 16416 | tf_op jit(solution)/shard_map/ppermute | solution.py:21
  38.6 1.8 %collective-permute-start.13 = (f32[16,256]{1,0:T(8,128)S(1)}, f32[16,256]{1,0:T(8,128)S(1)}, u32[]{:S(2)}, u32[]{:S(2)}) collective-permute-start(f32[16,256]{1,0:T(8,128)S(1)} %merge.5.refs_0_), channel_id=1, source_target_pairs={{0,128},{64,192},{128,0},{192,64},{1,129},{65,193},{129,1},{193,65... | collective-permute-start | bytes 49160 | tf_op jit(solution)/shard_map/ppermute | solution.py:26
  40.4 0.3 collective-permute-start.12
  40.7 1.7 %collective-permute-start.11 = (f32[16,256]{1,0:T(8,128)S(1)}, f32[16,256]{1,0:T(8,128)S(1)}, u32[]{:S(2)}, u32[]{:S(2)}) collective-permute-start(f32[16,256]{1,0:T(8,128)S(1)} %merge.5.refs_0_), channel_id=1, source_target_pairs={{0,64},{64,128},{128,192},{192,0},{1,65},{65,129},{129,193},{193,1... | collective-permute-start | bytes 49160 | tf_op jit(solution)/shard_map/ppermute | solution.py:26
  42.4 1.5 %collective-permute-done.13.refs_3_ = f32[16,256]{1,0:T(8,128)S(1)} collective-permute-done((f32[16,256]{1,0:T(8,128)S(1)}, f32[16,256]{1,0:T(8,128)S(1)}, u32[]{:S(2)}, u32[]{:S(2)}) %collective-permute-start.13) | collective-permute-done | bytes 16416 | tf_op jit(solution)/shard_map/ppermute | solution.py:26
  44.1 1.5 %collective-permute-done.11.refs_1_ = f32[16,256]{1,0:T(8,128)S(1)} collective-permute-done((f32[16,256]{1,0:T(8,128)S(1)}, f32[16,256]{1,0:T(8,128)S(1)}, u32[]{:S(2)}, u32[]{:S(2)}) %collective-permute-start.11) | collective-permute-done | bytes 16416 | tf_op jit(solution)/shard_map/ppermute | solution.py:26
  45.7 5.9 %collective-permute-start.15 = (f32[16,256]{1,0:T(8,128)S(1)}, f32[16,256]{1,0:T(8,128)S(1)}, u32[]{:S(2)}, u32[]{:S(2)}) collective-permute-start(f32[16,256]{1,0:T(8,128)S(1)} %merge.6.refs_0_), channel_id=1, source_target_pairs={{0,14},{2,0},{4,2},{6,4},{8,6},{10,8},{12,10},{14,12},{1,15},{3,1}... | collective-permute-start | bytes 49160 | tf_op jit(solution)/shard_map/ppermute | solution.py:26
  51.6 1.4 %collective-permute-done.15.refs_2_ = f32[16,256]{1,0:T(8,128)S(1)} collective-permute-done((f32[16,256]{1,0:T(8,128)S(1)}, f32[16,256]{1,0:T(8,128)S(1)}, u32[]{:S(2)}, u32[]{:S(2)}) %collective-permute-start.15) | collective-permute-done | bytes 16416 | tf_op jit(solution)/shard_map/ppermute | solution.py:26
  53.0 3.5 %collective-permute-done.14.refs_1_ = f32[16,256]{1,0:T(8,128)S(1)} collective-permute-done((f32[16,256]{1,0:T(8,128)S(1)}, f32[16,256]{1,0:T(8,128)S(1)}, u32[]{:S(2)}, u32[]{:S(2)}) %collective-permute-start.14) | collective-permute-done | bytes 16416 | tf_op jit(solution)/shard_map/ppermute | solution.py:26
  56.7 2.4 %collective-permute-start.16 = (f32[16,256]{1,0:T(8,128)S(1)}, f32[16,256]{1,0:T(8,128)S(1)}, u32[]{:S(2)}, u32[]{:S(2)}) collective-permute-start(f32[16,256]{1,0:T(8,128)S(1)} %get-tuple-element.42.refs_4_), channel_id=1, source_target_pairs={{0,10},{2,12},{4,14},{6,0},{8,2},{10,4},{12,6},{14,8},{1,11},{3,13... | collective-permute-start | bytes 49160 | tf_op jit(solution)/shard_map/ppermute | solution.py:26
  59.0 3.5 %collective-permute-done.17.refs_6_ = f32[16,256]{1,0:T(8,128)S(1)} collective-permute-done((f32[16,256]{1,0:T(8,128)S(1)}, f32[16,256]{1,0:T(8,128)S(1)}, u32[]{:S(2)}, u32[]{:S(2)}) %collective-permute-start.17) | collective-permute-done | bytes 16416 | tf_op jit(solution)/shard_map/ppermute | solution.py:26
  62.5 1.8 %slope.1 = (bf16[640,256]{1,0:T(8,128)(2,1)S(1)}, bf16[128,2560]{1,0:T(8,128)(2,1)S(1)}, f32[128,2560]{1,0:T(8,128)S(1)}, f32[2]{0:T(128)}) custom-call(f32[640,128]{1,0:T(8,128)S(1)} %get-tuple-element.33.refs_0_, f32[640,128]{1,0:T(8,128)S(1)} %get-tuple-element.38.refs_1_, f32[640,128]{1,0:T(8,128)S(1)} %get-tuple-element.39.refs_2_, ...), custom_call_target="tpu_custom_call" | custom-call | flops 838860800 | bytes 8388608 | tf_op jit(solution)/shard_map/slope/pallas_call | solution.py:228
  64.4 2.1 %collective-permute-done.18.got_ref = bf16[128,2560]{1,0:T(8,128)(2,1)S(1)} collective-permute-done((bf16[128,2560]{1,0:T(8,128)(2,1)S(1)}, bf16[128,2560]{1,0:T(8,128)(2,1)S(1)}, u32[]{:S(2)}, u32[]{:S(2)}) %collective-permute-start.18) | collective-permute-done | bytes 655392 | tf_op jit(solution)/shard_map/ppermute | solution.py:21
  66.7 0.6 collective-permute-start.19
  67.3 1.8 %collective-permute-start.20 = (bf16[32,2560]{1,0:T(8,128)(2,1)S(1)}, bf16[32,2560]{1,0:T(8,128)(2,1)S(1)}, u32[]{:S(2)}, u32[]{:S(2)}) collective-permute-start(bf16[32,2560]{1,0:T(8,128)(2,1)S(1)} %get-tuple-element.49), channel_id=1, source_target_pairs={{0,128},{64,192},{128,0},{192,64},{1,129},{65,193},{129,1},{193,65... | collective-permute-start | bytes 491528 | tf_op jit(solution)/shard_map/ppermute | solution.py:26
  69.0 1.0 %collective-permute-start.21 = (bf16[32,2560]{1,0:T(8,128)(2,1)S(1)}, bf16[32,2560]{1,0:T(8,128)(2,1)S(1)}, u32[]{:S(2)}, u32[]{:S(2)}) collective-permute-start(bf16[32,2560]{1,0:T(8,128)(2,1)S(1)} %get-tuple-element.50), channel_id=1, source_target_pairs={{0,192},{64,0},{128,64},{192,128},{1,193},{65,1},{129,65},{193,129... | collective-permute-start | bytes 491528 | tf_op jit(solution)/shard_map/ppermute | solution.py:26
  70.0 3.5 %weight.1 = (bf16[640,2560]{1,0:T(8,128)(2,1)}, f32[8,128]{1,0:T(8,128)S(1)}) custom-call(bf16[640,256]{1,0:T(8,128)(2,1)S(1)} %get-tuple-element.51.g_ref, bf16[128,2560]{1,0:T(8,128)(2,1)S(1)} %get-tuple-element.52.a_ref, bf16[128,2560]{1,0:T(8,128)(2,1)S(1)} %get-tuple-element.53.b_ref), custom_call_target="tpu_custom_call" | custom-call | flops 838860800 | bytes 6291456 | tf_op jit(solution)/shard_map/weight/pallas_call | solution.py:257
  73.6 4.1 %collective-permute-done.19.a_ref = bf16[32,2560]{1,0:T(8,128)(2,1)S(1)} collective-permute-done((bf16[32,2560]{1,0:T(8,128)(2,1)S(1)}, bf16[32,2560]{1,0:T(8,128)(2,1)S(1)}, u32[]{:S(2)}, u32[]{:S(2)}) %collective-permute-start.19) | collective-permute-done | bytes 163872 | tf_op jit(solution)/shard_map/ppermute | solution.py:26
  77.7 0.6 collective-permute-done.21.c_ref
  78.4 0.9 collective-permute-start.22
  79.3 3.6 %collective-permute-done.22.got_ref = bf16[16,2560]{1,0:T(8,128)(2,1)S(1)} collective-permute-done((bf16[16,2560]{1,0:T(8,128)(2,1)S(1)}, bf16[16,2560]{1,0:T(8,128)(2,1)S(1)}, u32[]{:S(2)}, u32[]{:S(2)}) %collective-permute-start.22) | collective-permute-done | bytes 81952 | tf_op jit(solution)/shard_map/ppermute | solution.py:21
  83.0 3.2 %collective-permute-start.23 = (f32[3,16,320]{2,1,0:T(8,128)S(1)}, f32[3,16,320]{2,1,0:T(8,128)S(1)}, u32[]{:S(2)}, u32[]{:S(2)}) collective-permute-start(f32[3,16,320]{2,1,0:T(8,128)S(1)} %get-tuple-element.58), channel_id=1, source_target_pairs={{0,6},{2,8},{4,10},{6,12},{8,14},{10,0},{12,2},{14,4},{1,7},{3,9},... | collective-permute-start | bytes 184328 | tf_op jit(solution)/shard_map/ppermute | solution.py:26
  86.3 2.0 %collective-permute-start.24 = (f32[2,16,320]{2,1,0:T(8,128)S(1)}, f32[2,16,320]{2,1,0:T(8,128)S(1)}, u32[]{:S(2)}, u32[]{:S(2)}) collective-permute-start(f32[2,16,320]{2,1,0:T(8,128)S(1)} %get-tuple-element.59), channel_id=1, source_target_pairs={{0,12},{2,14},{4,0},{6,2},{8,4},{10,6},{12,8},{14,10},{1,13},{3,15... | collective-permute-start | bytes 122888 | tf_op jit(solution)/shard_map/ppermute | solution.py:26
  88.2 3.0 %collective-permute-done.24 = f32[2,16,320]{2,1,0:T(8,128)S(1)} collective-permute-done((f32[2,16,320]{2,1,0:T(8,128)S(1)}, f32[2,16,320]{2,1,0:T(8,128)S(1)}, u32[]{:S(2)}, u32[]{:S(2)}) %collective-permute-start.24) | collective-permute-done | bytes 40992 | tf_op jit(solution)/shard_map/ppermute | solution.py:26
  91.3 2.4 %collective-permute-start.25 = (f32[16,320]{1,0:T(8,128)S(1)}, f32[16,320]{1,0:T(8,128)S(1)}, u32[]{:S(2)}, u32[]{:S(2)}) collective-permute-start(f32[16,320]{1,0:T(8,128)S(1)} %get-tuple-element.61), channel_id=1, source_target_pairs={{0,2},{2,4},{4,6},{6,8},{8,10},{10,12},{12,14},{14,0},{1,3},{3,5},... | collective-permute-start | bytes 61448 | tf_op jit(solution)/shard_map/ppermute | solution.py:26
  93.7 1.5 %collective-permute-start.26 = (f32[16,320]{1,0:T(8,128)S(1)}, f32[16,320]{1,0:T(8,128)S(1)}, u32[]{:S(2)}, u32[]{:S(2)}) collective-permute-start(f32[16,320]{1,0:T(8,128)S(1)} %get-tuple-element.62), channel_id=1, source_target_pairs={{0,14},{2,0},{4,2},{6,4},{8,6},{10,8},{12,10},{14,12},{1,15},{3,1}... | collective-permute-start | bytes 61448 | tf_op jit(solution)/shard_map/ppermute | solution.py:26
  95.2 1.7 %collective-permute-done.25 = f32[16,320]{1,0:T(8,128)S(1)} collective-permute-done((f32[16,320]{1,0:T(8,128)S(1)}, f32[16,320]{1,0:T(8,128)S(1)}, u32[]{:S(2)}, u32[]{:S(2)}) %collective-permute-start.25) | collective-permute-done | bytes 20512 | tf_op jit(solution)/shard_map/ppermute | solution.py:26
  96.9 0.6 collective-permute-done.26
  97.5 0.6 fusion.6
  (37 shorter events, 1.6 us)
Async XLA Ops:
  0.6 0.9 copy-start.4
  1.5 0.9 copy-start.5
  2.4 7.1 %collective-permute-start = (bf16[16,6656]{1,0:T(8,128)(2,1)S(1)}, bf16[16,6656]{1,0:T(8,128)(2,1)S(1)}, u32[]{:S(2)}, u32[]{:S(2)}) collective-permute-start(bf16[16,6656]{1,0:T(8,128)(2,1)S(1)} %join.1.a_ref), channel_id=1, source_target_pairs={{0,32},{32,0},{1,33},{33,1},{2,34},{34,2},{3,35},{35,3},{4,36},{36... | collective-permute-start | bytes 638984 | tf_op jit(solution)/shard_map/ppermute | solution.py:21
  3.7 7.2 %collective-permute-start.3 = (bf16[16,6656]{1,0:T(8,128)(2,1)S(1)}, bf16[16,6656]{1,0:T(8,128)(2,1)S(1)}, u32[]{:S(2)}, u32[]{:S(2)}) collective-permute-start(bf16[16,6656]{1,0:T(8,128)(2,1)S(1)} %join.1.a_ref), channel_id=1, source_target_pairs={{0,192},{64,0},{128,64},{192,128},{1,193},{65,1},{129,65},{193,129... | collective-permute-start | bytes 638984 | tf_op jit(solution)/shard_map/ppermute | solution.py:26
  6.7 7.6 %collective-permute-start.2 = (bf16[16,6656]{1,0:T(8,128)(2,1)S(1)}, bf16[16,6656]{1,0:T(8,128)(2,1)S(1)}, u32[]{:S(2)}, u32[]{:S(2)}) collective-permute-start(bf16[16,6656]{1,0:T(8,128)(2,1)S(1)} %join.1.a_ref), channel_id=1, source_target_pairs={{0,64},{64,128},{128,192},{192,0},{1,65},{65,129},{129,193},{193,1... | collective-permute-start | bytes 638984 | tf_op jit(solution)/shard_map/ppermute | solution.py:26
  9.6 6.9 %collective-permute-start.1 = (bf16[32,6656]{1,0:T(8,128)(2,1)S(1)}, bf16[32,6656]{1,0:T(8,128)(2,1)S(1)}, u32[]{:S(2)}, u32[]{:S(2)}) collective-permute-start(bf16[32,6656]{1,0:T(8,128)(2,1)S(1)} %pair.2.refs_0_), channel_id=1, source_target_pairs={{0,16},{16,0},{1,17},{17,1},{2,18},{18,2},{3,19},{19,3},{4,20},{20... | collective-permute-start | bytes 1277960 | tf_op jit(solution)/shard_map/ppermute | solution.py:21
  14.4 2.0 %collective-permute-start.4 = (bf16[32,6656]{1,0:T(8,128)(2,1)S(1)}, bf16[32,6656]{1,0:T(8,128)(2,1)S(1)}, u32[]{:S(2)}, u32[]{:S(2)}) collective-permute-start(bf16[32,6656]{1,0:T(8,128)(2,1)S(1)} %pair.3.refs_2_), channel_id=1, source_target_pairs={{0,16},{16,0},{1,17},{17,1},{2,18},{18,2},{3,19},{19,3},{4,20},{20... | collective-permute-start | bytes 1277960 | tf_op jit(solution)/shard_map/ppermute | solution.py:21
  14.5 13.7 %collective-permute-start.7 = (bf16[32,6656]{1,0:T(8,128)(2,1)S(1)}, bf16[32,6656]{1,0:T(8,128)(2,1)S(1)}, u32[]{:S(2)}, u32[]{:S(2)}) collective-permute-start(bf16[32,6656]{1,0:T(8,128)(2,1)S(1)} %pair.2.refs_0_), channel_id=1, source_target_pairs={{0,128},{64,192},{128,0},{192,64},{1,129},{65,193},{129,1},{193,65... | collective-permute-start | bytes 1277960 | tf_op jit(solution)/shard_map/ppermute | solution.py:26
  14.6 13.6 %collective-permute-start.5 = (bf16[32,6656]{1,0:T(8,128)(2,1)S(1)}, bf16[32,6656]{1,0:T(8,128)(2,1)S(1)}, u32[]{:S(2)}, u32[]{:S(2)}) collective-permute-start(bf16[32,6656]{1,0:T(8,128)(2,1)S(1)} %pair.3.refs_2_), channel_id=1, source_target_pairs={{0,32},{32,0},{1,33},{33,1},{2,34},{34,2},{3,35},{35,3},{4,36},{36... | collective-permute-start | bytes 1277960 | tf_op jit(solution)/shard_map/ppermute | solution.py:21
  15.5 0.7 copy-start.6
  16.5 1.9 %copy-start = (bf16[640,2560]{1,0:T(8,128)(2,1)S(1)}, bf16[640,2560]{1,0:T(8,128)(2,1)}, u32[]{:S(2)}) copy-start(bf16[640,2560]{1,0:T(8,128)(2,1)} %refs_9_.1) | copy-start | bytes 9830404
  18.4 2.5 %copy-start.2 = (bf16[640,4096]{1,0:T(8,128)(2,1)S(1)}, bf16[640,4096]{1,0:T(8,128)(2,1)}, u32[]{:S(2)}) copy-start(bf16[640,4096]{1,0:T(8,128)(2,1)} %refs_5_.3) | copy-start | bytes 15728644
  20.9 9.8 %copy-start.1 = (bf16[640,2560]{1,0:T(8,128)(2,1)S(1)}, bf16[640,2560]{1,0:T(8,128)(2,1)}, u32[]{:S(2)}) copy-start(bf16[640,2560]{1,0:T(8,128)(2,1)} %refs_9_.1) | copy-start | bytes 9830404
  20.9 9.8 %copy-start.3 = (bf16[640,4096]{1,0:T(8,128)(2,1)S(1)}, bf16[640,4096]{1,0:T(8,128)(2,1)}, u32[]{:S(2)}) copy-start(bf16[640,4096]{1,0:T(8,128)(2,1)} %refs_5_.3) | copy-start | bytes 15728644
  28.3 1.8 %collective-permute-start.6 = (bf16[32,6656]{1,0:T(8,128)(2,1)S(1)}, bf16[32,6656]{1,0:T(8,128)(2,1)S(1)}, u32[]{:S(2)}, u32[]{:S(2)}) collective-permute-start(bf16[32,6656]{1,0:T(8,128)(2,1)S(1)} %collective-permute-done.5.refs_0_), channel_id=1, source_target_pairs={{0,16},{16,0},{1,17},{17,1},{2,18},{18,2},{3,19},{19,3},{4,20},{20... | collective-permute-start | bytes 1277960 | tf_op jit(solution)/shard_map/ppermute | solution.py:21
  28.3 2.4 %collective-permute-start.8 = (bf16[32,6656]{1,0:T(8,128)(2,1)S(1)}, bf16[32,6656]{1,0:T(8,128)(2,1)S(1)}, u32[]{:S(2)}, u32[]{:S(2)}) collective-permute-start(bf16[32,6656]{1,0:T(8,128)(2,1)S(1)} %collective-permute-done.7.refs_2_), channel_id=1, source_target_pairs={{0,16},{16,0},{1,17},{17,1},{2,18},{18,2},{3,19},{19,3},{4,20},{20... | collective-permute-start | bytes 1277960 | tf_op jit(solution)/shard_map/ppermute | solution.py:21
  33.5 1.2 %collective-permute-start.9 = (f32[16,256]{1,0:T(8,128)S(1)}, f32[16,256]{1,0:T(8,128)S(1)}, u32[]{:S(2)}, u32[]{:S(2)}) collective-permute-start(f32[16,256]{1,0:T(8,128)S(1)} %get-tuple-element.41.refs_0_), channel_id=1, source_target_pairs={{0,16},{16,0},{1,17},{17,1},{2,18},{18,2},{3,19},{19,3},{4,20},{20... | collective-permute-start | bytes 49160 | tf_op jit(solution)/shard_map/ppermute | solution.py:21
  34.7 3.8 %collective-permute-start.10 = (f32[16,256]{1,0:T(8,128)S(1)}, f32[16,256]{1,0:T(8,128)S(1)}, u32[]{:S(2)}, u32[]{:S(2)}) collective-permute-start(f32[16,256]{1,0:T(8,128)S(1)} %merge.4.refs_0_), channel_id=1, source_target_pairs={{0,32},{32,0},{1,33},{33,1},{2,34},{34,2},{3,35},{35,3},{4,36},{36... | collective-permute-start | bytes 49160 | tf_op jit(solution)/shard_map/ppermute | solution.py:21
  38.6 5.3 %collective-permute-start.13 = (f32[16,256]{1,0:T(8,128)S(1)}, f32[16,256]{1,0:T(8,128)S(1)}, u32[]{:S(2)}, u32[]{:S(2)}) collective-permute-start(f32[16,256]{1,0:T(8,128)S(1)} %merge.5.refs_0_), channel_id=1, source_target_pairs={{0,128},{64,192},{128,0},{192,64},{1,129},{65,193},{129,1},{193,65... | collective-permute-start | bytes 49160 | tf_op jit(solution)/shard_map/ppermute | solution.py:26
  40.4 3.7 %collective-permute-start.12 = (f32[16,256]{1,0:T(8,128)S(1)}, f32[16,256]{1,0:T(8,128)S(1)}, u32[]{:S(2)}, u32[]{:S(2)}) collective-permute-start(f32[16,256]{1,0:T(8,128)S(1)} %merge.5.refs_0_), channel_id=1, source_target_pairs={{0,192},{64,0},{128,64},{192,128},{1,193},{65,1},{129,65},{193,129... | collective-permute-start | bytes 49160 | tf_op jit(solution)/shard_map/ppermute | solution.py:26
  40.7 5.0 %collective-permute-start.11 = (f32[16,256]{1,0:T(8,128)S(1)}, f32[16,256]{1,0:T(8,128)S(1)}, u32[]{:S(2)}, u32[]{:S(2)}) collective-permute-start(f32[16,256]{1,0:T(8,128)S(1)} %merge.5.refs_0_), channel_id=1, source_target_pairs={{0,64},{64,128},{128,192},{192,0},{1,65},{65,129},{129,193},{193,1... | collective-permute-start | bytes 49160 | tf_op jit(solution)/shard_map/ppermute | solution.py:26
  45.7 7.4 %collective-permute-start.15 = (f32[16,256]{1,0:T(8,128)S(1)}, f32[16,256]{1,0:T(8,128)S(1)}, u32[]{:S(2)}, u32[]{:S(2)}) collective-permute-start(f32[16,256]{1,0:T(8,128)S(1)} %merge.6.refs_0_), channel_id=1, source_target_pairs={{0,14},{2,0},{4,2},{6,4},{8,6},{10,8},{12,10},{14,12},{1,15},{3,1}... | collective-permute-start | bytes 49160 | tf_op jit(solution)/shard_map/ppermute | solution.py:26
  51.6 4.9 %collective-permute-start.14 = (f32[16,256]{1,0:T(8,128)S(1)}, f32[16,256]{1,0:T(8,128)S(1)}, u32[]{:S(2)}, u32[]{:S(2)}) collective-permute-start(f32[16,256]{1,0:T(8,128)S(1)} %merge.6.refs_0_), channel_id=1, source_target_pairs={{0,2},{2,4},{4,6},{6,8},{8,10},{10,12},{12,14},{14,0},{1,3},{3,5},... | collective-permute-start | bytes 49160 | tf_op jit(solution)/shard_map/ppermute | solution.py:26
  56.6 5.9 %collective-permute-start.17 = (f32[16,256]{1,0:T(8,128)S(1)}, f32[16,256]{1,0:T(8,128)S(1)}, u32[]{:S(2)}, u32[]{:S(2)}) collective-permute-start(f32[16,256]{1,0:T(8,128)S(1)} %get-tuple-element.43), channel_id=1, source_target_pairs={{0,4},{2,6},{4,8},{6,10},{8,12},{10,14},{12,0},{14,2},{1,5},{3,7},... | collective-permute-start | bytes 49160 | tf_op jit(solution)/shard_map/ppermute | solution.py:26
  56.7 5.8 %collective-permute-start.16 = (f32[16,256]{1,0:T(8,128)S(1)}, f32[16,256]{1,0:T(8,128)S(1)}, u32[]{:S(2)}, u32[]{:S(2)}) collective-permute-start(f32[16,256]{1,0:T(8,128)S(1)} %get-tuple-element.42.refs_4_), channel_id=1, source_target_pairs={{0,10},{2,12},{4,14},{6,0},{8,2},{10,4},{12,6},{14,8},{1,11},{3,13... | collective-permute-start | bytes 49160 | tf_op jit(solution)/shard_map/ppermute | solution.py:26
  64.3 2.2 %collective-permute-start.18 = (bf16[128,2560]{1,0:T(8,128)(2,1)S(1)}, bf16[128,2560]{1,0:T(8,128)(2,1)S(1)}, u32[]{:S(2)}, u32[]{:S(2)}) collective-permute-start(bf16[128,2560]{1,0:T(8,128)(2,1)S(1)} %get-tuple-element.46), channel_id=1, source_target_pairs={{0,16},{16,0},{1,17},{17,1},{2,18},{18,2},{3,19},{19,3},{4,20},{20... | collective-permute-start | bytes 1966088 | tf_op jit(solution)/shard_map/ppermute | solution.py:21
  66.7 11.0 %collective-permute-start.19 = (bf16[32,2560]{1,0:T(8,128)(2,1)S(1)}, bf16[32,2560]{1,0:T(8,128)(2,1)S(1)}, u32[]{:S(2)}, u32[]{:S(2)}) collective-permute-start(bf16[32,2560]{1,0:T(8,128)(2,1)S(1)} %get-tuple-element.48), channel_id=1, source_target_pairs={{0,64},{64,128},{128,192},{192,0},{1,65},{65,129},{129,193},{193,1... | collective-permute-start | bytes 491528 | tf_op jit(solution)/shard_map/ppermute | solution.py:26
  67.3 10.4 %collective-permute-start.20 = (bf16[32,2560]{1,0:T(8,128)(2,1)S(1)}, bf16[32,2560]{1,0:T(8,128)(2,1)S(1)}, u32[]{:S(2)}, u32[]{:S(2)}) collective-permute-start(bf16[32,2560]{1,0:T(8,128)(2,1)S(1)} %get-tuple-element.49), channel_id=1, source_target_pairs={{0,128},{64,192},{128,0},{192,64},{1,129},{65,193},{129,1},{193,65... | collective-permute-start | bytes 491528 | tf_op jit(solution)/shard_map/ppermute | solution.py:26
  69.0 9.3 %collective-permute-start.21 = (bf16[32,2560]{1,0:T(8,128)(2,1)S(1)}, bf16[32,2560]{1,0:T(8,128)(2,1)S(1)}, u32[]{:S(2)}, u32[]{:S(2)}) collective-permute-start(bf16[32,2560]{1,0:T(8,128)(2,1)S(1)} %get-tuple-element.50), channel_id=1, source_target_pairs={{0,192},{64,0},{128,64},{192,128},{1,193},{65,1},{129,65},{193,129... | collective-permute-start | bytes 491528 | tf_op jit(solution)/shard_map/ppermute | solution.py:26
  78.4 4.5 %collective-permute-start.22 = (bf16[16,2560]{1,0:T(8,128)(2,1)S(1)}, bf16[16,2560]{1,0:T(8,128)(2,1)S(1)}, u32[]{:S(2)}, u32[]{:S(2)}) collective-permute-start(bf16[16,2560]{1,0:T(8,128)(2,1)S(1)} %get-tuple-element.56), channel_id=1, source_target_pairs={{0,32},{32,0},{1,33},{33,1},{2,34},{34,2},{3,35},{35,3},{4,36},{36... | collective-permute-start | bytes 245768 | tf_op jit(solution)/shard_map/ppermute | solution.py:21
  83.0 8.2 %collective-permute-start.23 = (f32[3,16,320]{2,1,0:T(8,128)S(1)}, f32[3,16,320]{2,1,0:T(8,128)S(1)}, u32[]{:S(2)}, u32[]{:S(2)}) collective-permute-start(f32[3,16,320]{2,1,0:T(8,128)S(1)} %get-tuple-element.58), channel_id=1, source_target_pairs={{0,6},{2,8},{4,10},{6,12},{8,14},{10,0},{12,2},{14,4},{1,7},{3,9},... | collective-permute-start | bytes 184328 | tf_op jit(solution)/shard_map/ppermute | solution.py:26
  86.3 5.0 %collective-permute-start.24 = (f32[2,16,320]{2,1,0:T(8,128)S(1)}, f32[2,16,320]{2,1,0:T(8,128)S(1)}, u32[]{:S(2)}, u32[]{:S(2)}) collective-permute-start(f32[2,16,320]{2,1,0:T(8,128)S(1)} %get-tuple-element.59), channel_id=1, source_target_pairs={{0,12},{2,14},{4,0},{6,2},{8,4},{10,6},{12,8},{14,10},{1,13},{3,15... | collective-permute-start | bytes 122888 | tf_op jit(solution)/shard_map/ppermute | solution.py:26
  91.3 5.6 %collective-permute-start.25 = (f32[16,320]{1,0:T(8,128)S(1)}, f32[16,320]{1,0:T(8,128)S(1)}, u32[]{:S(2)}, u32[]{:S(2)}) collective-permute-start(f32[16,320]{1,0:T(8,128)S(1)} %get-tuple-element.61), channel_id=1, source_target_pairs={{0,2},{2,4},{4,6},{6,8},{8,10},{10,12},{12,14},{14,0},{1,3},{3,5},... | collective-permute-start | bytes 61448 | tf_op jit(solution)/shard_map/ppermute | solution.py:26
  93.7 3.8 %collective-permute-start.26 = (f32[16,320]{1,0:T(8,128)S(1)}, f32[16,320]{1,0:T(8,128)S(1)}, u32[]{:S(2)}, u32[]{:S(2)}) collective-permute-start(f32[16,320]{1,0:T(8,128)S(1)} %get-tuple-element.62), channel_id=1, source_target_pairs={{0,14},{2,0},{4,2},{6,4},{8,6},{10,8},{12,10},{14,12},{1,15},{3,1}... | collective-permute-start | bytes 61448 | tf_op jit(solution)/shard_map/ppermute | solution.py:26

commit v4 on v3

--- a/solution.py
+++ b/solution.py
@@ -11,7 +11,6 @@
 RING_Y, PAIR_X, CORES, RING_Z = 4, 2, 2, 8
 SIZES = {"y": RING_Y, "x": PAIR_X, "c": CORES, "z": RING_Z}
 MB = 1 << 20
-JOIN_MB = 4
 bf16, f32 = jnp.bfloat16, jnp.float32
 VMEM = pl.BlockSpec(memory_space=pltpu.VMEM)
 SMEM = pl.BlockSpec(memory_space=pltpu.SMEM)
@@ -30,13 +29,14 @@
 LATE = ((3, 1), (1, 1), (2, 0), (2, 1))
 
 
-def gather_rows(block):
+def gather_rows(block, tgt):
     across = swap(block, "x")
     prev = shift(block, "y", 1)
     next_ = shift(block, "y", 3)
     sides, here = pair(prev, next_), pair(block, across)
-    early = here, swap(here, "c"), sides, swap(sides, "c")
-    return early, (swap(sides, "x"), shift(here, "y", 2))
+    held, tgt = lax.optimization_barrier((here, tgt))
+    early = here, swap(held, "c"), sides, swap(sides, "c")
+    return early, (swap(sides, "x"), shift(here, "y", 2)), tgt
 
 
 def first_entry(vocab):
@@ -68,7 +68,7 @@
         out_shape=jax.ShapeDtypeStruct((rows, student.shape[1] + teacher.shape[1]), bf16),
         in_specs=[VMEM] * 2,
         out_specs=VMEM,
-        compiler_params=pltpu.CompilerParams(vmem_limit_bytes=JOIN_MB * MB),
+        compiler_params=pltpu.CompilerParams(vmem_limit_bytes=4 * MB),
         name="join",
     )(student, teacher)
 
@@ -123,21 +123,22 @@
     )(targets)
 
 
-def half_logits(blocks, ws_ref, wt_ref, tgt, s_ref, t_ref, hs_ref, ht_ref):
+def half_logits(blocks, ws_ref, wt_ref, tgt, s_ref, t_ref, hs_ref):
     width = ws_ref.shape[1]
     for i, ref in enumerate(blocks):
         hs_ref[i * 32 : i * 32 + 32, :] = ref[:, :width]
-        ht_ref[i * 32 : i * 32 + 32, :] = ref[:, width:]
+    ht = jnp.concatenate([ref[:, width:] for ref in blocks], 0)
     dims = (((1,), (1,)), ((), ()))
     s = lax.dot_general(ws_ref[...], hs_ref[...], dims, preferred_element_type=f32)
     s_ref[...] = s
     ms = jnp.max(s, axis=0, keepdims=True)
     total = lambda v: jnp.sum(v, axis=0, keepdims=True)
     hit = lax.broadcasted_iota(jnp.int32, s.shape, 0) == tgt - first_entry(s.shape[0])
-    z1 = total(jnp.exp(s - ms))
-    z2 = total(jnp.exp((s - ms) * 0.5))
+    root = jnp.exp((s - ms) * 0.5)
+    z1 = total(root * root)
+    z2 = total(root)
     picked = total(jnp.where(hit, s, 0.0))
-    t = lax.dot_general(wt_ref[...], ht_ref[...], dims, preferred_element_type=f32)
+    t = lax.dot_general(wt_ref[...], ht, dims, preferred_element_type=f32)
     t_ref[...] = t
     mt = jnp.max(t, axis=0, keepdims=True)
     et = jnp.exp((t - mt) * 0.5)
@@ -150,16 +151,16 @@
 
 def early_kernel(*refs):
     ws_ref, wt_ref, tgt_ref = refs[4:7]
-    s_ref, t_ref, hs_ref, part_ref, ht_ref = refs[7:]
+    s_ref, t_ref, hs_ref, part_ref = refs[7:]
     tgt = tgt_ref[:, :128]
-    part_ref[...] = half_logits(refs[:4], ws_ref, wt_ref, tgt, s_ref, t_ref, hs_ref, ht_ref)
+    part_ref[...] = half_logits(refs[:4], ws_ref, wt_ref, tgt, s_ref, t_ref, hs_ref)
 
 
 def late_kernel(*refs):
     ws_ref, wt_ref, tgt_ref, early_ref, pick_ref = refs[4:9]
-    s_ref, t_ref, hs_ref, part_ref, ht_ref = refs[9:]
+    s_ref, t_ref, hs_ref, part_ref = refs[9:]
     tgt = tgt_ref[:, 128:]
-    part = half_logits(refs[:4], ws_ref, wt_ref, tgt, s_ref, t_ref, hs_ref, ht_ref)
+    part = half_logits(refs[:4], ws_ref, wt_ref, tgt, s_ref, t_ref, hs_ref)
     part = jnp.concatenate([early_ref[...], part], 1)
     part_ref[...] = permuted(part, pick_ref[...], True)
 
@@ -178,7 +179,6 @@
         ),
         in_specs=[VMEM] * (7 + len(extra)),
         out_specs=(VMEM,) * 4,
-        scratch_shapes=[pltpu.VMEM((rows, wt.shape[1]), bf16)],
         compiler_params=pltpu.CompilerParams(vmem_limit_bytes=20 * MB),
         cost_estimate=pl.CostEstimate(
             flops=2 * vocab * rows * (width + wt.shape[1]),
@@ -207,9 +207,10 @@
         at = slice(i * 128, i * 128 + 128)
         d = s_refs[i][...] - ms[:, at]
         hit = lax.broadcasted_iota(jnp.int32, d.shape, 0) == tgt[:, at]
-        g = jnp.exp(d * 0.5) * r2[:, at]
+        root = jnp.exp(d * 0.5)
+        g = root * r2[:, at]
         g = g - jnp.exp(t_refs[i][...] * 0.5 - half_mt[:, at]) * rt[:, at]
-        g = g + (jnp.exp(d) * r1[:, at] - jnp.where(hit, 0.5, 0.0))
+        g = g + (root * root * r1[:, at] - jnp.where(hit, 0.5, 0.0))
         g_ref[:, at] = g.astype(bf16)
     p = lax.dot_general(
         g_ref[...], ws_ref[...], (((0,), (0,)), ((), ())), preferred_element_type=f32
@@ -386,15 +387,30 @@
     )(own, *moved, after)
 
 
+def far_kernel(mine_ref, a_ref, b_ref, next_ref, prev_ref, own_ref):
+    next_ref[...] = mine_ref[2] + a_ref[2]
+    prev_ref[...] = mine_ref[0] + a_ref[0] + b_ref[1]
+    own_ref[...] = mine_ref[1] + a_ref[1] + b_ref[0]
+
+
+def add_far(mine, from_a, from_b):
+    return pl.pallas_call(
+        far_kernel,
+        out_shape=(jax.ShapeDtypeStruct(mine.shape[1:], f32),) * 3,
+        in_specs=[VMEM] * 3,
+        out_specs=(VMEM,) * 3,
+        compiler_params=pltpu.CompilerParams(vmem_limit_bytes=2 * MB),
+        name="add_far",
+    )(mine, from_a, from_b)
+
+
 def reduce_rows(send, keep, after):
     own, *parts = add_core(keep, swap(send, "c"))
     moved = [shift(part, "y", d + 1) for d, part in enumerate(parts)]
     own, part = add_ring(own, moved, after)
     ahead, behind, mine = split_features(own, swap(part, "x"))
     from_a, from_b = shift(ahead, "z", 3), shift(behind, "z", 6)
-    to_next = mine[2] + from_a[2]
-    to_prev = mine[0] + from_a[0] + from_b[1]
-    own = mine[1] + from_a[1] + from_b[0]
+    to_next, to_prev, own = add_far(mine, from_a, from_b)
     return own + shift(to_next, "z", 1) + shift(to_prev, "z", 7)
 
 
@@ -403,10 +419,12 @@
     rows = micro * tokens
     block = join(hidden_student.reshape(rows, -1), hidden_teacher.reshape(rows, -1))
     tgt, pick = row_order(targets)
-    early, (sides, far) = gather_rows(block)
+    early, (sides, far), tgt = gather_rows(block, tgt)
     s_early, t_early, h_early, part = compute_logits(early, w_student, w_teacher, tgt)
-    far, part = lax.optimization_barrier((far, part))
-    late = sides, swap(sides, "c"), far, swap(far, "c")
+    sides, part = lax.optimization_barrier((sides, part))
+    sides_swapped = swap(sides, "c")
+    far, sides_swapped = lax.optimization_barrier((far, sides_swapped))
+    late = sides, sides_swapped, far, swap(far, "c")
     s_late, t_late, h_late, part = compute_logits(late, w_student, w_teacher, tgt, (part, pick))
     parts = exchange_totals(part)
     s, t = (s_early, s_late), (t_early, t_late)

time: 99.1 us -> 98.3 us (level)
  starting transfers between devices: 32.8 us -> 31.4 us
  waiting for transfers between devices: 45.6 us -> 46.8 us
    ppermute x10, waiting for transfers between devices: 14.3 us -> 17 us  [swap(): lax.ppermute(value, axis, [(i, i ^ mask) for i in range(SIZES[axis])])]
    ppermute x17, starting transfers between devices: 27.8 us -> 26.2 us  [shift(): lax.ppermute(value, axis, [(i, (i + step) % size) for i in range(size)])]
    ppermute x17, waiting for transfers between devices: 31.3 us -> 29.8 us  [shift(): lax.ppermute(value, axis, [(i, (i + step) % size) for i in range(size)])]
where the time goes in v4:
time: 98.3 us; the launch traced here: 97.7 us
  waiting for transfers between devices  46.8 us (48%)
  starting transfers between devices  31.4 us (32%)
  Pallas kernels  11.3 us (11%)
  local copies, waits for them, and re-layouts  6.88 us (7%)
    ppermute x17, waiting for transfers between devices, shift(): lax.ppermute(value, axis, [(i, (i + step) % size) for i in range(size)])  29.8 us
    ppermute x17, starting transfers between devices, shift(): lax.ppermute(value, axis, [(i, (i + step) % size) for i in range(size)])  26.2 us
    ppermute x10, waiting for transfers between devices, swap(): lax.ppermute(value, axis, [(i, i ^ mask) for i in range(SIZES[axis])])  17 us
    unnamed x14, local copies, waits for them, and re-layouts  6.88 us
    pallas_call x2, Pallas kernels, compute_logits(): pl.pallas_call(late_kernel if extra else early_kernel, out_shape=(shape((...  5.26 us
    ppermute x10, starting transfers between devices, swap(): lax.ppermute(value, axis, [(i, i ^ mask) for i in range(SIZES[axis])])  5.22 us
    pallas_call x1, Pallas kernels, compute_weight(): pl.pallas_call(weight_kernel, out_shape=(shape((vocab, width), bf16), sha...  3.53 us
  transfers between devices with their start and end apart: 27, of which 21 were waited for; matrix products, arithmetic and copies ran while one was open for 0% of the time, Pallas kernels for 6%

profile of v4, /device:TPU:4, one launch (start us, length us, event | category | flops | bytes accessed | tf_op | source)
XLA Modules:
  0.0 97.7 jit_solution(3288682938356947626)
XLA Ops:
  0.6 0.9 copy-done.4
  1.5 0.9 copy-done.5
  2.4 1.3 %collective-permute-start = (bf16[16,6656]{1,0:T(8,128)(2,1)S(1)}, bf16[16,6656]{1,0:T(8,128)(2,1)S(1)}, u32[]{:S(2)}, u32[]{:S(2)}) collective-permute-start(bf16[16,6656]{1,0:T(8,128)(2,1)S(1)} %join.1.a_ref), channel_id=1, source_target_pairs={{0,32},{32,0},{1,33},{33,1},{2,34},{34,2},{3,35},{35,3},{4,36},{36... | collective-permute-start | bytes 638984 | tf_op jit(solution)/shard_map/ppermute | solution.py:20
  3.7 3.0 %collective-permute-start.3 = (bf16[16,6656]{1,0:T(8,128)(2,1)S(1)}, bf16[16,6656]{1,0:T(8,128)(2,1)S(1)}, u32[]{:S(2)}, u32[]{:S(2)}) collective-permute-start(bf16[16,6656]{1,0:T(8,128)(2,1)S(1)} %join.1.a_ref), channel_id=1, source_target_pairs={{0,192},{64,0},{128,64},{192,128},{1,193},{65,1},{129,65},{193,129... | collective-permute-start | bytes 638984 | tf_op jit(solution)/shard_map/ppermute | solution.py:25
  6.7 0.7 copy-done.6
  7.4 0.2 row_order.1
  7.6 1.9 %collective-permute-done.b_ref = bf16[16,6656]{1,0:T(8,128)(2,1)S(1)} collective-permute-done((bf16[16,6656]{1,0:T(8,128)(2,1)S(1)}, bf16[16,6656]{1,0:T(8,128)(2,1)S(1)}, u32[]{:S(2)}, u32[]{:S(2)}) %collective-permute-start) | collective-permute-done | bytes 213024 | tf_op jit(solution)/shard_map/ppermute | solution.py:20
  9.7 1.3 %collective-permute-done.3.b_ref = bf16[16,6656]{1,0:T(8,128)(2,1)S(1)} collective-permute-done((bf16[16,6656]{1,0:T(8,128)(2,1)S(1)}, bf16[16,6656]{1,0:T(8,128)(2,1)S(1)}, u32[]{:S(2)}, u32[]{:S(2)}) %collective-permute-start.3) | collective-permute-done | bytes 213024 | tf_op jit(solution)/shard_map/ppermute | solution.py:25
  11.0 3.4 %collective-permute-done.2.a_ref = bf16[16,6656]{1,0:T(8,128)(2,1)S(1)} collective-permute-done((bf16[16,6656]{1,0:T(8,128)(2,1)S(1)}, bf16[16,6656]{1,0:T(8,128)(2,1)S(1)}, u32[]{:S(2)}, u32[]{:S(2)}) %collective-permute-start.2) | collective-permute-done | bytes 213024 | tf_op jit(solution)/shard_map/ppermute | solution.py:25
  14.5 0.9 collective-permute-start.5
  15.4 0.8 collective-permute-done.4.refs_3_
  16.3 1.9 %copy-done = bf16[640,2560]{1,0:T(8,128)(2,1)S(1)} copy-done((bf16[640,2560]{1,0:T(8,128)(2,1)S(1)}, bf16[640,2560]{1,0:T(8,128)(2,1)}, u32[]{:S(2)}) %copy-start) | copy-done | bytes 3276824
  18.2 2.5 %copy-done.2 = bf16[640,4096]{1,0:T(8,128)(2,1)S(1)} copy-done((bf16[640,4096]{1,0:T(8,128)(2,1)S(1)}, bf16[640,4096]{1,0:T(8,128)(2,1)}, u32[]{:S(2)}) %copy-start.2) | copy-done | bytes 5242904
  20.7 2.5 %early_logits.1 = (f32[640,128]{1,0:T(8,128)S(1)}, f32[640,128]{1,0:T(8,128)S(1)}, bf16[128,2560]{1,0:T(8,128)(2,1)S(1)}, f32[16,128]{1,0:T(8,128)S(1)}) custom-call(bf16[32,6656]{1,0:T(8,128)(2,1)S(1)} %pair.2.refs_0_, bf16[32,6656]{1,0:T(8,128)(2,1)S(1)} %collective-permute-done.1.refs_1_, bf16[32,6656]{1,0:T(8,128)(2,1)S(1)} %pair.3.refs_2_, ...), custom_call_target="tpu_custom_call" | custom-call | flops 1090519040 | bytes 12582912 | tf_op jit(solution)/shard_map/early_logits/pallas_call | solution.py:172
  23.2 3.6 %collective-permute-done.5.refs_0_ = bf16[32,6656]{1,0:T(8,128)(2,1)S(1)} collective-permute-done((bf16[32,6656]{1,0:T(8,128)(2,1)S(1)}, bf16[32,6656]{1,0:T(8,128)(2,1)S(1)}, u32[]{:S(2)}, u32[]{:S(2)}) %collective-permute-start.5) | collective-permute-done | bytes 426016 | tf_op jit(solution)/shard_map/ppermute | solution.py:20
  26.8 2.0 %collective-permute-done.6.refs_2_ = bf16[32,6656]{1,0:T(8,128)(2,1)S(1)} collective-permute-done((bf16[32,6656]{1,0:T(8,128)(2,1)S(1)}, bf16[32,6656]{1,0:T(8,128)(2,1)S(1)}, u32[]{:S(2)}, u32[]{:S(2)}) %collective-permute-start.6) | collective-permute-done | bytes 426016 | tf_op jit(solution)/shard_map/ppermute | solution.py:25
  28.8 1.8 %collective-permute-done.8.refs_3_ = bf16[32,6656]{1,0:T(8,128)(2,1)S(1)} collective-permute-done((bf16[32,6656]{1,0:T(8,128)(2,1)S(1)}, bf16[32,6656]{1,0:T(8,128)(2,1)S(1)}, u32[]{:S(2)}, u32[]{:S(2)}) %collective-permute-start.8) | collective-permute-done | bytes 426016 | tf_op jit(solution)/shard_map/ppermute | solution.py:20
  30.6 2.8 %late_logits.1 = (f32[640,128]{1,0:T(8,128)S(1)}, f32[640,128]{1,0:T(8,128)S(1)}, bf16[128,2560]{1,0:T(8,128)(2,1)S(1)}, f32[16,256]{1,0:T(8,128)S(1)}) custom-call(bf16[32,6656]{1,0:T(8,128)(2,1)S(1)} %collective-permute-done.5.refs_0_, bf16[32,6656]{1,0:T(8,128)(2,1)S(1)} %collective-permute-done.7.refs_1_, ...), custom_call_target="tpu_custom_call" | custom-call | flops 1090519040 | bytes 12582912 | tf_op jit(solution)/shard_map/late_logits/pallas_call | solution.py:172
  33.5 1.0 %collective-permute-done.9.refs_1_ = f32[16,256]{1,0:T(8,128)S(1)} collective-permute-done((f32[16,256]{1,0:T(8,128)S(1)}, f32[16,256]{1,0:T(8,128)S(1)}, u32[]{:S(2)}, u32[]{:S(2)}) %collective-permute-start.9) | collective-permute-done | bytes 16416 | tf_op jit(solution)/shard_map/ppermute | solution.py:20
  34.6 1.3 %collective-permute-start.10 = (f32[16,256]{1,0:T(8,128)S(1)}, f32[16,256]{1,0:T(8,128)S(1)}, u32[]{:S(2)}, u32[]{:S(2)}) collective-permute-start(f32[16,256]{1,0:T(8,128)S(1)} %merge.4.refs_0_), channel_id=1, source_target_pairs={{0,32},{32,0},{1,33},{33,1},{2,34},{34,2},{3,35},{35,3},{4,36},{36... | collective-permute-start | bytes 49160 | tf_op jit(solution)/shard_map/ppermute | solution.py:20
  35.9 2.5 %collective-permute-done.10.refs_1_ = f32[16,256]{1,0:T(8,128)S(1)} collective-permute-done((f32[16,256]{1,0:T(8,128)S(1)}, f32[16,256]{1,0:T(8,128)S(1)}, u32[]{:S(2)}, u32[]{:S(2)}) %collective-permute-start.10) | collective-permute-done | bytes 16416 | tf_op jit(solution)/shard_map/ppermute | solution.py:20
  38.4 0.4 collective-permute-start.13
  38.8 1.5 %collective-permute-start.12 = (f32[16,256]{1,0:T(8,128)S(1)}, f32[16,256]{1,0:T(8,128)S(1)}, u32[]{:S(2)}, u32[]{:S(2)}) collective-permute-start(f32[16,256]{1,0:T(8,128)S(1)} %merge.5.refs_0_), channel_id=1, source_target_pairs={{0,192},{64,0},{128,64},{192,128},{1,193},{65,1},{129,65},{193,129... | collective-permute-start | bytes 49160 | tf_op jit(solution)/shard_map/ppermute | solution.py:25
  40.3 0.6 collective-permute-start.11
  40.8 2.9 %collective-permute-done.13.refs_3_ = f32[16,256]{1,0:T(8,128)S(1)} collective-permute-done((f32[16,256]{1,0:T(8,128)S(1)}, f32[16,256]{1,0:T(8,128)S(1)}, u32[]{:S(2)}, u32[]{:S(2)}) %collective-permute-start.13) | collective-permute-done | bytes 16416 | tf_op jit(solution)/shard_map/ppermute | solution.py:25
  43.8 1.4 %collective-permute-done.11.refs_1_ = f32[16,256]{1,0:T(8,128)S(1)} collective-permute-done((f32[16,256]{1,0:T(8,128)S(1)}, f32[16,256]{1,0:T(8,128)S(1)}, u32[]{:S(2)}, u32[]{:S(2)}) %collective-permute-start.11) | collective-permute-done | bytes 16416 | tf_op jit(solution)/shard_map/ppermute | solution.py:25
  45.2 5.9 %collective-permute-start.15 = (f32[16,256]{1,0:T(8,128)S(1)}, f32[16,256]{1,0:T(8,128)S(1)}, u32[]{:S(2)}, u32[]{:S(2)}) collective-permute-start(f32[16,256]{1,0:T(8,128)S(1)} %merge.6.refs_0_), channel_id=1, source_target_pairs={{0,14},{2,0},{4,2},{6,4},{8,6},{10,8},{12,10},{14,12},{1,15},{3,1}... | collective-permute-start | bytes 49160 | tf_op jit(solution)/shard_map/ppermute | solution.py:25
  51.2 1.4 %collective-permute-done.15.refs_2_ = f32[16,256]{1,0:T(8,128)S(1)} collective-permute-done((f32[16,256]{1,0:T(8,128)S(1)}, f32[16,256]{1,0:T(8,128)S(1)}, u32[]{:S(2)}, u32[]{:S(2)}) %collective-permute-start.15) | collective-permute-done | bytes 16416 | tf_op jit(solution)/shard_map/ppermute | solution.py:25
  52.6 3.5 %collective-permute-done.14.refs_1_ = f32[16,256]{1,0:T(8,128)S(1)} collective-permute-done((f32[16,256]{1,0:T(8,128)S(1)}, f32[16,256]{1,0:T(8,128)S(1)}, u32[]{:S(2)}, u32[]{:S(2)}) %collective-permute-start.14) | collective-permute-done | bytes 16416 | tf_op jit(solution)/shard_map/ppermute | solution.py:25
  56.2 2.4 %collective-permute-start.16 = (f32[16,256]{1,0:T(8,128)S(1)}, f32[16,256]{1,0:T(8,128)S(1)}, u32[]{:S(2)}, u32[]{:S(2)}) collective-permute-start(f32[16,256]{1,0:T(8,128)S(1)} %get-tuple-element.53.refs_4_), channel_id=1, source_target_pairs={{0,10},{2,12},{4,14},{6,0},{8,2},{10,4},{12,6},{14,8},{1,11},{3,13... | collective-permute-start | bytes 49160 | tf_op jit(solution)/shard_map/ppermute | solution.py:25
  58.6 3.5 %collective-permute-done.17.refs_6_ = f32[16,256]{1,0:T(8,128)S(1)} collective-permute-done((f32[16,256]{1,0:T(8,128)S(1)}, f32[16,256]{1,0:T(8,128)S(1)}, u32[]{:S(2)}, u32[]{:S(2)}) %collective-permute-start.17) | collective-permute-done | bytes 16416 | tf_op jit(solution)/shard_map/ppermute | solution.py:25
  62.1 1.8 %slope.1 = (bf16[640,256]{1,0:T(8,128)(2,1)S(1)}, bf16[128,2560]{1,0:T(8,128)(2,1)S(1)}, f32[128,2560]{1,0:T(8,128)S(1)}, f32[2]{0:T(128)}) custom-call(f32[640,128]{1,0:T(8,128)S(1)} %get-tuple-element.42.refs_0_, f32[640,128]{1,0:T(8,128)S(1)} %get-tuple-element.49.refs_1_, f32[640,128]{1,0:T(8,128)S(1)} %get-tuple-element.50.refs_2_, ...), custom_call_target="tpu_custom_call" | custom-call | flops 838860800 | bytes 8388608 | tf_op jit(solution)/shard_map/slope/pallas_call | solution.py:229
  64.0 2.1 %collective-permute-done.18.got_ref = bf16[128,2560]{1,0:T(8,128)(2,1)S(1)} collective-permute-done((bf16[128,2560]{1,0:T(8,128)(2,1)S(1)}, bf16[128,2560]{1,0:T(8,128)(2,1)S(1)}, u32[]{:S(2)}, u32[]{:S(2)}) %collective-permute-start.18) | collective-permute-done | bytes 655392 | tf_op jit(solution)/shard_map/ppermute | solution.py:20
  66.3 2.6 %collective-permute-start.20 = (bf16[32,2560]{1,0:T(8,128)(2,1)S(1)}, bf16[32,2560]{1,0:T(8,128)(2,1)S(1)}, u32[]{:S(2)}, u32[]{:S(2)}) collective-permute-start(bf16[32,2560]{1,0:T(8,128)(2,1)S(1)} %get-tuple-element.60), channel_id=1, source_target_pairs={{0,128},{64,192},{128,0},{192,64},{1,129},{65,193},{129,1},{193,65... | collective-permute-start | bytes 491528 | tf_op jit(solution)/shard_map/ppermute | solution.py:25
  68.9 0.6 collective-permute-start.21
  69.5 3.5 %weight.1 = (bf16[640,2560]{1,0:T(8,128)(2,1)}, f32[8,128]{1,0:T(8,128)S(1)}) custom-call(bf16[640,256]{1,0:T(8,128)(2,1)S(1)} %get-tuple-element.62.g_ref, bf16[128,2560]{1,0:T(8,128)(2,1)S(1)} %get-tuple-element.63.a_ref, bf16[128,2560]{1,0:T(8,128)(2,1)S(1)} %get-tuple-element.64.b_ref), custom_call_target="tpu_custom_call" | custom-call | flops 838860800 | bytes 6291456 | tf_op jit(solution)/shard_map/weight/pallas_call | solution.py:258
  73.1 4.2 %collective-permute-done.19.a_ref = bf16[32,2560]{1,0:T(8,128)(2,1)S(1)} collective-permute-done((bf16[32,2560]{1,0:T(8,128)(2,1)S(1)}, bf16[32,2560]{1,0:T(8,128)(2,1)S(1)}, u32[]{:S(2)}, u32[]{:S(2)}) %collective-permute-start.19) | collective-permute-done | bytes 163872 | tf_op jit(solution)/shard_map/ppermute | solution.py:25
  77.3 0.6 collective-permute-done.21.c_ref
  78.0 1.3 %collective-permute-start.22 = (bf16[16,2560]{1,0:T(8,128)(2,1)S(1)}, bf16[16,2560]{1,0:T(8,128)(2,1)S(1)}, u32[]{:S(2)}, u32[]{:S(2)}) collective-permute-start(bf16[16,2560]{1,0:T(8,128)(2,1)S(1)} %get-tuple-element.67), channel_id=1, source_target_pairs={{0,32},{32,0},{1,33},{33,1},{2,34},{34,2},{3,35},{35,3},{4,36},{36... | collective-permute-start | bytes 245768 | tf_op jit(solution)/shard_map/ppermute | solution.py:20
  79.2 3.2 %collective-permute-done.22.got_ref = bf16[16,2560]{1,0:T(8,128)(2,1)S(1)} collective-permute-done((bf16[16,2560]{1,0:T(8,128)(2,1)S(1)}, bf16[16,2560]{1,0:T(8,128)(2,1)S(1)}, u32[]{:S(2)}, u32[]{:S(2)}) %collective-permute-start.22) | collective-permute-done | bytes 81952 | tf_op jit(solution)/shard_map/ppermute | solution.py:20
  82.6 3.2 %collective-permute-start.23 = (f32[3,16,320]{2,1,0:T(8,128)S(1)}, f32[3,16,320]{2,1,0:T(8,128)S(1)}, u32[]{:S(2)}, u32[]{:S(2)}) collective-permute-start(f32[3,16,320]{2,1,0:T(8,128)S(1)} %get-tuple-element.69), channel_id=1, source_target_pairs={{0,6},{2,8},{4,10},{6,12},{8,14},{10,0},{12,2},{14,4},{1,7},{3,9},... | collective-permute-start | bytes 184328 | tf_op jit(solution)/shard_map/ppermute | solution.py:25
  85.8 2.0 %collective-permute-start.24 = (f32[2,16,320]{2,1,0:T(8,128)S(1)}, f32[2,16,320]{2,1,0:T(8,128)S(1)}, u32[]{:S(2)}, u32[]{:S(2)}) collective-permute-start(f32[2,16,320]{2,1,0:T(8,128)S(1)} %get-tuple-element.70), channel_id=1, source_target_pairs={{0,12},{2,14},{4,0},{6,2},{8,4},{10,6},{12,8},{14,10},{1,13},{3,15... | collective-permute-start | bytes 122888 | tf_op jit(solution)/shard_map/ppermute | solution.py:25
  87.8 3.0 %collective-permute-done.24.b_ref = f32[2,16,320]{2,1,0:T(8,128)S(1)} collective-permute-done((f32[2,16,320]{2,1,0:T(8,128)S(1)}, f32[2,16,320]{2,1,0:T(8,128)S(1)}, u32[]{:S(2)}, u32[]{:S(2)}) %collective-permute-start.24) | collective-permute-done | bytes 40992 | tf_op jit(solution)/shard_map/ppermute | solution.py:25
  90.8 2.4 %collective-permute-start.25 = (f32[16,320]{1,0:T(8,128)S(1)}, f32[16,320]{1,0:T(8,128)S(1)}, u32[]{:S(2)}, u32[]{:S(2)}) collective-permute-start(f32[16,320]{1,0:T(8,128)S(1)} %get-tuple-element.72), channel_id=1, source_target_pairs={{0,2},{2,4},{4,6},{6,8},{8,10},{10,12},{12,14},{14,0},{1,3},{3,5},... | collective-permute-start | bytes 61448 | tf_op jit(solution)/shard_map/ppermute | solution.py:25
  93.2 1.5 %collective-permute-start.26 = (f32[16,320]{1,0:T(8,128)S(1)}, f32[16,320]{1,0:T(8,128)S(1)}, u32[]{:S(2)}, u32[]{:S(2)}) collective-permute-start(f32[16,320]{1,0:T(8,128)S(1)} %get-tuple-element.73), channel_id=1, source_target_pairs={{0,14},{2,0},{4,2},{6,4},{8,6},{10,8},{12,10},{14,12},{1,15},{3,1}... | collective-permute-start | bytes 61448 | tf_op jit(solution)/shard_map/ppermute | solution.py:25
  94.7 1.7 %collective-permute-done.25 = f32[16,320]{1,0:T(8,128)S(1)} collective-permute-done((f32[16,320]{1,0:T(8,128)S(1)}, f32[16,320]{1,0:T(8,128)S(1)}, u32[]{:S(2)}, u32[]{:S(2)}) %collective-permute-start.25) | collective-permute-done | bytes 20512 | tf_op jit(solution)/shard_map/ppermute | solution.py:25
  96.4 0.6 collective-permute-done.26
  97.1 0.6 fusion
  (37 shorter events, 1.1 us)
Async XLA Ops:
  0.6 0.9 copy-start.4
  1.5 0.9 copy-start.5
  2.4 7.1 %collective-permute-start = (bf16[16,6656]{1,0:T(8,128)(2,1)S(1)}, bf16[16,6656]{1,0:T(8,128)(2,1)S(1)}, u32[]{:S(2)}, u32[]{:S(2)}) collective-permute-start(bf16[16,6656]{1,0:T(8,128)(2,1)S(1)} %join.1.a_ref), channel_id=1, source_target_pairs={{0,32},{32,0},{1,33},{33,1},{2,34},{34,2},{3,35},{35,3},{4,36},{36... | collective-permute-start | bytes 638984 | tf_op jit(solution)/shard_map/ppermute | solution.py:20
  3.7 7.2 %collective-permute-start.3 = (bf16[16,6656]{1,0:T(8,128)(2,1)S(1)}, bf16[16,6656]{1,0:T(8,128)(2,1)S(1)}, u32[]{:S(2)}, u32[]{:S(2)}) collective-permute-start(bf16[16,6656]{1,0:T(8,128)(2,1)S(1)} %join.1.a_ref), channel_id=1, source_target_pairs={{0,192},{64,0},{128,64},{192,128},{1,193},{65,1},{129,65},{193,129... | collective-permute-start | bytes 638984 | tf_op jit(solution)/shard_map/ppermute | solution.py:25
  6.7 7.6 %collective-permute-start.2 = (bf16[16,6656]{1,0:T(8,128)(2,1)S(1)}, bf16[16,6656]{1,0:T(8,128)(2,1)S(1)}, u32[]{:S(2)}, u32[]{:S(2)}) collective-permute-start(bf16[16,6656]{1,0:T(8,128)(2,1)S(1)} %join.1.a_ref), channel_id=1, source_target_pairs={{0,64},{64,128},{128,192},{192,0},{1,65},{65,129},{129,193},{193,1... | collective-permute-start | bytes 638984 | tf_op jit(solution)/shard_map/ppermute | solution.py:25
  6.7 0.7 copy-start.6
  9.6 5.9 %collective-permute-start.1 = (bf16[32,6656]{1,0:T(8,128)(2,1)S(1)}, bf16[32,6656]{1,0:T(8,128)(2,1)S(1)}, u32[]{:S(2)}, u32[]{:S(2)}) collective-permute-start(bf16[32,6656]{1,0:T(8,128)(2,1)S(1)} %pair.2.refs_0_), channel_id=1, source_target_pairs={{0,16},{16,0},{1,17},{17,1},{2,18},{18,2},{3,19},{19,3},{4,20},{20... | collective-permute-start | bytes 1277960 | tf_op jit(solution)/shard_map/ppermute | solution.py:20
  14.4 1.9 %collective-permute-start.4 = (bf16[32,6656]{1,0:T(8,128)(2,1)S(1)}, bf16[32,6656]{1,0:T(8,128)(2,1)S(1)}, u32[]{:S(2)}, u32[]{:S(2)}) collective-permute-start(bf16[32,6656]{1,0:T(8,128)(2,1)S(1)} %pair.3.refs_2_), channel_id=1, source_target_pairs={{0,16},{16,0},{1,17},{17,1},{2,18},{18,2},{3,19},{19,3},{4,20},{20... | collective-permute-start | bytes 1277960 | tf_op jit(solution)/shard_map/ppermute | solution.py:20
  14.5 12.2 %collective-permute-start.5 = (bf16[32,6656]{1,0:T(8,128)(2,1)S(1)}, bf16[32,6656]{1,0:T(8,128)(2,1)S(1)}, u32[]{:S(2)}, u32[]{:S(2)}) collective-permute-start(bf16[32,6656]{1,0:T(8,128)(2,1)S(1)} %pair.3.refs_2_), channel_id=1, source_target_pairs={{0,32},{32,0},{1,33},{33,1},{2,34},{34,2},{3,35},{35,3},{4,36},{36... | collective-permute-start | bytes 1277960 | tf_op jit(solution)/shard_map/ppermute | solution.py:20
  15.4 13.4 %collective-permute-start.6 = (bf16[32,6656]{1,0:T(8,128)(2,1)S(1)}, bf16[32,6656]{1,0:T(8,128)(2,1)S(1)}, u32[]{:S(2)}, u32[]{:S(2)}) collective-permute-start(bf16[32,6656]{1,0:T(8,128)(2,1)S(1)} %pair.2.refs_0_), channel_id=1, source_target_pairs={{0,128},{64,192},{128,0},{192,64},{1,129},{65,193},{129,1},{193,65... | collective-permute-start | bytes 1277960 | tf_op jit(solution)/shard_map/ppermute | solution.py:25
  16.3 1.9 %copy-start = (bf16[640,2560]{1,0:T(8,128)(2,1)S(1)}, bf16[640,2560]{1,0:T(8,128)(2,1)}, u32[]{:S(2)}) copy-start(bf16[640,2560]{1,0:T(8,128)(2,1)} %refs_9_.1) | copy-start | bytes 9830404
  18.2 2.5 %copy-start.2 = (bf16[640,4096]{1,0:T(8,128)(2,1)S(1)}, bf16[640,4096]{1,0:T(8,128)(2,1)}, u32[]{:S(2)}) copy-start(bf16[640,4096]{1,0:T(8,128)(2,1)} %refs_5_.3) | copy-start | bytes 15728644
  20.7 9.9 %copy-start.1 = (bf16[640,2560]{1,0:T(8,128)(2,1)S(1)}, bf16[640,2560]{1,0:T(8,128)(2,1)}, u32[]{:S(2)}) copy-start(bf16[640,2560]{1,0:T(8,128)(2,1)} %refs_9_.1) | copy-start | bytes 9830404
  20.7 9.9 %copy-start.3 = (bf16[640,4096]{1,0:T(8,128)(2,1)S(1)}, bf16[640,4096]{1,0:T(8,128)(2,1)}, u32[]{:S(2)}) copy-start(bf16[640,4096]{1,0:T(8,128)(2,1)} %refs_5_.3) | copy-start | bytes 15728644
  26.8 2.1 %collective-permute-start.7 = (bf16[32,6656]{1,0:T(8,128)(2,1)S(1)}, bf16[32,6656]{1,0:T(8,128)(2,1)S(1)}, u32[]{:S(2)}, u32[]{:S(2)}) collective-permute-start(bf16[32,6656]{1,0:T(8,128)(2,1)S(1)} %collective-permute-done.5.refs_0_), channel_id=1, source_target_pairs={{0,16},{16,0},{1,17},{17,1},{2,18},{18,2},{3,19},{19,3},{4,20},{20... | collective-permute-start | bytes 1277960 | tf_op jit(solution)/shard_map/ppermute | solution.py:20
  28.8 1.8 %collective-permute-start.8 = (bf16[32,6656]{1,0:T(8,128)(2,1)S(1)}, bf16[32,6656]{1,0:T(8,128)(2,1)S(1)}, u32[]{:S(2)}, u32[]{:S(2)}) collective-permute-start(bf16[32,6656]{1,0:T(8,128)(2,1)S(1)} %collective-permute-done.6.refs_2_), channel_id=1, source_target_pairs={{0,16},{16,0},{1,17},{17,1},{2,18},{18,2},{3,19},{19,3},{4,20},{20... | collective-permute-start | bytes 1277960 | tf_op jit(solution)/shard_map/ppermute | solution.py:20
  33.4 1.2 %collective-permute-start.9 = (f32[16,256]{1,0:T(8,128)S(1)}, f32[16,256]{1,0:T(8,128)S(1)}, u32[]{:S(2)}, u32[]{:S(2)}) collective-permute-start(f32[16,256]{1,0:T(8,128)S(1)} %get-tuple-element.52.refs_0_), channel_id=1, source_target_pairs={{0,16},{16,0},{1,17},{17,1},{2,18},{18,2},{3,19},{19,3},{4,20},{20... | collective-permute-start | bytes 49160 | tf_op jit(solution)/shard_map/ppermute | solution.py:20
  34.6 3.8 %collective-permute-start.10 = (f32[16,256]{1,0:T(8,128)S(1)}, f32[16,256]{1,0:T(8,128)S(1)}, u32[]{:S(2)}, u32[]{:S(2)}) collective-permute-start(f32[16,256]{1,0:T(8,128)S(1)} %merge.4.refs_0_), channel_id=1, source_target_pairs={{0,32},{32,0},{1,33},{33,1},{2,34},{34,2},{3,35},{35,3},{4,36},{36... | collective-permute-start | bytes 49160 | tf_op jit(solution)/shard_map/ppermute | solution.py:20
  38.4 5.3 %collective-permute-start.13 = (f32[16,256]{1,0:T(8,128)S(1)}, f32[16,256]{1,0:T(8,128)S(1)}, u32[]{:S(2)}, u32[]{:S(2)}) collective-permute-start(f32[16,256]{1,0:T(8,128)S(1)} %merge.5.refs_0_), channel_id=1, source_target_pairs={{0,128},{64,192},{128,0},{192,64},{1,129},{65,193},{129,1},{193,65... | collective-permute-start | bytes 49160 | tf_op jit(solution)/shard_map/ppermute | solution.py:25
  38.8 5.0 %collective-permute-start.12 = (f32[16,256]{1,0:T(8,128)S(1)}, f32[16,256]{1,0:T(8,128)S(1)}, u32[]{:S(2)}, u32[]{:S(2)}) collective-permute-start(f32[16,256]{1,0:T(8,128)S(1)} %merge.5.refs_0_), channel_id=1, source_target_pairs={{0,192},{64,0},{128,64},{192,128},{1,193},{65,1},{129,65},{193,129... | collective-permute-start | bytes 49160 | tf_op jit(solution)/shard_map/ppermute | solution.py:25
  40.3 5.0 %collective-permute-start.11 = (f32[16,256]{1,0:T(8,128)S(1)}, f32[16,256]{1,0:T(8,128)S(1)}, u32[]{:S(2)}, u32[]{:S(2)}) collective-permute-start(f32[16,256]{1,0:T(8,128)S(1)} %merge.5.refs_0_), channel_id=1, source_target_pairs={{0,64},{64,128},{128,192},{192,0},{1,65},{65,129},{129,193},{193,1... | collective-permute-start | bytes 49160 | tf_op jit(solution)/shard_map/ppermute | solution.py:25
  45.2 7.4 %collective-permute-start.15 = (f32[16,256]{1,0:T(8,128)S(1)}, f32[16,256]{1,0:T(8,128)S(1)}, u32[]{:S(2)}, u32[]{:S(2)}) collective-permute-start(f32[16,256]{1,0:T(8,128)S(1)} %merge.6.refs_0_), channel_id=1, source_target_pairs={{0,14},{2,0},{4,2},{6,4},{8,6},{10,8},{12,10},{14,12},{1,15},{3,1}... | collective-permute-start | bytes 49160 | tf_op jit(solution)/shard_map/ppermute | solution.py:25
  51.2 4.9 %collective-permute-start.14 = (f32[16,256]{1,0:T(8,128)S(1)}, f32[16,256]{1,0:T(8,128)S(1)}, u32[]{:S(2)}, u32[]{:S(2)}) collective-permute-start(f32[16,256]{1,0:T(8,128)S(1)} %merge.6.refs_0_), channel_id=1, source_target_pairs={{0,2},{2,4},{4,6},{6,8},{8,10},{10,12},{12,14},{14,0},{1,3},{3,5},... | collective-permute-start | bytes 49160 | tf_op jit(solution)/shard_map/ppermute | solution.py:25
  56.1 5.9 %collective-permute-start.17 = (f32[16,256]{1,0:T(8,128)S(1)}, f32[16,256]{1,0:T(8,128)S(1)}, u32[]{:S(2)}, u32[]{:S(2)}) collective-permute-start(f32[16,256]{1,0:T(8,128)S(1)} %get-tuple-element.54), channel_id=1, source_target_pairs={{0,4},{2,6},{4,8},{6,10},{8,12},{10,14},{12,0},{14,2},{1,5},{3,7},... | collective-permute-start | bytes 49160 | tf_op jit(solution)/shard_map/ppermute | solution.py:25
  56.2 5.8 %collective-permute-start.16 = (f32[16,256]{1,0:T(8,128)S(1)}, f32[16,256]{1,0:T(8,128)S(1)}, u32[]{:S(2)}, u32[]{:S(2)}) collective-permute-start(f32[16,256]{1,0:T(8,128)S(1)} %get-tuple-element.53.refs_4_), channel_id=1, source_target_pairs={{0,10},{2,12},{4,14},{6,0},{8,2},{10,4},{12,6},{14,8},{1,11},{3,13... | collective-permute-start | bytes 49160 | tf_op jit(solution)/shard_map/ppermute | solution.py:25
  63.9 2.2 %collective-permute-start.18 = (bf16[128,2560]{1,0:T(8,128)(2,1)S(1)}, bf16[128,2560]{1,0:T(8,128)(2,1)S(1)}, u32[]{:S(2)}, u32[]{:S(2)}) collective-permute-start(bf16[128,2560]{1,0:T(8,128)(2,1)S(1)} %get-tuple-element.57), channel_id=1, source_target_pairs={{0,16},{16,0},{1,17},{17,1},{2,18},{18,2},{3,19},{19,3},{4,20},{20... | collective-permute-start | bytes 1966088 | tf_op jit(solution)/shard_map/ppermute | solution.py:20
  66.2 11.0 %collective-permute-start.19 = (bf16[32,2560]{1,0:T(8,128)(2,1)S(1)}, bf16[32,2560]{1,0:T(8,128)(2,1)S(1)}, u32[]{:S(2)}, u32[]{:S(2)}) collective-permute-start(bf16[32,2560]{1,0:T(8,128)(2,1)S(1)} %get-tuple-element.59), channel_id=1, source_target_pairs={{0,64},{64,128},{128,192},{192,0},{1,65},{65,129},{129,193},{193,1... | collective-permute-start | bytes 491528 | tf_op jit(solution)/shard_map/ppermute | solution.py:25
  66.3 11.0 %collective-permute-start.20 = (bf16[32,2560]{1,0:T(8,128)(2,1)S(1)}, bf16[32,2560]{1,0:T(8,128)(2,1)S(1)}, u32[]{:S(2)}, u32[]{:S(2)}) collective-permute-start(bf16[32,2560]{1,0:T(8,128)(2,1)S(1)} %get-tuple-element.60), channel_id=1, source_target_pairs={{0,128},{64,192},{128,0},{192,64},{1,129},{65,193},{129,1},{193,65... | collective-permute-start | bytes 491528 | tf_op jit(solution)/shard_map/ppermute | solution.py:25
  68.9 9.0 %collective-permute-start.21 = (bf16[32,2560]{1,0:T(8,128)(2,1)S(1)}, bf16[32,2560]{1,0:T(8,128)(2,1)S(1)}, u32[]{:S(2)}, u32[]{:S(2)}) collective-permute-start(bf16[32,2560]{1,0:T(8,128)(2,1)S(1)} %get-tuple-element.61), channel_id=1, source_target_pairs={{0,192},{64,0},{128,64},{192,128},{1,193},{65,1},{129,65},{193,129... | collective-permute-start | bytes 491528 | tf_op jit(solution)/shard_map/ppermute | solution.py:25
  78.0 4.5 %collective-permute-start.22 = (bf16[16,2560]{1,0:T(8,128)(2,1)S(1)}, bf16[16,2560]{1,0:T(8,128)(2,1)S(1)}, u32[]{:S(2)}, u32[]{:S(2)}) collective-permute-start(bf16[16,2560]{1,0:T(8,128)(2,1)S(1)} %get-tuple-element.67), channel_id=1, source_target_pairs={{0,32},{32,0},{1,33},{33,1},{2,34},{34,2},{3,35},{35,3},{4,36},{36... | collective-permute-start | bytes 245768 | tf_op jit(solution)/shard_map/ppermute | solution.py:20
  82.6 8.2 %collective-permute-start.23 = (f32[3,16,320]{2,1,0:T(8,128)S(1)}, f32[3,16,320]{2,1,0:T(8,128)S(1)}, u32[]{:S(2)}, u32[]{:S(2)}) collective-permute-start(f32[3,16,320]{2,1,0:T(8,128)S(1)} %get-tuple-element.69), channel_id=1, source_target_pairs={{0,6},{2,8},{4,10},{6,12},{8,14},{10,0},{12,2},{14,4},{1,7},{3,9},... | collective-permute-start | bytes 184328 | tf_op jit(solution)/shard_map/ppermute | solution.py:25
  85.8 5.0 %collective-permute-start.24 = (f32[2,16,320]{2,1,0:T(8,128)S(1)}, f32[2,16,320]{2,1,0:T(8,128)S(1)}, u32[]{:S(2)}, u32[]{:S(2)}) collective-permute-start(f32[2,16,320]{2,1,0:T(8,128)S(1)} %get-tuple-element.70), channel_id=1, source_target_pairs={{0,12},{2,14},{4,0},{6,2},{8,4},{10,6},{12,8},{14,10},{1,13},{3,15... | collective-permute-start | bytes 122888 | tf_op jit(solution)/shard_map/ppermute | solution.py:25
  90.8 5.6 %collective-permute-start.25 = (f32[16,320]{1,0:T(8,128)S(1)}, f32[16,320]{1,0:T(8,128)S(1)}, u32[]{:S(2)}, u32[]{:S(2)}) collective-permute-start(f32[16,320]{1,0:T(8,128)S(1)} %get-tuple-element.72), channel_id=1, source_target_pairs={{0,2},{2,4},{4,6},{6,8},{8,10},{10,12},{12,14},{14,0},{1,3},{3,5},... | collective-permute-start | bytes 61448 | tf_op jit(solution)/shard_map/ppermute | solution.py:25
  93.2 3.8 %collective-permute-start.26 = (f32[16,320]{1,0:T(8,128)S(1)}, f32[16,320]{1,0:T(8,128)S(1)}, u32[]{:S(2)}, u32[]{:S(2)}) collective-permute-start(f32[16,320]{1,0:T(8,128)S(1)} %get-tuple-element.73), channel_id=1, source_target_pairs={{0,14},{2,0},{4,2},{6,4},{8,6},{10,8},{12,10},{14,12},{1,15},{3,1}... | collective-permute-start | bytes 61448 | tf_op jit(solution)/shard_map/ppermute | solution.py:25

commit v5 on v4

--- a/solution.py
+++ b/solution.py
@@ -406,7 +406,7 @@
 
 def reduce_rows(send, keep, after):
     own, *parts = add_core(keep, swap(send, "c"))
-    moved = [shift(part, "y", d + 1) for d, part in enumerate(parts)]
+    moved = [shift(parts[d - 1], "y", d) for d in (1, 3, 2)]
     own, part = add_ring(own, moved, after)
     ahead, behind, mine = split_features(own, swap(part, "x"))
     from_a, from_b = shift(ahead, "z", 3), shift(behind, "z", 6)

time: 98.3 us -> 97.7 us (level)
  transfers between devices with their start and end apart: 27 -> 27, of which waited for: 21 -> 20; matrix products, arithmetic and copies ran while one was open for 0% -> 0% of each run, Pallas kernels for 6% -> 6%
where the time goes in v5:
time: 97.7 us; the launch traced here: 96.8 us
  waiting for transfers between devices  46.3 us (47%)
  starting transfers between devices  30.9 us (32%)
  Pallas kernels  11.3 us (12%)
  local copies, waits for them, and re-layouts  6.88 us (7%)
    ppermute x17, waiting for transfers between devices, shift(): lax.ppermute(value, axis, [(i, (i + step) % size) for i in range(size)])  29.3 us
    ppermute x17, starting transfers between devices, shift(): lax.ppermute(value, axis, [(i, (i + step) % size) for i in range(size)])  25.7 us
    ppermute x10, waiting for transfers between devices, swap(): lax.ppermute(value, axis, [(i, i ^ mask) for i in range(SIZES[axis])])  17 us
    unnamed x14, local copies, waits for them, and re-layouts  6.88 us
    pallas_call x2, Pallas kernels, compute_logits(): pl.pallas_call(late_kernel if extra else early_kernel, out_shape=(shape((...  5.26 us
    ppermute x10, starting transfers between devices, swap(): lax.ppermute(value, axis, [(i, i ^ mask) for i in range(SIZES[axis])])  5.22 us
    pallas_call x1, Pallas kernels, compute_weight(): pl.pallas_call(weight_kernel, out_shape=(shape((vocab, width), bf16), sha...  3.54 us
  transfers between devices with their start and end apart: 27, of which 20 were waited for; matrix products, arithmetic and copies ran while one was open for 0% of the time, Pallas kernels for 6%

profile of v5, /device:TPU:4, one launch (start us, length us, event | category | flops | bytes accessed | tf_op | source)
XLA Modules:
  0.0 96.8 jit_solution(17145634355536206175)
XLA Ops:
  0.6 0.9 copy-done.4
  1.5 0.9 copy-done.5
  2.4 1.3 %collective-permute-start = (bf16[16,6656]{1,0:T(8,128)(2,1)S(1)}, bf16[16,6656]{1,0:T(8,128)(2,1)S(1)}, u32[]{:S(2)}, u32[]{:S(2)}) collective-permute-start(bf16[16,6656]{1,0:T(8,128)(2,1)S(1)} %join.1.a_ref), channel_id=1, source_target_pairs={{0,32},{32,0},{1,33},{33,1},{2,34},{34,2},{3,35},{35,3},{4,36},{36... | collective-permute-start | bytes 638984 | tf_op jit(solution)/shard_map/ppermute | solution.py:20
  3.7 3.0 %collective-permute-start.3 = (bf16[16,6656]{1,0:T(8,128)(2,1)S(1)}, bf16[16,6656]{1,0:T(8,128)(2,1)S(1)}, u32[]{:S(2)}, u32[]{:S(2)}) collective-permute-start(bf16[16,6656]{1,0:T(8,128)(2,1)S(1)} %join.1.a_ref), channel_id=1, source_target_pairs={{0,192},{64,0},{128,64},{192,128},{1,193},{65,1},{129,65},{193,129... | collective-permute-start | bytes 638984 | tf_op jit(solution)/shard_map/ppermute | solution.py:25
  6.7 0.7 copy-done.6
  7.4 0.2 row_order.1
  7.6 1.9 %collective-permute-done.b_ref = bf16[16,6656]{1,0:T(8,128)(2,1)S(1)} collective-permute-done((bf16[16,6656]{1,0:T(8,128)(2,1)S(1)}, bf16[16,6656]{1,0:T(8,128)(2,1)S(1)}, u32[]{:S(2)}, u32[]{:S(2)}) %collective-permute-start) | collective-permute-done | bytes 213024 | tf_op jit(solution)/shard_map/ppermute | solution.py:20
  9.7 1.3 %collective-permute-done.3.b_ref = bf16[16,6656]{1,0:T(8,128)(2,1)S(1)} collective-permute-done((bf16[16,6656]{1,0:T(8,128)(2,1)S(1)}, bf16[16,6656]{1,0:T(8,128)(2,1)S(1)}, u32[]{:S(2)}, u32[]{:S(2)}) %collective-permute-start.3) | collective-permute-done | bytes 213024 | tf_op jit(solution)/shard_map/ppermute | solution.py:25
  11.0 3.4 %collective-permute-done.2.a_ref = bf16[16,6656]{1,0:T(8,128)(2,1)S(1)} collective-permute-done((bf16[16,6656]{1,0:T(8,128)(2,1)S(1)}, bf16[16,6656]{1,0:T(8,128)(2,1)S(1)}, u32[]{:S(2)}, u32[]{:S(2)}) %collective-permute-start.2) | collective-permute-done | bytes 213024 | tf_op jit(solution)/shard_map/ppermute | solution.py:25
  14.5 0.9 collective-permute-start.5
  15.4 0.8 collective-permute-done.4.refs_3_
  16.3 1.9 %copy-done = bf16[640,2560]{1,0:T(8,128)(2,1)S(1)} copy-done((bf16[640,2560]{1,0:T(8,128)(2,1)S(1)}, bf16[640,2560]{1,0:T(8,128)(2,1)}, u32[]{:S(2)}) %copy-start) | copy-done | bytes 3276824
  18.2 2.5 %copy-done.2 = bf16[640,4096]{1,0:T(8,128)(2,1)S(1)} copy-done((bf16[640,4096]{1,0:T(8,128)(2,1)S(1)}, bf16[640,4096]{1,0:T(8,128)(2,1)}, u32[]{:S(2)}) %copy-start.2) | copy-done | bytes 5242904
  20.7 2.5 %early_logits.1 = (f32[640,128]{1,0:T(8,128)S(1)}, f32[640,128]{1,0:T(8,128)S(1)}, bf16[128,2560]{1,0:T(8,128)(2,1)S(1)}, f32[16,128]{1,0:T(8,128)S(1)}) custom-call(bf16[32,6656]{1,0:T(8,128)(2,1)S(1)} %pair.2.refs_0_, bf16[32,6656]{1,0:T(8,128)(2,1)S(1)} %collective-permute-done.1.refs_1_, bf16[32,6656]{1,0:T(8,128)(2,1)S(1)} %pair.3.refs_2_, ...), custom_call_target="tpu_custom_call" | custom-call | flops 1090519040 | bytes 12582912 | tf_op jit(solution)/shard_map/early_logits/pallas_call | solution.py:172
  23.2 3.6 %collective-permute-done.5.refs_0_ = bf16[32,6656]{1,0:T(8,128)(2,1)S(1)} collective-permute-done((bf16[32,6656]{1,0:T(8,128)(2,1)S(1)}, bf16[32,6656]{1,0:T(8,128)(2,1)S(1)}, u32[]{:S(2)}, u32[]{:S(2)}) %collective-permute-start.5) | collective-permute-done | bytes 426016 | tf_op jit(solution)/shard_map/ppermute | solution.py:20
  26.8 2.0 %collective-permute-done.6.refs_2_ = bf16[32,6656]{1,0:T(8,128)(2,1)S(1)} collective-permute-done((bf16[32,6656]{1,0:T(8,128)(2,1)S(1)}, bf16[32,6656]{1,0:T(8,128)(2,1)S(1)}, u32[]{:S(2)}, u32[]{:S(2)}) %collective-permute-start.6) | collective-permute-done | bytes 426016 | tf_op jit(solution)/shard_map/ppermute | solution.py:25
  28.8 1.8 %collective-permute-done.8.refs_3_ = bf16[32,6656]{1,0:T(8,128)(2,1)S(1)} collective-permute-done((bf16[32,6656]{1,0:T(8,128)(2,1)S(1)}, bf16[32,6656]{1,0:T(8,128)(2,1)S(1)}, u32[]{:S(2)}, u32[]{:S(2)}) %collective-permute-start.8) | collective-permute-done | bytes 426016 | tf_op jit(solution)/shard_map/ppermute | solution.py:20
  30.6 2.8 %late_logits.1 = (f32[640,128]{1,0:T(8,128)S(1)}, f32[640,128]{1,0:T(8,128)S(1)}, bf16[128,2560]{1,0:T(8,128)(2,1)S(1)}, f32[16,256]{1,0:T(8,128)S(1)}) custom-call(bf16[32,6656]{1,0:T(8,128)(2,1)S(1)} %collective-permute-done.5.refs_0_, bf16[32,6656]{1,0:T(8,128)(2,1)S(1)} %collective-permute-done.7.refs_1_, ...), custom_call_target="tpu_custom_call" | custom-call | flops 1090519040 | bytes 12582912 | tf_op jit(solution)/shard_map/late_logits/pallas_call | solution.py:172
  33.4 0.2 collective-permute-start.9
  33.5 1.0 %collective-permute-done.9.refs_1_ = f32[16,256]{1,0:T(8,128)S(1)} collective-permute-done((f32[16,256]{1,0:T(8,128)S(1)}, f32[16,256]{1,0:T(8,128)S(1)}, u32[]{:S(2)}, u32[]{:S(2)}) %collective-permute-start.9) | collective-permute-done | bytes 16416 | tf_op jit(solution)/shard_map/ppermute | solution.py:20
  34.6 1.3 %collective-permute-start.10 = (f32[16,256]{1,0:T(8,128)S(1)}, f32[16,256]{1,0:T(8,128)S(1)}, u32[]{:S(2)}, u32[]{:S(2)}) collective-permute-start(f32[16,256]{1,0:T(8,128)S(1)} %merge.4.refs_0_), channel_id=1, source_target_pairs={{0,32},{32,0},{1,33},{33,1},{2,34},{34,2},{3,35},{35,3},{4,36},{36... | collective-permute-start | bytes 49160 | tf_op jit(solution)/shard_map/ppermute | solution.py:20
  35.9 2.5 %collective-permute-done.10.refs_1_ = f32[16,256]{1,0:T(8,128)S(1)} collective-permute-done((f32[16,256]{1,0:T(8,128)S(1)}, f32[16,256]{1,0:T(8,128)S(1)}, u32[]{:S(2)}, u32[]{:S(2)}) %collective-permute-start.10) | collective-permute-done | bytes 16416 | tf_op jit(solution)/shard_map/ppermute | solution.py:20
  38.4 0.4 collective-permute-start.13
  38.8 1.5 %collective-permute-start.12 = (f32[16,256]{1,0:T(8,128)S(1)}, f32[16,256]{1,0:T(8,128)S(1)}, u32[]{:S(2)}, u32[]{:S(2)}) collective-permute-start(f32[16,256]{1,0:T(8,128)S(1)} %merge.5.refs_0_), channel_id=1, source_target_pairs={{0,192},{64,0},{128,64},{192,128},{1,193},{65,1},{129,65},{193,129... | collective-permute-start | bytes 49160 | tf_op jit(solution)/shard_map/ppermute | solution.py:25
  40.3 0.6 collective-permute-start.11
  40.8 2.9 %collective-permute-done.13.refs_3_ = f32[16,256]{1,0:T(8,128)S(1)} collective-permute-done((f32[16,256]{1,0:T(8,128)S(1)}, f32[16,256]{1,0:T(8,128)S(1)}, u32[]{:S(2)}, u32[]{:S(2)}) %collective-permute-start.13) | collective-permute-done | bytes 16416 | tf_op jit(solution)/shard_map/ppermute | solution.py:25
  43.8 1.4 %collective-permute-done.11.refs_1_ = f32[16,256]{1,0:T(8,128)S(1)} collective-permute-done((f32[16,256]{1,0:T(8,128)S(1)}, f32[16,256]{1,0:T(8,128)S(1)}, u32[]{:S(2)}, u32[]{:S(2)}) %collective-permute-start.11) | collective-permute-done | bytes 16416 | tf_op jit(solution)/shard_map/ppermute | solution.py:25
  45.2 5.9 %collective-permute-start.15 = (f32[16,256]{1,0:T(8,128)S(1)}, f32[16,256]{1,0:T(8,128)S(1)}, u32[]{:S(2)}, u32[]{:S(2)}) collective-permute-start(f32[16,256]{1,0:T(8,128)S(1)} %merge.6.refs_0_), channel_id=1, source_target_pairs={{0,14},{2,0},{4,2},{6,4},{8,6},{10,8},{12,10},{14,12},{1,15},{3,1}... | collective-permute-start | bytes 49160 | tf_op jit(solution)/shard_map/ppermute | solution.py:25
  51.2 1.4 %collective-permute-done.15.refs_2_ = f32[16,256]{1,0:T(8,128)S(1)} collective-permute-done((f32[16,256]{1,0:T(8,128)S(1)}, f32[16,256]{1,0:T(8,128)S(1)}, u32[]{:S(2)}, u32[]{:S(2)}) %collective-permute-start.15) | collective-permute-done | bytes 16416 | tf_op jit(solution)/shard_map/ppermute | solution.py:25
  52.6 3.5 %collective-permute-done.14.refs_1_ = f32[16,256]{1,0:T(8,128)S(1)} collective-permute-done((f32[16,256]{1,0:T(8,128)S(1)}, f32[16,256]{1,0:T(8,128)S(1)}, u32[]{:S(2)}, u32[]{:S(2)}) %collective-permute-start.14) | collective-permute-done | bytes 16416 | tf_op jit(solution)/shard_map/ppermute | solution.py:25
  56.2 2.4 %collective-permute-start.16 = (f32[16,256]{1,0:T(8,128)S(1)}, f32[16,256]{1,0:T(8,128)S(1)}, u32[]{:S(2)}, u32[]{:S(2)}) collective-permute-start(f32[16,256]{1,0:T(8,128)S(1)} %get-tuple-element.53.refs_4_), channel_id=1, source_target_pairs={{0,10},{2,12},{4,14},{6,0},{8,2},{10,4},{12,6},{14,8},{1,11},{3,13... | collective-permute-start | bytes 49160 | tf_op jit(solution)/shard_map/ppermute | solution.py:25
  58.6 3.5 %collective-permute-done.17.refs_6_ = f32[16,256]{1,0:T(8,128)S(1)} collective-permute-done((f32[16,256]{1,0:T(8,128)S(1)}, f32[16,256]{1,0:T(8,128)S(1)}, u32[]{:S(2)}, u32[]{:S(2)}) %collective-permute-start.17) | collective-permute-done | bytes 16416 | tf_op jit(solution)/shard_map/ppermute | solution.py:25
  62.1 1.8 %slope.1 = (bf16[640,256]{1,0:T(8,128)(2,1)S(1)}, bf16[128,2560]{1,0:T(8,128)(2,1)S(1)}, f32[128,2560]{1,0:T(8,128)S(1)}, f32[2]{0:T(128)}) custom-call(f32[640,128]{1,0:T(8,128)S(1)} %get-tuple-element.42.refs_0_, f32[640,128]{1,0:T(8,128)S(1)} %get-tuple-element.49.refs_1_, f32[640,128]{1,0:T(8,128)S(1)} %get-tuple-element.50.refs_2_, ...), custom_call_target="tpu_custom_call" | custom-call | flops 838860800 | bytes 8388608 | tf_op jit(solution)/shard_map/slope/pallas_call | solution.py:229
  64.0 2.1 %collective-permute-done.18.got_ref = bf16[128,2560]{1,0:T(8,128)(2,1)S(1)} collective-permute-done((bf16[128,2560]{1,0:T(8,128)(2,1)S(1)}, bf16[128,2560]{1,0:T(8,128)(2,1)S(1)}, u32[]{:S(2)}, u32[]{:S(2)}) %collective-permute-start.18) | collective-permute-done | bytes 655392 | tf_op jit(solution)/shard_map/ppermute | solution.py:20
  66.1 0.1 add_core.1
  66.3 3.2 %collective-permute-start.20 = (bf16[32,2560]{1,0:T(8,128)(2,1)S(1)}, bf16[32,2560]{1,0:T(8,128)(2,1)S(1)}, u32[]{:S(2)}, u32[]{:S(2)}) collective-permute-start(bf16[32,2560]{1,0:T(8,128)(2,1)S(1)} %get-tuple-element.60), channel_id=1, source_target_pairs={{0,192},{64,0},{128,64},{192,128},{1,193},{65,1},{129,65},{193,129... | collective-permute-start | bytes 491528 | tf_op jit(solution)/shard_map/ppermute | solution.py:25
  69.5 3.5 %weight.1 = (bf16[640,2560]{1,0:T(8,128)(2,1)}, f32[8,128]{1,0:T(8,128)S(1)}) custom-call(bf16[640,256]{1,0:T(8,128)(2,1)S(1)} %get-tuple-element.62.g_ref, bf16[128,2560]{1,0:T(8,128)(2,1)S(1)} %get-tuple-element.63.a_ref, bf16[128,2560]{1,0:T(8,128)(2,1)S(1)} %get-tuple-element.64.b_ref), custom_call_target="tpu_custom_call" | custom-call | flops 838860800 | bytes 6291456 | tf_op jit(solution)/shard_map/weight/pallas_call | solution.py:258
  73.1 4.2 %collective-permute-done.19.a_ref = bf16[32,2560]{1,0:T(8,128)(2,1)S(1)} collective-permute-done((bf16[32,2560]{1,0:T(8,128)(2,1)S(1)}, bf16[32,2560]{1,0:T(8,128)(2,1)S(1)}, u32[]{:S(2)}, u32[]{:S(2)}) %collective-permute-start.19) | collective-permute-done | bytes 163872 | tf_op jit(solution)/shard_map/ppermute | solution.py:25
  77.3 1.3 %collective-permute-start.22 = (bf16[16,2560]{1,0:T(8,128)(2,1)S(1)}, bf16[16,2560]{1,0:T(8,128)(2,1)S(1)}, u32[]{:S(2)}, u32[]{:S(2)}) collective-permute-start(bf16[16,2560]{1,0:T(8,128)(2,1)S(1)} %get-tuple-element.67), channel_id=1, source_target_pairs={{0,32},{32,0},{1,33},{33,1},{2,34},{34,2},{3,35},{35,3},{4,36},{36... | collective-permute-start | bytes 245768 | tf_op jit(solution)/shard_map/ppermute | solution.py:20
  78.6 3.2 %collective-permute-done.22.got_ref = bf16[16,2560]{1,0:T(8,128)(2,1)S(1)} collective-permute-done((bf16[16,2560]{1,0:T(8,128)(2,1)S(1)}, bf16[16,2560]{1,0:T(8,128)(2,1)S(1)}, u32[]{:S(2)}, u32[]{:S(2)}) %collective-permute-start.22) | collective-permute-done | bytes 81952 | tf_op jit(solution)/shard_map/ppermute | solution.py:20
  82.0 3.2 %collective-permute-start.23 = (f32[3,16,320]{2,1,0:T(8,128)S(1)}, f32[3,16,320]{2,1,0:T(8,128)S(1)}, u32[]{:S(2)}, u32[]{:S(2)}) collective-permute-start(f32[3,16,320]{2,1,0:T(8,128)S(1)} %get-tuple-element.69), channel_id=1, source_target_pairs={{0,6},{2,8},{4,10},{6,12},{8,14},{10,0},{12,2},{14,4},{1,7},{3,9},... | collective-permute-start | bytes 184328 | tf_op jit(solution)/shard_map/ppermute | solution.py:25
  85.2 2.0 %collective-permute-start.24 = (f32[2,16,320]{2,1,0:T(8,128)S(1)}, f32[2,16,320]{2,1,0:T(8,128)S(1)}, u32[]{:S(2)}, u32[]{:S(2)}) collective-permute-start(f32[2,16,320]{2,1,0:T(8,128)S(1)} %get-tuple-element.70), channel_id=1, source_target_pairs={{0,12},{2,14},{4,0},{6,2},{8,4},{10,6},{12,8},{14,10},{1,13},{3,15... | collective-permute-start | bytes 122888 | tf_op jit(solution)/shard_map/ppermute | solution.py:25
  87.2 3.0 %collective-permute-done.24.b_ref = f32[2,16,320]{2,1,0:T(8,128)S(1)} collective-permute-done((f32[2,16,320]{2,1,0:T(8,128)S(1)}, f32[2,16,320]{2,1,0:T(8,128)S(1)}, u32[]{:S(2)}, u32[]{:S(2)}) %collective-permute-start.24) | collective-permute-done | bytes 40992 | tf_op jit(solution)/shard_map/ppermute | solution.py:25
  90.2 0.8 collective-permute-done.23.a_ref
  91.0 1.2 %collective-permute-start.25 = (f32[16,320]{1,0:T(8,128)S(1)}, f32[16,320]{1,0:T(8,128)S(1)}, u32[]{:S(2)}, u32[]{:S(2)}) collective-permute-start(f32[16,320]{1,0:T(8,128)S(1)} %get-tuple-element.72), channel_id=1, source_target_pairs={{0,2},{2,4},{4,6},{6,8},{8,10},{10,12},{12,14},{14,0},{1,3},{3,5},... | collective-permute-start | bytes 61448 | tf_op jit(solution)/shard_map/ppermute | solution.py:25
  92.2 2.2 %collective-permute-start.26 = (f32[16,320]{1,0:T(8,128)S(1)}, f32[16,320]{1,0:T(8,128)S(1)}, u32[]{:S(2)}, u32[]{:S(2)}) collective-permute-start(f32[16,320]{1,0:T(8,128)S(1)} %get-tuple-element.73), channel_id=1, source_target_pairs={{0,14},{2,0},{4,2},{6,4},{8,6},{10,8},{12,10},{14,12},{1,15},{3,1}... | collective-permute-start | bytes 61448 | tf_op jit(solution)/shard_map/ppermute | solution.py:25
  94.4 1.7 %collective-permute-done.25 = f32[16,320]{1,0:T(8,128)S(1)} collective-permute-done((f32[16,320]{1,0:T(8,128)S(1)}, f32[16,320]{1,0:T(8,128)S(1)}, u32[]{:S(2)}, u32[]{:S(2)}) %collective-permute-start.25) | collective-permute-done | bytes 20512 | tf_op jit(solution)/shard_map/ppermute | solution.py:25
  96.1 0.6 fusion
  (37 shorter events, 0.8 us)
Async XLA Ops:
  0.6 0.9 copy-start.4
  1.5 0.9 copy-start.5
  2.4 7.1 %collective-permute-start = (bf16[16,6656]{1,0:T(8,128)(2,1)S(1)}, bf16[16,6656]{1,0:T(8,128)(2,1)S(1)}, u32[]{:S(2)}, u32[]{:S(2)}) collective-permute-start(bf16[16,6656]{1,0:T(8,128)(2,1)S(1)} %join.1.a_ref), channel_id=1, source_target_pairs={{0,32},{32,0},{1,33},{33,1},{2,34},{34,2},{3,35},{35,3},{4,36},{36... | collective-permute-start | bytes 638984 | tf_op jit(solution)/shard_map/ppermute | solution.py:20
  3.7 7.2 %collective-permute-start.3 = (bf16[16,6656]{1,0:T(8,128)(2,1)S(1)}, bf16[16,6656]{1,0:T(8,128)(2,1)S(1)}, u32[]{:S(2)}, u32[]{:S(2)}) collective-permute-start(bf16[16,6656]{1,0:T(8,128)(2,1)S(1)} %join.1.a_ref), channel_id=1, source_target_pairs={{0,192},{64,0},{128,64},{192,128},{1,193},{65,1},{129,65},{193,129... | collective-permute-start | bytes 638984 | tf_op jit(solution)/shard_map/ppermute | solution.py:25
  6.7 7.6 %collective-permute-start.2 = (bf16[16,6656]{1,0:T(8,128)(2,1)S(1)}, bf16[16,6656]{1,0:T(8,128)(2,1)S(1)}, u32[]{:S(2)}, u32[]{:S(2)}) collective-permute-start(bf16[16,6656]{1,0:T(8,128)(2,1)S(1)} %join.1.a_ref), channel_id=1, source_target_pairs={{0,64},{64,128},{128,192},{192,0},{1,65},{65,129},{129,193},{193,1... | collective-permute-start | bytes 638984 | tf_op jit(solution)/shard_map/ppermute | solution.py:25
  6.7 0.7 copy-start.6
  9.6 5.9 %collective-permute-start.1 = (bf16[32,6656]{1,0:T(8,128)(2,1)S(1)}, bf16[32,6656]{1,0:T(8,128)(2,1)S(1)}, u32[]{:S(2)}, u32[]{:S(2)}) collective-permute-start(bf16[32,6656]{1,0:T(8,128)(2,1)S(1)} %pair.2.refs_0_), channel_id=1, source_target_pairs={{0,16},{16,0},{1,17},{17,1},{2,18},{18,2},{3,19},{19,3},{4,20},{20... | collective-permute-start | bytes 1277960 | tf_op jit(solution)/shard_map/ppermute | solution.py:20
  14.4 1.9 %collective-permute-start.4 = (bf16[32,6656]{1,0:T(8,128)(2,1)S(1)}, bf16[32,6656]{1,0:T(8,128)(2,1)S(1)}, u32[]{:S(2)}, u32[]{:S(2)}) collective-permute-start(bf16[32,6656]{1,0:T(8,128)(2,1)S(1)} %pair.3.refs_2_), channel_id=1, source_target_pairs={{0,16},{16,0},{1,17},{17,1},{2,18},{18,2},{3,19},{19,3},{4,20},{20... | collective-permute-start | bytes 1277960 | tf_op jit(solution)/shard_map/ppermute | solution.py:20
  14.5 12.2 %collective-permute-start.5 = (bf16[32,6656]{1,0:T(8,128)(2,1)S(1)}, bf16[32,6656]{1,0:T(8,128)(2,1)S(1)}, u32[]{:S(2)}, u32[]{:S(2)}) collective-permute-start(bf16[32,6656]{1,0:T(8,128)(2,1)S(1)} %pair.3.refs_2_), channel_id=1, source_target_pairs={{0,32},{32,0},{1,33},{33,1},{2,34},{34,2},{3,35},{35,3},{4,36},{36... | collective-permute-start | bytes 1277960 | tf_op jit(solution)/shard_map/ppermute | solution.py:20
  15.4 13.4 %collective-permute-start.6 = (bf16[32,6656]{1,0:T(8,128)(2,1)S(1)}, bf16[32,6656]{1,0:T(8,128)(2,1)S(1)}, u32[]{:S(2)}, u32[]{:S(2)}) collective-permute-start(bf16[32,6656]{1,0:T(8,128)(2,1)S(1)} %pair.2.refs_0_), channel_id=1, source_target_pairs={{0,128},{64,192},{128,0},{192,64},{1,129},{65,193},{129,1},{193,65... | collective-permute-start | bytes 1277960 | tf_op jit(solution)/shard_map/ppermute | solution.py:25
  16.3 1.9 %copy-start = (bf16[640,2560]{1,0:T(8,128)(2,1)S(1)}, bf16[640,2560]{1,0:T(8,128)(2,1)}, u32[]{:S(2)}) copy-start(bf16[640,2560]{1,0:T(8,128)(2,1)} %refs_9_.1) | copy-start | bytes 9830404
  18.2 2.5 %copy-start.2 = (bf16[640,4096]{1,0:T(8,128)(2,1)S(1)}, bf16[640,4096]{1,0:T(8,128)(2,1)}, u32[]{:S(2)}) copy-start(bf16[640,4096]{1,0:T(8,128)(2,1)} %refs_5_.3) | copy-start | bytes 15728644
  20.7 9.9 %copy-start.1 = (bf16[640,2560]{1,0:T(8,128)(2,1)S(1)}, bf16[640,2560]{1,0:T(8,128)(2,1)}, u32[]{:S(2)}) copy-start(bf16[640,2560]{1,0:T(8,128)(2,1)} %refs_9_.1) | copy-start | bytes 9830404
  20.7 9.9 %copy-start.3 = (bf16[640,4096]{1,0:T(8,128)(2,1)S(1)}, bf16[640,4096]{1,0:T(8,128)(2,1)}, u32[]{:S(2)}) copy-start(bf16[640,4096]{1,0:T(8,128)(2,1)} %refs_5_.3) | copy-start | bytes 15728644
  26.8 2.1 %collective-permute-start.7 = (bf16[32,6656]{1,0:T(8,128)(2,1)S(1)}, bf16[32,6656]{1,0:T(8,128)(2,1)S(1)}, u32[]{:S(2)}, u32[]{:S(2)}) collective-permute-start(bf16[32,6656]{1,0:T(8,128)(2,1)S(1)} %collective-permute-done.5.refs_0_), channel_id=1, source_target_pairs={{0,16},{16,0},{1,17},{17,1},{2,18},{18,2},{3,19},{19,3},{4,20},{20... | collective-permute-start | bytes 1277960 | tf_op jit(solution)/shard_map/ppermute | solution.py:20
  28.8 1.8 %collective-permute-start.8 = (bf16[32,6656]{1,0:T(8,128)(2,1)S(1)}, bf16[32,6656]{1,0:T(8,128)(2,1)S(1)}, u32[]{:S(2)}, u32[]{:S(2)}) collective-permute-start(bf16[32,6656]{1,0:T(8,128)(2,1)S(1)} %collective-permute-done.6.refs_2_), channel_id=1, source_target_pairs={{0,16},{16,0},{1,17},{17,1},{2,18},{18,2},{3,19},{19,3},{4,20},{20... | collective-permute-start | bytes 1277960 | tf_op jit(solution)/shard_map/ppermute | solution.py:20
  33.4 1.2 %collective-permute-start.9 = (f32[16,256]{1,0:T(8,128)S(1)}, f32[16,256]{1,0:T(8,128)S(1)}, u32[]{:S(2)}, u32[]{:S(2)}) collective-permute-start(f32[16,256]{1,0:T(8,128)S(1)} %get-tuple-element.52.refs_0_), channel_id=1, source_target_pairs={{0,16},{16,0},{1,17},{17,1},{2,18},{18,2},{3,19},{19,3},{4,20},{20... | collective-permute-start | bytes 49160 | tf_op jit(solution)/shard_map/ppermute | solution.py:20
  34.6 3.8 %collective-permute-start.10 = (f32[16,256]{1,0:T(8,128)S(1)}, f32[16,256]{1,0:T(8,128)S(1)}, u32[]{:S(2)}, u32[]{:S(2)}) collective-permute-start(f32[16,256]{1,0:T(8,128)S(1)} %merge.4.refs_0_), channel_id=1, source_target_pairs={{0,32},{32,0},{1,33},{33,1},{2,34},{34,2},{3,35},{35,3},{4,36},{36... | collective-permute-start | bytes 49160 | tf_op jit(solution)/shard_map/ppermute | solution.py:20
  38.4 5.3 %collective-permute-start.13 = (f32[16,256]{1,0:T(8,128)S(1)}, f32[16,256]{1,0:T(8,128)S(1)}, u32[]{:S(2)}, u32[]{:S(2)}) collective-permute-start(f32[16,256]{1,0:T(8,128)S(1)} %merge.5.refs_0_), channel_id=1, source_target_pairs={{0,128},{64,192},{128,0},{192,64},{1,129},{65,193},{129,1},{193,65... | collective-permute-start | bytes 49160 | tf_op jit(solution)/shard_map/ppermute | solution.py:25
  38.8 5.0 %collective-permute-start.12 = (f32[16,256]{1,0:T(8,128)S(1)}, f32[16,256]{1,0:T(8,128)S(1)}, u32[]{:S(2)}, u32[]{:S(2)}) collective-permute-start(f32[16,256]{1,0:T(8,128)S(1)} %merge.5.refs_0_), channel_id=1, source_target_pairs={{0,192},{64,0},{128,64},{192,128},{1,193},{65,1},{129,65},{193,129... | collective-permute-start | bytes 49160 | tf_op jit(solution)/shard_map/ppermute | solution.py:25
  40.3 5.0 %collective-permute-start.11 = (f32[16,256]{1,0:T(8,128)S(1)}, f32[16,256]{1,0:T(8,128)S(1)}, u32[]{:S(2)}, u32[]{:S(2)}) collective-permute-start(f32[16,256]{1,0:T(8,128)S(1)} %merge.5.refs_0_), channel_id=1, source_target_pairs={{0,64},{64,128},{128,192},{192,0},{1,65},{65,129},{129,193},{193,1... | collective-permute-start | bytes 49160 | tf_op jit(solution)/shard_map/ppermute | solution.py:25
  45.2 7.4 %collective-permute-start.15 = (f32[16,256]{1,0:T(8,128)S(1)}, f32[16,256]{1,0:T(8,128)S(1)}, u32[]{:S(2)}, u32[]{:S(2)}) collective-permute-start(f32[16,256]{1,0:T(8,128)S(1)} %merge.6.refs_0_), channel_id=1, source_target_pairs={{0,14},{2,0},{4,2},{6,4},{8,6},{10,8},{12,10},{14,12},{1,15},{3,1}... | collective-permute-start | bytes 49160 | tf_op jit(solution)/shard_map/ppermute | solution.py:25
  51.2 4.9 %collective-permute-start.14 = (f32[16,256]{1,0:T(8,128)S(1)}, f32[16,256]{1,0:T(8,128)S(1)}, u32[]{:S(2)}, u32[]{:S(2)}) collective-permute-start(f32[16,256]{1,0:T(8,128)S(1)} %merge.6.refs_0_), channel_id=1, source_target_pairs={{0,2},{2,4},{4,6},{6,8},{8,10},{10,12},{12,14},{14,0},{1,3},{3,5},... | collective-permute-start | bytes 49160 | tf_op jit(solution)/shard_map/ppermute | solution.py:25
  56.1 5.9 %collective-permute-start.17 = (f32[16,256]{1,0:T(8,128)S(1)}, f32[16,256]{1,0:T(8,128)S(1)}, u32[]{:S(2)}, u32[]{:S(2)}) collective-permute-start(f32[16,256]{1,0:T(8,128)S(1)} %get-tuple-element.54), channel_id=1, source_target_pairs={{0,4},{2,6},{4,8},{6,10},{8,12},{10,14},{12,0},{14,2},{1,5},{3,7},... | collective-permute-start | bytes 49160 | tf_op jit(solution)/shard_map/ppermute | solution.py:25
  56.2 5.8 %collective-permute-start.16 = (f32[16,256]{1,0:T(8,128)S(1)}, f32[16,256]{1,0:T(8,128)S(1)}, u32[]{:S(2)}, u32[]{:S(2)}) collective-permute-start(f32[16,256]{1,0:T(8,128)S(1)} %get-tuple-element.53.refs_4_), channel_id=1, source_target_pairs={{0,10},{2,12},{4,14},{6,0},{8,2},{10,4},{12,6},{14,8},{1,11},{3,13... | collective-permute-start | bytes 49160 | tf_op jit(solution)/shard_map/ppermute | solution.py:25
  63.9 2.2 %collective-permute-start.18 = (bf16[128,2560]{1,0:T(8,128)(2,1)S(1)}, bf16[128,2560]{1,0:T(8,128)(2,1)S(1)}, u32[]{:S(2)}, u32[]{:S(2)}) collective-permute-start(bf16[128,2560]{1,0:T(8,128)(2,1)S(1)} %get-tuple-element.57), channel_id=1, source_target_pairs={{0,16},{16,0},{1,17},{17,1},{2,18},{18,2},{3,19},{19,3},{4,20},{20... | collective-permute-start | bytes 1966088 | tf_op jit(solution)/shard_map/ppermute | solution.py:20
  66.2 11.0 %collective-permute-start.19 = (bf16[32,2560]{1,0:T(8,128)(2,1)S(1)}, bf16[32,2560]{1,0:T(8,128)(2,1)S(1)}, u32[]{:S(2)}, u32[]{:S(2)}) collective-permute-start(bf16[32,2560]{1,0:T(8,128)(2,1)S(1)} %get-tuple-element.59), channel_id=1, source_target_pairs={{0,64},{64,128},{128,192},{192,0},{1,65},{65,129},{129,193},{193,1... | collective-permute-start | bytes 491528 | tf_op jit(solution)/shard_map/ppermute | solution.py:25
  66.3 11.0 %collective-permute-start.20 = (bf16[32,2560]{1,0:T(8,128)(2,1)S(1)}, bf16[32,2560]{1,0:T(8,128)(2,1)S(1)}, u32[]{:S(2)}, u32[]{:S(2)}) collective-permute-start(bf16[32,2560]{1,0:T(8,128)(2,1)S(1)} %get-tuple-element.60), channel_id=1, source_target_pairs={{0,192},{64,0},{128,64},{192,128},{1,193},{65,1},{129,65},{193,129... | collective-permute-start | bytes 491528 | tf_op jit(solution)/shard_map/ppermute | solution.py:25
  69.5 7.7 %collective-permute-start.21 = (bf16[32,2560]{1,0:T(8,128)(2,1)S(1)}, bf16[32,2560]{1,0:T(8,128)(2,1)S(1)}, u32[]{:S(2)}, u32[]{:S(2)}) collective-permute-start(bf16[32,2560]{1,0:T(8,128)(2,1)S(1)} %get-tuple-element.61), channel_id=1, source_target_pairs={{0,128},{64,192},{128,0},{192,64},{1,129},{65,193},{129,1},{193,65... | collective-permute-start | bytes 491528 | tf_op jit(solution)/shard_map/ppermute | solution.py:25
  77.3 4.5 %collective-permute-start.22 = (bf16[16,2560]{1,0:T(8,128)(2,1)S(1)}, bf16[16,2560]{1,0:T(8,128)(2,1)S(1)}, u32[]{:S(2)}, u32[]{:S(2)}) collective-permute-start(bf16[16,2560]{1,0:T(8,128)(2,1)S(1)} %get-tuple-element.67), channel_id=1, source_target_pairs={{0,32},{32,0},{1,33},{33,1},{2,34},{34,2},{3,35},{35,3},{4,36},{36... | collective-permute-start | bytes 245768 | tf_op jit(solution)/shard_map/ppermute | solution.py:20
  82.0 9.0 %collective-permute-start.23 = (f32[3,16,320]{2,1,0:T(8,128)S(1)}, f32[3,16,320]{2,1,0:T(8,128)S(1)}, u32[]{:S(2)}, u32[]{:S(2)}) collective-permute-start(f32[3,16,320]{2,1,0:T(8,128)S(1)} %get-tuple-element.69), channel_id=1, source_target_pairs={{0,6},{2,8},{4,10},{6,12},{8,14},{10,0},{12,2},{14,4},{1,7},{3,9},... | collective-permute-start | bytes 184328 | tf_op jit(solution)/shard_map/ppermute | solution.py:25
  85.2 5.0 %collective-permute-start.24 = (f32[2,16,320]{2,1,0:T(8,128)S(1)}, f32[2,16,320]{2,1,0:T(8,128)S(1)}, u32[]{:S(2)}, u32[]{:S(2)}) collective-permute-start(f32[2,16,320]{2,1,0:T(8,128)S(1)} %get-tuple-element.70), channel_id=1, source_target_pairs={{0,12},{2,14},{4,0},{6,2},{8,4},{10,6},{12,8},{14,10},{1,13},{3,15... | collective-permute-start | bytes 122888 | tf_op jit(solution)/shard_map/ppermute | solution.py:25
  91.0 5.1 %collective-permute-start.25 = (f32[16,320]{1,0:T(8,128)S(1)}, f32[16,320]{1,0:T(8,128)S(1)}, u32[]{:S(2)}, u32[]{:S(2)}) collective-permute-start(f32[16,320]{1,0:T(8,128)S(1)} %get-tuple-element.72), channel_id=1, source_target_pairs={{0,2},{2,4},{4,6},{6,8},{8,10},{10,12},{12,14},{14,0},{1,3},{3,5},... | collective-permute-start | bytes 61448 | tf_op jit(solution)/shard_map/ppermute | solution.py:25
  92.2 4.0 %collective-permute-start.26 = (f32[16,320]{1,0:T(8,128)S(1)}, f32[16,320]{1,0:T(8,128)S(1)}, u32[]{:S(2)}, u32[]{:S(2)}) collective-permute-start(f32[16,320]{1,0:T(8,128)S(1)} %get-tuple-element.73), channel_id=1, source_target_pairs={{0,14},{2,0},{4,2},{6,4},{8,6},{10,8},{12,10},{14,12},{1,15},{3,1}... | collective-permute-start | bytes 61448 | tf_op jit(solution)/shard_map/ppermute | solution.py:25
